TPU v7x, 32 devices: a whole 2x2x4 slice. The times are simulated.
32 devices in a mesh: seq: 8 (over z, x), head: 4 (over y, core).
Axes of the slice: x: 2, y: 2, z: 4, core: 2. Of those that a mesh axis runs over, the one named last changes fastest.
Arguments:
- frames: bfloat16 [2048, 1024], P('seq'), may hold values from -6 to 6
- norm_gain: float32 [1024], replicated, may hold values from 0.5 to 1.5
- w_qkv: bfloat16 [3, 1024, 1024], P(None, None, 'head'), may hold values from -2 to 2
- w_out: bfloat16 [1024, 1024], P('head'), may hold values from -0.1875 to 0.1875
- w_proj: bfloat16 [1024, 512], replicated, may hold values from -0.1875 to 0.1875
- text_table: bfloat16 [32768, 512], P(('seq', 'head')), may hold values from -6 to 6
- token_ids: int32 [64, 16], replicated, may hold values from 0 to 32767
- span_bounds: int32 [64, 2], P(('seq', 'head')), may hold values from 0 to 2048, as said below
- contrast_divisor: float32 [1], replicated, may hold values from 10 to 30
Outputs:
- interval_embedding_derivative: float32 [64, 512], P(('seq', 'head'))
- loss_terms: float32 [64], P(('seq', 'head'))
Inputs may be any that keep to these rules, and one draw needn't show every extreme that they name: `span_bounds`: both entries are multiples of 128 and the first is smaller than the second.
All inputs are finite; a program needn't handle non-finite values.
Results may differ from a plain program's by a relative error of at most 0.006.
Values may be sent and summed in bfloat16 or wider, within the bound.
No kernel may reach another device: no remote copies, remote signals or barrier semaphores. Data moves between devices by JAX's collectives and lax.ppermute only.
A program may use at most 64 MiB of HBM per device.

v0:
```python
import jax
import jax.numpy as jnp
from jax import lax
from jax.sharding import PartitionSpec as P

HDIM = 64
E = 512
BLK = 128


def extended(cells, sides, width):
    for axis, dim in sides:
        count = lax.axis_size(axis)
        ends = count - 1
        head = lax.slice_in_dim(cells, 0, width, axis=dim)
        tail = lax.slice_in_dim(cells, cells.shape[dim] - width, cells.shape[dim], axis=dim)
        cells = jnp.concatenate(
            [
                lax.ppermute(tail, axis, [(i, (i + 1) % count) for i in range(ends)]),
                cells,
                lax.ppermute(head, axis, [((i + 1) % count, i) for i in range(ends)]),
            ],
            axis=dim,
        )
    return cells


def log_total(values, axis):
    return jnp.log(jnp.sum(jnp.exp(values), axis=axis))


def unit_rows(values):
    return (
        values * lax.rsqrt(jnp.mean(values * values, axis=-1, keepdims=True) + 1e-06) * E ** (-0.5)
    )


def token_counts(chosen, vocab_ids):

    def add_token(position, counts):
        column = lax.dynamic_index_in_dim(chosen, position, 1, keepdims=False)
        return counts + (column[:, None] == vocab_ids[None, :]).astype(jnp.float32)

    return lax.fori_loop(
        0, chosen.shape[1], add_token, jnp.zeros((chosen.shape[0], vocab_ids.shape[0]), jnp.float32)
    )


def local(
    frames, norm_gain, w_qkv, w_out, w_proj, text_table, token_ids, span_bounds, contrast_divisor
):
    frame_rows = frames.shape[0]
    head_cols = w_qkv.shape[2]
    local_heads = head_cols // HDIM
    seq_count = lax.axis_size("seq")
    total_frames = frame_rows * seq_count
    first_frame = lax.axis_index("seq") * frame_rows
    as32 = frames.astype(jnp.float32)
    normed = (
        as32 * lax.rsqrt(jnp.mean(as32 * as32, axis=-1, keepdims=True) + 1e-05) * norm_gain
    ).astype(jnp.bfloat16)
    queries = jnp.dot(normed, w_qkv[0], preferred_element_type=jnp.float32).astype(jnp.bfloat16)
    keys_now = jnp.dot(normed, w_qkv[1], preferred_element_type=jnp.float32).astype(jnp.bfloat16)
    values_now = jnp.dot(normed, w_qkv[2], preferred_element_type=jnp.float32).astype(jnp.bfloat16)
    pairs = jnp.concatenate([keys_now, values_now], axis=1)
    padded = extended(pairs, (("seq", 0),), frame_rows)
    query_block = min(512, frame_rows)
    span_width = 2 * frame_rows + query_block

    def attend(block):
        begin = block * query_block
        query_part = queries.reshape(query_block, local_heads, HDIM)
        key_part = padded[:, :head_cols].reshape(span_width, local_heads, HDIM)
        value_part = padded[:, head_cols:].reshape(span_width, local_heads, HDIM)
        scores = jnp.einsum(
            "qhd,khd->hqk", query_part, key_part, preferred_element_type=jnp.float32
        ) * HDIM ** (-0.5)
        query_pos = first_frame + begin + jnp.arange(query_block, dtype=jnp.int32)
        key_pos = first_frame + begin - frame_rows + jnp.arange(span_width, dtype=jnp.int32)
        allowed = (
            (jnp.abs(query_pos[:, None] - key_pos[None, :]) <= frame_rows)
            & (key_pos >= 0)[None, :]
            & (key_pos < total_frames)[None, :]
        )
        scores = jnp.where(allowed[None], scores, -1e30)
        top = jnp.max(scores, axis=2, keepdims=True)
        probs = jnp.exp(scores - top)
        denom = jnp.sum(probs, axis=2)
        mixed = jnp.einsum(
            "hqk,khd->qhd",
            probs.astype(jnp.bfloat16),
            value_part,
            preferred_element_type=jnp.float32,
        )
        return (mixed / denom.T[:, :, None]).astype(jnp.bfloat16).reshape(query_block, head_cols)

    attended = lax.map(attend, jnp.arange(frame_rows // query_block, dtype=jnp.int32)).reshape(
        frame_rows, head_cols
    )
    block_count = frame_rows // BLK
    out_sums = attended.astype(jnp.float32).reshape(block_count, BLK, head_cols).sum(axis=1)
    head_slot = lax.axis_index("head")
    own_features = lax.dynamic_slice_in_dim(as32, head_slot * head_cols, head_cols, 1)
    feature_sums = own_features.reshape(block_count, BLK, head_cols).sum(axis=1)
    proj_rows = lax.dynamic_slice_in_dim(w_proj, head_slot * head_cols, head_cols, 0)
    through_out = jnp.dot(out_sums, w_out.astype(jnp.float32), precision=lax.Precision.HIGHEST)
    partial_value = jnp.dot(
        through_out, w_proj.astype(jnp.float32), precision=lax.Precision.HIGHEST
    ) + jnp.dot(feature_sums, proj_rows.astype(jnp.float32), precision=lax.Precision.HIGHEST)
    everyone = lax.all_gather(partial_value, ("seq", "head"), axis=0, tiled=True)
    head_count = lax.axis_size("head")
    block_table = (
        everyone.reshape(seq_count, head_count, block_count, -1)
        .sum(axis=1)
        .reshape(seq_count * block_count, -1)
    )
    total_blocks = block_table.shape[0]
    block_ids = jnp.arange(total_blocks, dtype=jnp.int32)
    lower = span_bounds[:, 0] // BLK
    upper = span_bounds[:, 1] // BLK
    span_mask = (
        (block_ids[None, :] >= lower[:, None]) & (block_ids[None, :] < upper[:, None])
    ).astype(jnp.float32)
    pooled = jnp.dot(span_mask, block_table, precision=lax.Precision.HIGHEST)
    interval_embedding_rows = unit_rows(pooled).astype(jnp.bfloat16)
    own_caps = span_bounds.shape[0]
    all_caps = token_ids.shape[0]
    slot = lax.axis_index(("seq", "head"))
    first_caption = slot * own_caps
    head_count = lax.axis_size("head")
    table_block = lax.all_gather(text_table, "head", axis=0, tiled=True)
    block_vocab = table_block.shape[0]
    block_words = lax.axis_index("seq") * block_vocab + jnp.arange(block_vocab, dtype=jnp.int32)
    layout = token_ids.reshape(seq_count, head_count, own_caps, token_ids.shape[1])
    group_ids = lax.dynamic_index_in_dim(layout, head_slot, 1, keepdims=False).reshape(
        seq_count * own_caps, token_ids.shape[1]
    )
    counts = token_counts(group_ids, block_words)
    raw = lax.psum_scatter(
        jnp.dot(counts.astype(jnp.bfloat16), table_block, preferred_element_type=jnp.float32),
        "seq",
        scatter_dimension=0,
        tiled=True,
    )
    caption_own = unit_rows(raw).astype(jnp.bfloat16)
    spans_all, captions_all = (
        lax.all_gather(interval_embedding_rows, ("seq", "head"), axis=0, tiled=True),
        lax.all_gather(caption_own, ("seq", "head"), axis=0, tiled=True),
    )
    normalizer_divisor = contrast_divisor[0]
    row_logits = (
        jnp.einsum("je,ie->ji", caption_own, spans_all, preferred_element_type=jnp.float32)
        * normalizer_divisor
    )
    col_logits = (
        jnp.einsum(
            "je,ie->ji", captions_all, interval_embedding_rows, preferred_element_type=jnp.float32
        )
        * normalizer_divisor
    )
    row_total = log_total(row_logits, 1)
    col_total = log_total(col_logits, 0)
    own_square = lax.dynamic_slice_in_dim(row_logits, first_caption, own_caps, 1)
    loss_terms = 0.5 * (row_total + col_total) - jnp.diagonal(own_square)
    row_totals = lax.all_gather(row_total, ("seq", "head"), axis=0, tiled=True)
    marker = (
        jnp.arange(all_caps, dtype=jnp.int32)[:, None]
        == first_caption + jnp.arange(own_caps, dtype=jnp.int32)[None, :]
    ).astype(jnp.float32)
    derivative_multipliers = (
        0.5 * jnp.exp(col_logits - row_totals[:, None])
        + 0.5 * jnp.exp(col_logits - col_total[None, :])
        - marker
    ).astype(jnp.bfloat16)
    interval_embedding_derivative = (
        jnp.einsum(
            "ji,je->ie", derivative_multipliers, captions_all, preferred_element_type=jnp.float32
        )
        * normalizer_divisor
    )
    return (interval_embedding_derivative, loss_terms)


def solution(mesh):
    placed = (
        P("seq", None),
        P(),
        P(None, None, "head"),
        P("head", None),
        P(),
        P(("seq", "head"), None),
        P(),
        P(("seq", "head"), None),
        P(),
    )
    return jax.shard_map(
        local,
        mesh=mesh,
        in_specs=placed,
        out_specs=(P(("seq", "head"), None), P(("seq", "head"))),
        check_vma=False,
    )
```

profile of v0, /device:TPU:0, one launch (start us, length us, event | category | flops | bytes accessed | tf_op | source)
XLA Modules:
  0.0 235.4 jit_solution(9203655861618520605)
XLA Ops:
  7.2 0.0 copy-start
  7.2 0.0 all-gather.5.cloned.1.call-start
  7.2 1.3 multiply_reduce_fusion
  8.5 1.7 convolution_convert_fusion.1
  10.2 0.0 copy-start.1
  10.2 1.7 convolution_convert_fusion.2
  12.0 0.0 copy-start.6
  12.0 0.7 pad_maximum_fusion.1
  12.7 5.7 %collective-permute-start = (bf16[256,512]{0,1:T(8,128)(2,1)}, bf16[256,512]{0,1:T(8,128)(2,1)}, u32[]{:S(2)}, u32[]{:S(2)}) collective-permute-start(bf16[256,512]{0,1:T(8,128)(2,1)} %pad_maximum_fusion.1), channel_id=1, source_target_pairs={{0,4},{4,8},{8,12},{12,16},{16,20},{20,24},{24,28},{1,5},{5,9},{9,... | collective-permute-start | bytes 786440 | tf_op jit(solution)/shard_map/ppermute | solution.py:19
  18.4 1.3 collective-permute-start.1
  19.7 0.0 all-gather.5.cloned.1.call-update
  19.7 0.1 copy.14
  19.8 0.1 copy.15
  19.9 2.4 %while.18 = (s32[]{:T(128)}, f32[16,4096]{1,0:T(8,128)S(1)}, s32[16,16]{0,1:T(8,128)S(1)}, s32[]{:T(128)}, s32[]{:T(128)}, /*index=5*/s32[]{:T(128)}) while((s32[]{:T(128)}, f32[16,4096]{1,0:T(8,128)S(1)}, s32[16,16]{0,1:T(8,128)S(1)}, s32[]{:T(128)}, s32[]{:T(128)}, /*index=5*/s32[]{:T(128)}) %tuple.49), condition=%wide.region_1.2_spmd.clone, body=%wide.region_0.0_spmd.clone.sunk | while | flops 266243 | bytes 557335 | solution.py:44
  19.9 0.1 select_add_fusion.2
  20.0 0.1 select_add_fusion.2
  20.2 0.1 select_add_fusion.2
  20.4 0.1 select_add_fusion.2
  20.5 0.1 select_add_fusion.2
  20.7 0.1 select_add_fusion.2
  20.8 0.1 select_add_fusion.2
  21.0 0.1 select_add_fusion.2
  21.1 0.1 select_add_fusion.2
  21.3 0.1 select_add_fusion.2
  21.4 0.1 select_add_fusion.2
  21.6 0.1 select_add_fusion.2
  21.7 0.1 select_add_fusion.2
  21.9 0.1 select_add_fusion.2
  22.1 0.1 select_add_fusion.2
  22.2 0.1 select_add_fusion.2
  22.4 0.2 fusion.43
  22.6 0.3 fusion.22
  22.9 0.1 convert_element_type.58
  23.7 0.6 dynamic-slice
  24.9 0.1 or_reduce_fusion
  25.1 1.5 convolution_convert_fusion
  26.6 2.5 %collective-permute-done = bf16[256,512]{0,1:T(8,128)(2,1)} collective-permute-done((bf16[256,512]{0,1:T(8,128)(2,1)}, bf16[256,512]{0,1:T(8,128)(2,1)}, u32[]{:S(2)}, u32[]{:S(2)}) %collective-permute-start) | collective-permute-done | bytes 262176 | tf_op jit(solution)/shard_map/ppermute | solution.py:19
  29.1 1.1 pad_maximum_fusion
  30.3 0.1 fusion.55
  30.4 0.8 fusion.2
  31.2 0.9 fusion.3
  32.1 1.0 fusion.18
  33.1 0.1 reshape.159
  33.3 0.3 reduce_sum.85
  33.6 0.4 fusion.56
  34.0 0.5 fusion.57
  34.5 0.2 fusion.11
  34.7 42.4 %all-gather.1 = f32[32,2,512]{2,1,0:T(2,128)S(1)} all-gather(f32[1,2,512]{2,1,0:T(2,128)S(1)} %fusion.11), channel_id=1, replica_groups=mesh['seq'=8,'head'=4] {'seq','head'}, dimensions={0}, use_global_device_ids=true | all-gather | bytes 135168 | tf_op jit(solution)/shard_map/all_gather | solution.py:110
  77.2 0.3 multiply_reduce_fusion.1
  77.5 0.1 fusion.73
  77.6 36.8 %all-gather.2 = bf16[32,2,512]{2,1,0:T(2,128)(2,1)S(1)} all-gather(bf16[1,2,512]{2,1,0:T(2,128)(2,1)S(1)} %fusion.73), channel_id=1, replica_groups=mesh['seq'=8,'head'=4] {'seq','head'}, dimensions={0}, use_global_device_ids=true | all-gather | bytes 67584 | tf_op jit(solution)/shard_map/all_gather | solution.py:147
  114.4 0.0 all-gather.5.cloned.1.call-done
  114.5 2.8 %fusion.30 = f32[16,512]{1,0:T(8,128)S(1)} fusion(bf16[4096,512]{1,0:T(8,128)(2,1)} %all-gather.5.cloned.1.call-done, f32[16,4096]{1,0:T(8,128)S(1)} %get-tuple-element.96), kind=kOutput, calls=%fused_computation.40 | convolution fusion | flops 67174400 | bytes 4489216 | tf_op jit(solution)/shard_map/dot_general | solution.py:140
  117.3 33.0 %all-reduce.1 = f32[16,512]{1,0:T(8,128)S(1)} all-reduce(f32[16,512]{1,0:T(8,128)S(1)} %fusion.30), channel_id=2, replica_groups=mesh['seq'=8,'head'=4] {'seq'}, use_global_device_ids=true, to_apply=%region_2.3.clone | all-reduce | flops 8192 | bytes 65536
  150.3 0.1 multiply_reduce_fusion.2
  150.4 0.1 fusion.74
  150.5 38.5 %all-gather = bf16[32,2,512]{2,1,0:T(2,128)(2,1)S(1)} all-gather(bf16[1,2,512]{2,1,0:T(2,128)(2,1)S(1)} %fusion.74), channel_id=1, replica_groups=mesh['seq'=8,'head'=4] {'seq','head'}, dimensions={0}, use_global_device_ids=true | all-gather | bytes 67584 | tf_op jit(solution)/shard_map/all_gather | solution.py:148
  189.1 0.3 exponential_reduce_fusion.1
  189.4 0.1 constant_dynamic-slice_fusion
  189.5 0.6 gather_fusion
  190.1 0.3 exponential_reduce_fusion
  190.4 0.5 multiply_subtract_fusion
  190.9 36.8 %all-reduce = f32[64]{0:T(128)S(1)} all-reduce(f32[64]{0:T(128)S(1)} %get-tuple-element.137), channel_id=1, replica_groups=mesh['seq'=8,'head'=4] {'seq','head'}, use_global_device_ids=true, to_apply=%add | all-reduce | flops 64 | bytes 512
  227.8 0.8 convolution_multiply_fusion
  (59 shorter events, 0.5 us)
Async XLA Ops:
  7.2 26.8 %copy-start = (bf16[1024,512]{1,0:T(8,128)(2,1)S(1)}, bf16[1024,512]{1,0:T(8,128)(2,1)}, u32[]{:S(2)}) copy-start(bf16[1024,512]{1,0:T(8,128)(2,1)} %param.15) | copy-start | bytes 3145732
  7.2 12.5 %copy-start.3 = (s32[64,16]{0,1:T(8,128)S(1)}, s32[64,16]{0,1:T(8,128)}, u32[]{:S(2)}) copy-start(s32[64,16]{0,1:T(8,128)} %param.17) | copy-start | bytes 12292
  7.2 107.3 %all-gather.5.cloned.1.call-start = ((), (), s32[]{:S(2)}) async-start(), calls=%async_computation | async-start | bytes 5242880 | tf_op jit(solution)/shard_map/all_gather | solution.py:131
  10.2 12.1 %copy-start.4 = (s32[2,2]{1,0:T(2,128)S(1)}, s32[2,2]{1,0:T(2,128)}, u32[]{:S(2)}) copy-start(s32[2,2]{1,0:T(2,128)} %param.18) | copy-start | bytes 52
  10.2 12.7 %copy-start.1 = (bf16[256,1024]{1,0:T(8,128)(2,1)S(1)}, bf16[256,1024]{1,0:T(8,128)(2,1)}, u32[]{:S(2)}) copy-start(bf16[256,1024]{1,0:T(8,128)(2,1)} %param.11) | copy-start | bytes 1572868
  12.0 11.7 %copy-start.6 = (u32[32]{0:T(128)S(1)}, u32[32]{0:T(128)}, u32[]{:S(2)}) copy-start(u32[32]{0:T(128)} %constant.147) | copy-start | bytes 388
  12.7 12.4 %copy-start.5 = (f32[1024]{0:T(1024)S(1)}, f32[1024]{0:T(1024)}, u32[]{:S(2)}) copy-start(f32[1024]{0:T(1024)} %param.12) | copy-start | bytes 12292
  12.7 16.4 %collective-permute-start = (bf16[256,512]{0,1:T(8,128)(2,1)}, bf16[256,512]{0,1:T(8,128)(2,1)}, u32[]{:S(2)}, u32[]{:S(2)}) collective-permute-start(bf16[256,512]{0,1:T(8,128)(2,1)} %pad_maximum_fusion.1), channel_id=1, source_target_pairs={{0,4},{4,8},{8,12},{12,16},{16,20},{20,24},{24,28},{1,5},{5,9},{9,... | collective-permute-start | bytes 786440 | tf_op jit(solution)/shard_map/ppermute | solution.py:19
  18.4 10.8 %collective-permute-start.1 = (bf16[256,512]{0,1:T(8,128)(2,1)}, bf16[256,512]{0,1:T(8,128)(2,1)}, u32[]{:S(2)}, u32[]{:S(2)}) collective-permute-start(bf16[256,512]{0,1:T(8,128)(2,1)} %pad_maximum_fusion.1), channel_id=1, source_target_pairs={{4,0},{8,4},{12,8},{16,12},{20,16},{24,20},{28,24},{5,1},{9,5},{13... | collective-permute-start | bytes 786440 | tf_op jit(solution)/shard_map/ppermute | solution.py:21
  32.1 1.5 copy-start.2
Sparse Core Ops, SparseCore 0:
  19.8 37.5 all-gather.4
where the time goes:
time: 237 us; the launch traced here: 235 us
  blocking collectives  188 us (79%)
  between operations  15.6 us (7%)
  matrix products  12.3 us (5%)
  other arithmetic  7.81 us (3%)
  starting transfers between devices  7 us (3%)
  waiting for transfers between devices  2.57 us (1%)
    unnamed x2, blocking collectives  69.8 us
    all_gather x1, blocking collectives, local(): lax.all_gather(partial_value, ('seq', 'head'), axis=0, tiled=True)  42.4 us
    all_gather x1, blocking collectives, local(): lax.all_gather(caption_own, ('seq', 'head'), axis=0, tiled=True)  38.5 us
    all_gather x1, blocking collectives, local(): lax.all_gather(interval_embedding_rows, ('seq', 'head'), axis=0, tiled=True)  36.8 us
    ppermute x1, starting transfers between devices, extended(): lax.ppermute(tail, axis, [(i, (i + 1) % count) for i in range(ends)])  5.68 us
  transfers between devices with their start and end apart: 3, of which 1 were waited for; matrix products, arithmetic and copies ran while one was open for 5% of the time, Pallas kernels for 0%

commit v1 on v0

v1 whole, which is shorter than its diff:
```python
import jax
import jax.numpy as jnp
from jax import lax
from jax.sharding import PartitionSpec as P

HDIM = 64
E = 512
BLK = 128
EVERY = ("seq", "head")
LANES = 128


def unit_rows(values):
    return (
        values * lax.rsqrt(jnp.mean(values * values, axis=-1, keepdims=True) + 1e-06) * E ** (-0.5)
    )


def to_everyone(piece, devices):
    return lax.all_to_all(jnp.broadcast_to(piece[None], (devices,) + piece.shape), EVERY, 0, 0)


def local(
    frames, norm_gain, w_qkv, w_out, w_proj, text_table, token_ids, span_bounds, contrast_divisor
):
    frame_rows = frames.shape[0]
    head_cols = w_qkv.shape[2]
    local_heads = head_cols // HDIM
    seq_count = lax.axis_size("seq")
    head_count = lax.axis_size("head")
    devices = seq_count * head_count
    own_caps = span_bounds.shape[0]
    all_caps = token_ids.shape[0]
    slot = lax.axis_index(EVERY)
    head_slot = lax.axis_index("head")
    total_frames = frame_rows * seq_count
    first_frame = lax.axis_index("seq") * frame_rows

    as32 = frames.astype(jnp.float32)
    normed = (
        as32 * lax.rsqrt(jnp.mean(as32 * as32, axis=-1, keepdims=True) + 1e-05) * norm_gain
    ).astype(jnp.bfloat16)
    keys_now = jnp.dot(normed, w_qkv[1], preferred_element_type=jnp.float32).astype(jnp.bfloat16)
    values_now = jnp.dot(normed, w_qkv[2], preferred_element_type=jnp.float32).astype(jnp.bfloat16)
    pairs = jnp.concatenate([keys_now, values_now], axis=1)
    ends = seq_count - 1
    before = lax.ppermute(pairs, "seq", [(i, i + 1) for i in range(ends)])
    after = lax.ppermute(pairs, "seq", [(i + 1, i) for i in range(ends)])
    queries = jnp.dot(normed, w_qkv[0], preferred_element_type=jnp.float32).astype(jnp.bfloat16)

    vocab = text_table.shape[0]
    words = slot * vocab + jnp.arange(vocab, dtype=jnp.int32)
    counts = (token_ids[:, :, None] == words[None, None, :]).astype(jnp.float32).sum(axis=1)
    part = jnp.dot(counts.astype(jnp.bfloat16), text_table, preferred_element_type=jnp.float32)
    bounds = jnp.pad((span_bounds // BLK).astype(jnp.float32), ((0, 0), (0, LANES - 2)))
    sent = jnp.concatenate(
        [
            part.reshape(devices, own_caps, E),
            jnp.broadcast_to(bounds[None], (devices,) + bounds.shape),
        ],
        axis=2,
    )
    got = lax.all_to_all(sent, EVERY, 0, 0)
    caption_own = unit_rows(got[:, :, :E].sum(axis=0)).astype(jnp.bfloat16)
    lower = got[:, :, E].reshape(all_caps, 1)
    upper = got[:, :, E + 1].reshape(all_caps, 1)

    padded = jnp.concatenate([before, pairs, after], axis=0)
    span_width = 3 * frame_rows
    query_part = queries.reshape(frame_rows, local_heads, HDIM)
    key_part = padded[:, :head_cols].reshape(span_width, local_heads, HDIM)
    value_part = padded[:, head_cols:].reshape(span_width, local_heads, HDIM)
    scores = jnp.einsum(
        "qhd,khd->hqk", query_part, key_part, preferred_element_type=jnp.float32
    ) * HDIM ** (-0.5)
    query_pos = first_frame + jnp.arange(frame_rows, dtype=jnp.int32)
    key_pos = first_frame - frame_rows + jnp.arange(span_width, dtype=jnp.int32)
    allowed = (
        (jnp.abs(query_pos[:, None] - key_pos[None, :]) <= frame_rows)
        & (key_pos >= 0)[None, :]
        & (key_pos < total_frames)[None, :]
    )
    scores = jnp.where(allowed[None], scores, -1e30)
    top = jnp.max(scores, axis=2, keepdims=True)
    probs = jnp.exp(scores - top)
    denom = jnp.sum(probs, axis=2)
    mixed = jnp.einsum(
        "hqk,khd->qhd", probs.astype(jnp.bfloat16), value_part, preferred_element_type=jnp.float32
    )
    attended = (mixed / denom.T[:, :, None]).astype(jnp.bfloat16).reshape(frame_rows, head_cols)

    block_count = frame_rows // BLK
    out_sums = attended.astype(jnp.float32).reshape(block_count, BLK, head_cols).sum(axis=1)
    own_features = lax.dynamic_slice_in_dim(as32, head_slot * head_cols, head_cols, 1)
    feature_sums = own_features.reshape(block_count, BLK, head_cols).sum(axis=1)
    proj_rows = lax.dynamic_slice_in_dim(w_proj, head_slot * head_cols, head_cols, 0)
    through_out = jnp.dot(out_sums, w_out.astype(jnp.float32), precision=lax.Precision.HIGHEST)
    partial_value = jnp.dot(
        through_out, w_proj.astype(jnp.float32), precision=lax.Precision.HIGHEST
    ) + jnp.dot(feature_sums, proj_rows.astype(jnp.float32), precision=lax.Precision.HIGHEST)

    everyone = to_everyone(
        jnp.concatenate([partial_value, caption_own.astype(jnp.float32)], axis=0), devices
    )
    block_table = (
        everyone[:, :block_count]
        .reshape(seq_count, head_count, block_count, E)
        .sum(axis=1)
        .reshape(seq_count * block_count, E)
    )
    captions = everyone[:, block_count:].reshape(all_caps, E).astype(jnp.bfloat16)
    block_ids = jnp.arange(seq_count * block_count, dtype=jnp.int32).astype(jnp.float32)
    span_mask = ((block_ids[None, :] >= lower) & (block_ids[None, :] < upper)).astype(jnp.float32)
    pooled = jnp.dot(span_mask, block_table, precision=lax.Precision.HIGHEST)
    spans = unit_rows(pooled).astype(jnp.bfloat16)

    divisor = contrast_divisor[0]
    logits = jnp.einsum("je,ie->ji", captions, spans, preferred_element_type=jnp.float32) * divisor
    grown = jnp.exp(logits)
    row_total = jnp.log(jnp.sum(grown, axis=1))
    first = slot * own_caps
    own_logits = lax.dynamic_slice_in_dim(logits, first, own_caps, 1)
    col_total = jnp.log(jnp.sum(jnp.exp(own_logits), axis=0))
    marker = (
        jnp.arange(all_caps, dtype=jnp.int32)[:, None]
        == first + jnp.arange(own_caps, dtype=jnp.int32)[None, :]
    ).astype(jnp.float32)
    own_square = jnp.sum(own_logits * marker, axis=0)
    own_row_total = lax.dynamic_slice_in_dim(row_total, first, own_caps, 0)
    loss_terms = 0.5 * (own_row_total + col_total) - own_square
    weights = (
        0.5 * jnp.exp(own_logits - row_total[:, None])
        + 0.5 * jnp.exp(own_logits - col_total[None, :])
        - marker
    ).astype(jnp.bfloat16)
    derivative = (
        jnp.einsum("ji,je->ie", weights, captions, preferred_element_type=jnp.float32) * divisor
    )
    return (derivative, loss_terms)


def solution(mesh):
    placed = (
        P("seq", None),
        P(),
        P(None, None, "head"),
        P("head", None),
        P(),
        P(EVERY, None),
        P(),
        P(EVERY, None),
        P(),
    )
    return jax.shard_map(
        local,
        mesh=mesh,
        in_specs=placed,
        out_specs=(P(EVERY, None), P(EVERY)),
        check_vma=False,
    )
```

time: 237 us -> 49.6 us (0.21)
  blocking collectives: 188 us -> 0 us
  between operations: 15.6 us -> 1.67 us
  starting transfers between devices: 7 us -> 18.7 us
  waiting for transfers between devices: 2.57 us -> 10.5 us
  matrix products: 12.3 us -> 9.46 us
    all_gather x3 -> x0, blocking collectives: 118 us -> none  [the longest x1 42.4 us: local(): lax.all_gather(partial_value, ('seq', 'head'), axis=0, tiled=True)]
    unnamed x2 -> x0, blocking collectives: 69.8 us -> none
    all_to_all x0 -> x2, starting transfers between devices: none -> 11.9 us  [the longest x1 6.98 us: local(): got = lax.all_to_all(sent, EVERY, 0, 0)]
    all_to_all x0 -> x2, waiting for transfers between devices: none -> 10.5 us  [the longest x1 9.51 us: to_everyone(): lax.all_to_all(jnp.broadcast_to(piece[None], (devices,) + piece.shape), E...]
    dot_general x6 -> x5, matrix products: 6.06 us -> 3.15 us  [the longest x1 1.04 us: local(): jnp.einsum('hqk,khd->qhd', probs.astype(jnp.bfloat16), value_part, prefer...]
    ppermute x2, waiting for transfers between devices: 2.53 us -> 0.01 us  [the longest x1 0.01 us: local(): before = lax.ppermute(pairs, 'seq', [(i, i + 1) for i in range(ends)])]
  transfers between devices with their start and end apart: 3 -> 4, of which waited for: 1 -> 2; matrix products, arithmetic and copies ran while one was open for 5% -> 21% of each run, Pallas kernels for 0% -> 0%
where the time goes in v1:
time: 49.6 us; the launch traced here: 49.2 us
  starting transfers between devices  18.7 us (38%)
  waiting for transfers between devices  10.5 us (21%)
  matrix products  9.46 us (19%)
  other arithmetic  7.03 us (14%)
  local copies, waits for them, and re-layouts  1.82 us (4%)
  between operations  1.67 us (3%)
    all_to_all x1, waiting for transfers between devices, to_everyone(): lax.all_to_all(jnp.broadcast_to(piece[None], (devices,) + piece.shape), E...  9.51 us
    all_to_all x1, starting transfers between devices, local(): got = lax.all_to_all(sent, EVERY, 0, 0)  6.98 us
    ppermute x1, starting transfers between devices, local(): before = lax.ppermute(pairs, 'seq', [(i, i + 1) for i in range(ends)])  5.55 us
    all_to_all x1, starting transfers between devices, to_everyone(): lax.all_to_all(jnp.broadcast_to(piece[None], (devices,) + piece.shape), E...  4.89 us
    dot_general x1, matrix products, local(): jnp.dot(normed, w_qkv[2], preferred_element_type=jnp.float32)  1.72 us
    dot_general x1, matrix products, local(): jnp.dot(normed, w_qkv[1], preferred_element_type=jnp.float32)  1.67 us
    dot_general x1, matrix products, local(): jnp.dot(normed, w_qkv[0], preferred_element_type=jnp.float32)  1.49 us
    reduce_sum x1, other arithmetic, local(): jnp.mean(as32 * as32, axis=-1, keepdims=True) + 1e-05  1.31 us
  transfers between devices with their start and end apart: 4, of which 2 were waited for; matrix products, arithmetic and copies ran while one was open for 21% of the time, Pallas kernels for 0%

profile of v1, /device:TPU:0, one launch (start us, length us, event | category | flops | bytes accessed | tf_op | source)
XLA Modules:
  0.0 49.2 jit_solution(17722274948348001519)
XLA Ops:
  0.6 0.0 copy-start
  0.6 0.0 copy-start.4
  0.7 0.0 copy-start.5
  0.7 1.3 %multiply_reduce_fusion = f32[256]{0:T(256)S(1)} fusion(bf16[256,1024]{1,0:T(8,128)(2,1)} %param.9), kind=kLoop, calls=%fused_computation.19 | loop fusion | flops 786176 | bytes 525312 | tf_op jit(solution)/shard_map/reduce_sum | solution.py:41
  2.0 0.0 copy-start.1
  2.0 1.7 %convolution_convert_fusion.1 = bf16[256,256]{0,1:T(8,128)(2,1)S(1)} fusion(bf16[3,1024,256]{2,1,0:T(8,128)(2,1)} %param.11, f32[1024]{0:T(1024)} %param.10, f32[256]{0:T(256)S(1)} %add_rsqrt_fusion, bf16[256,1024]{1,0:T(8,128)(2,1)} %param.9), kind=kOutput, calls=%fused_computation.10 | convolution fusion | flops 135331840 | bytes 1184768 | tf_op jit(solution)/shard_map/dot_general | solution.py:44
  3.7 0.0 copy-start.6
  3.7 1.7 %convolution_convert_fusion.2 = bf16[256,256]{0,1:T(8,128)(2,1)S(1)} fusion(bf16[3,1024,256]{2,1,0:T(8,128)(2,1)} %param.11, f32[1024]{0:T(1024)} %param.10, f32[256]{0:T(256)S(1)} %add_rsqrt_fusion, bf16[256,1024]{1,0:T(8,128)(2,1)} %param.9), kind=kOutput, calls=%fused_computation.11 | convolution fusion | flops 135331840 | bytes 1184768 | tf_op jit(solution)/shard_map/dot_general | solution.py:43
  5.4 5.6 %collective-permute-start = (bf16[256,512]{0,1:T(8,128)(2,1)S(1)}, bf16[256,512]{0,1:T(8,128)(2,1)}, u32[]{:S(2)}, u32[]{:S(2)}) collective-permute-start(bf16[256,512]{0,1:T(8,128)(2,1)S(1)} %pad_maximum_fusion.1), channel_id=1, source_target_pairs={{0,4},{4,8},{8,12},{12,16},{16,20},{20,24},{24,28},{1,5},{5,9},{9,... | collective-permute-start | bytes 786440 | tf_op jit(solution)/shard_map/ppermute | solution.py:47
  11.0 1.3 %collective-permute-start.1 = (bf16[256,512]{0,1:T(8,128)(2,1)S(1)}, bf16[256,512]{0,1:T(8,128)(2,1)}, u32[]{:S(2)}, u32[]{:S(2)}) collective-permute-start(bf16[256,512]{0,1:T(8,128)(2,1)S(1)} %pad_maximum_fusion.1), channel_id=1, source_target_pairs={{4,0},{8,4},{12,8},{16,12},{20,16},{24,20},{28,24},{5,1},{9,5},{13... | collective-permute-start | bytes 786440 | tf_op jit(solution)/shard_map/ppermute | solution.py:48
  12.3 0.0 copy-done.4
  12.3 0.1 copy.25
  12.4 1.0 %convert_reduce_fusion = bf16[64,1024]{1,0:T(8,128)(2,1)S(1)} fusion(s32[1024]{0:T(1024)S(1)} %iota_add_fusion, s32[64,16]{1,0:T(8,128)S(1)} %copy.25), kind=kLoop, calls=%fused_computation | loop fusion | flops 3080192 | bytes 139264 | tf_op jit(solution)/shard_map/reduce_sum | solution.py:53
  13.4 0.0 copy-done
  13.4 0.3 fusion.54
  13.7 0.1 reshape.160
  13.8 0.0 copy-done.5
  13.9 0.7 %pad_maximum_fusion.2 = f32[32,2,640]{2,1,0:T(2,128)} fusion(f32[32,2,128]{2,1,0:T(2,128)S(1)} %broadcast_in_dim.14, f32[32,2,512]{2,1,0:T(2,128)S(1)} %reshape.160), kind=kLoop, calls=%fused_computation.34 | loop fusion | flops 40960 | bytes 327680 | tf_op jit(solution)/shard_map/concatenate | solution.py:56
  14.6 7.0 %all-to-all-start = ((f32[32,2,640]{2,1,0:T(2,128)}), f32[32,2,640]{2,1,0:T(2,128)S(1)}, u32[]{:S(2)}, u32[]{:S(2)}) async-start(f32[32,2,640]{2,1,0:T(2,128)} %pad_maximum_fusion.2), calls=%async_computation | async-start | bytes 327680 | tf_op jit(solution)/shard_map/all_to_all | solution.py:63
  21.6 0.3 fusion.19
  22.0 0.0 copy-done.1
  22.0 0.1 convert_element_type.71
  22.1 0.0 copy-done.6
  22.2 1.5 %convolution_convert_fusion = bf16[256,256]{0,1:T(8,128)(2,1)S(1)} fusion(bf16[3,1024,256]{2,1,0:T(8,128)(2,1)} %param.11, f32[1024]{0:T(1024)S(1)} %copy-done.6, f32[256]{0:T(256)S(1)} %add_rsqrt_fusion, bf16[256,1024]{1,0:T(8,128)(2,1)S(1)} %copy-done.1), kind=kOutput, calls=%fused_computation.9 | convolution fusion | flops 135331840 | bytes 1184768 | tf_op jit(solution)/shard_map/dot_general | solution.py:49
  23.6 0.0 collective-permute-done
  23.7 0.0 collective-permute-done.1
  23.7 1.1 %pad_maximum_fusion = bf16[768,512]{0,1:T(8,128)(2,1)S(1)} fusion(bf16[256,512]{0,1:T(8,128)(2,1)} %collective-permute-done.1, bf16[256,256]{0,1:T(8,128)(2,1)S(1)} %convolution_convert_fusion.1, bf16[256,256]{0,1:T(8,128)(2,1)S(1)} %convolution_convert_fusion.2, bf16[256,512]{0,1:T(8,128)(2,1)} %collective-permute-done), kind=kLoop, calls=%fused_computation.20 | loop fusion | flops 3145728 | bytes 1572864 | tf_op jit(solution)/shard_map/concatenate | solution.py:68
  24.8 0.1 fusion.51
  24.8 0.8 %fusion = (f32[4,256]{1,0:T(4,128)S(1)}, f32[4,256,768]{2,1,0:T(8,128)S(1)}) fusion(pred[256,768]{1,0:T(8,128)(4,1)S(1)} %fusion.19, bf16[256,4,64]{0,2,1:T(8,128)(2,1)S(1)} %bitcast.45, bf16[768,4,64]{0,2,1:T(8,128)(2,1)S(1)} %bitcast.43), kind=kOutput, calls=%fused_computation.3 | convolution fusion | flops 103021568 | bytes 3870720 | tf_op jit(solution)/shard_map/qhd,khd->hqk/dot_general | solution.py:73
  25.6 0.9 %fusion.1 = f32[4,256]{1,0:T(4,128)S(1)} fusion(f32[4,256,768]{2,1,0:T(8,128)S(1)} %get-tuple-element.11, f32[4,256]{1,0:T(4,128)S(1)} %get-tuple-element.10, pred[256,768]{1,0:T(8,128)(4,1)S(1)} %fusion.19), kind=kLoop, calls=%fused_computation.4 | loop fusion | flops 3144704 | bytes 3350528 | tf_op jit(solution)/shard_map/reduce_sum | solution.py:86
  26.6 0.0 copy-start.3
  26.6 0.0 copy-start.2
  26.6 1.0 %fusion.15 = f32[256,4,64]{0,2,1:T(8,128)S(1)} fusion(bf16[768,4,64]{0,2,1:T(8,128)(2,1)S(1)} %bitcast.44, f32[4,256,768]{2,1,0:T(8,128)S(1)} %get-tuple-element.11, f32[4,256]{1,0:T(4,128)S(1)} %get-tuple-element.10, pred[256,768]{1,0:T(8,128)(4,1)S(1)} %fusion.19, f32[256,4]{0,1:T(4,128)S(1)} %bitcast.46), kind=kOutput, calls=%fused_computation.17 | convolution fusion | flops 104005632 | bytes 4005888 | tf_op jit(solution)/shard_map/hqk,khd->qhd/dot_general | solution.py:87
  27.6 0.1 reshape.163
  27.8 0.3 reduce_sum.110
  28.1 0.0 copy-done.3
  28.1 0.4 fusion.52
  28.5 0.0 copy-done.2
  28.5 0.5 %fusion.53 = f32[2,512]{1,0:T(2,128)S(1)} fusion(f32[2,1024]{1,0:T(2,128)S(1)} %fusion.52, bf16[1024,512]{1,0:T(8,128)(2,1)S(1)} %copy-done.2), kind=kOutput, calls=%fused_computation.90 | convolution fusion | flops 12582912 | bytes 1060864 | tf_op jit(solution)/shard_map/dot_general | solution.py:98
  29.0 0.2 convolution_add_fusion
  29.2 1.0 %all-to-all-done = f32[32,2,640]{2,1,0:T(2,128)S(1)} async-done(((f32[32,2,640]{2,1,0:T(2,128)}), f32[32,2,640]{2,1,0:T(2,128)S(1)}, u32[]{:S(2)}, u32[]{:S(2)}) %all-to-all-start) | async-done | bytes 163872 | tf_op jit(solution)/shard_map/all_to_all | solution.py:63
  30.2 0.1 slice_reduce_fusion
  30.2 0.1 copy.30
  30.4 0.1 multiply_reduce_fusion.1
  30.5 0.1 fusion.40
  30.6 0.7 %broadcast_in_dim.15 = f32[32,4,512]{2,1,0:T(4,128)} broadcast(f32[4,512]{1,0:T(4,128)S(1)} %pad_maximum_fusion.3), dimensions={1,2} | broadcast | bytes 270336 | tf_op jit(solution)/shard_map/broadcast_in_dim | solution.py:20
  31.3 4.9 %all-to-all-start.1 = ((f32[32,4,512]{2,1,0:T(4,128)}), f32[32,4,512]{2,1,0:T(4,128)S(1)}, u32[]{:S(2)}, u32[]{:S(2)}) async-start(f32[32,4,512]{2,1,0:T(4,128)} %broadcast_in_dim.15), calls=%async_computation.1 | async-start | bytes 524288 | tf_op jit(solution)/shard_map/all_to_all | solution.py:20
  36.9 0.2 slice_reduce_fusion.2
  37.1 0.1 ge.30
  37.2 0.1 lt.34
  37.3 9.5 %all-to-all-done.1 = f32[32,4,512]{2,1,0:T(4,128)S(1)} async-done(((f32[32,4,512]{2,1,0:T(4,128)}), f32[32,4,512]{2,1,0:T(4,128)S(1)}, u32[]{:S(2)}, u32[]{:S(2)}) %all-to-all-start.1) | async-done | bytes 262176 | tf_op jit(solution)/shard_map/all_to_all | solution.py:20
  46.9 0.3 multiply_reduce_fusion.2
  47.2 0.1 slice.65
  47.4 0.2 exponential_reduce_fusion
  47.6 0.2 select_reduce_fusion
  47.8 0.6 %multiply_subtract_fusion = (f32[2]{0:T(128)}, f32[2]{0:T(128)S(1)}) fusion(f32[2]{0:T(128)S(1)} %get-tuple-element.4, f32[64]{0:T(128)S(1)} %log.14, s32[]{:T(128)S(6)} %select_n.20, f32[2]{0:T(128)S(1)} %get-tuple-element.5), kind=kLoop, calls=%fused_computation.75 | loop fusion | flops 6 | bytes 44 | tf_op jit(solution)/shard_map/sub | solution.py:130
  48.4 0.8 %convolution_multiply_fusion.1 = f32[2,512]{1,0:T(2,128)} fusion(bf16[64,512]{1,0:T(8,128)(2,1)S(1)} %convert_element_type.85, f32[]{:T(128)} %bitcast.42, s32[2]{0:T(128)S(1)} %iota_add_fusion.3, f32[2]{0:T(128)S(1)} %get-tuple-element.9, f32[64]{0:T(128)S(1)} %log.14, f32[64,64]{0,1:T(8,128)S(1)} %get-tuple-element.15, s32[]{:T(128)S(6)} %select_n.20), kind=kOutput, calls=%fused_computation.13 | convolution fusion | flops 133120 | bytes 72200 | tf_op jit(solution)/shard_map/ji,je->ie/dot_general | solution.py:137
  (19 shorter events, 0.3 us)
Async XLA Ops:
  0.6 12.8 %copy-start = (bf16[1024,512]{1,0:T(8,128)(2,1)S(1)}, bf16[1024,512]{1,0:T(8,128)(2,1)}, u32[]{:S(2)}) copy-start(bf16[1024,512]{1,0:T(8,128)(2,1)} %param.14) | copy-start | bytes 3145732
  0.6 11.6 %copy-start.4 = (s32[64,16]{0,1:T(8,128)S(1)}, s32[64,16]{0,1:T(8,128)}, u32[]{:S(2)}) copy-start(s32[64,16]{0,1:T(8,128)} %param.15) | copy-start | bytes 12292
  0.7 13.2 %copy-start.5 = (s32[2,2]{1,0:T(2,128)S(1)}, s32[2,2]{1,0:T(2,128)}, u32[]{:S(2)}) copy-start(s32[2,2]{1,0:T(2,128)} %param.16) | copy-start | bytes 52
  2.0 20.0 %copy-start.1 = (bf16[256,1024]{1,0:T(8,128)(2,1)S(1)}, bf16[256,1024]{1,0:T(8,128)(2,1)}, u32[]{:S(2)}) copy-start(bf16[256,1024]{1,0:T(8,128)(2,1)} %param.9) | copy-start | bytes 1572868
  3.7 18.4 %copy-start.6 = (f32[1024]{0:T(1024)S(1)}, f32[1024]{0:T(1024)}, u32[]{:S(2)}) copy-start(f32[1024]{0:T(1024)} %param.10) | copy-start | bytes 12292
  5.4 18.2 %collective-permute-start = (bf16[256,512]{0,1:T(8,128)(2,1)S(1)}, bf16[256,512]{0,1:T(8,128)(2,1)}, u32[]{:S(2)}, u32[]{:S(2)}) collective-permute-start(bf16[256,512]{0,1:T(8,128)(2,1)S(1)} %pad_maximum_fusion.1), channel_id=1, source_target_pairs={{0,4},{4,8},{8,12},{12,16},{16,20},{20,24},{24,28},{1,5},{5,9},{9,... | collective-permute-start | bytes 786440 | tf_op jit(solution)/shard_map/ppermute | solution.py:47
  11.0 12.7 %collective-permute-start.1 = (bf16[256,512]{0,1:T(8,128)(2,1)S(1)}, bf16[256,512]{0,1:T(8,128)(2,1)}, u32[]{:S(2)}, u32[]{:S(2)}) collective-permute-start(bf16[256,512]{0,1:T(8,128)(2,1)S(1)} %pad_maximum_fusion.1), channel_id=1, source_target_pairs={{4,0},{8,4},{12,8},{16,12},{20,16},{24,20},{28,24},{5,1},{9,5},{13... | collective-permute-start | bytes 786440 | tf_op jit(solution)/shard_map/ppermute | solution.py:48
  14.6 15.6 %all-to-all-start = ((f32[32,2,640]{2,1,0:T(2,128)}), f32[32,2,640]{2,1,0:T(2,128)S(1)}, u32[]{:S(2)}, u32[]{:S(2)}) async-start(f32[32,2,640]{2,1,0:T(2,128)} %pad_maximum_fusion.2), calls=%async_computation | async-start | bytes 327680 | tf_op jit(solution)/shard_map/all_to_all | solution.py:63
  26.6 1.6 %copy-start.3 = (bf16[256,1024]{1,0:T(8,128)(2,1)S(1)}, bf16[256,1024]{1,0:T(8,128)(2,1)}, u32[]{:S(2)}) copy-start(bf16[256,1024]{1,0:T(8,128)(2,1)} %param.12) | copy-start | bytes 1572868
  26.6 1.9 %copy-start.2 = (bf16[1024,512]{1,0:T(8,128)(2,1)S(1)}, bf16[1024,512]{1,0:T(8,128)(2,1)}, u32[]{:S(2)}) copy-start(bf16[1024,512]{1,0:T(8,128)(2,1)} %param.13) | copy-start | bytes 3145732
  31.3 15.5 %all-to-all-start.1 = ((f32[32,4,512]{2,1,0:T(4,128)}), f32[32,4,512]{2,1,0:T(4,128)S(1)}, u32[]{:S(2)}, u32[]{:S(2)}) async-start(f32[32,4,512]{2,1,0:T(4,128)} %broadcast_in_dim.15), calls=%async_computation.1 | async-start | bytes 524288 | tf_op jit(solution)/shard_map/all_to_all | solution.py:20

commit v2 on v1

v2 whole, which is shorter than its diff:
```python
import functools

import jax
import jax.numpy as jnp
from jax import lax
from jax.experimental import pallas as pl
from jax.experimental.pallas import tpu as pltpu
from jax.sharding import PartitionSpec as P

HDIM = 64
E = 512
BLK = 128
EVERY = ("seq", "head")
LANES = 128
SUB = 8
NEVER = -1e30
PIECE = jnp.bfloat16
VMEM = pl.BlockSpec(memory_space=pltpu.VMEM)
SMEM = pl.BlockSpec(memory_space=pltpu.SMEM)
ANY = pl.BlockSpec(memory_space=pl.ANY)
HIGHEST = lax.Precision.HIGHEST


def call(body, outs, ins, scratch=(), cost=(0, 0, 0), mib=40):
    return pl.pallas_call(
        body,
        out_shape=outs,
        in_specs=ins,
        out_specs=jax.tree.map(lambda _: VMEM, outs),
        scratch_shapes=scratch,
        compiler_params=pltpu.CompilerParams(vmem_limit_bytes=mib << 20),
        cost_estimate=pl.CostEstimate(
            flops=cost[0], bytes_accessed=cost[1], transcendentals=cost[2]
        ),
    )


def transposed_dot(left, right):
    return lax.dot_general(
        left, right, (((1,), (1,)), ((), ())), preferred_element_type=jnp.float32
    )


def qkv_kernel(
    frames_hbm, gain_ref, w_hbm, own_ref, p1_ref, p2_ref, p3_ref, frames, w, normed, sems
):
    rows = frames.shape[0]
    half = own_ref.shape[1]
    copies = [pltpu.make_async_copy(frames_hbm, frames, sems.at[0])] + [
        pltpu.make_async_copy(w_hbm.at[k], w.at[k], sems.at[1 + k]) for k in range(3)
    ]
    for k in (0, 2, 3, 1):
        copies[k].start()
    odd = lax.axis_index("seq") % 2 == 1
    copies[0].wait()
    step = min(64, rows)
    for r in range(0, rows, step):
        part = frames[r : r + step].astype(jnp.float32)
        scale = lax.rsqrt(jnp.mean(part * part, axis=-1, keepdims=True) + 1e-05)
        normed[r : r + step] = (part * scale * gain_ref[...]).astype(jnp.bfloat16)
    for k in (1, 2, 0):
        copies[1 + k].wait()
        both = jnp.dot(normed[...], w[k], preferred_element_type=jnp.float32).astype(jnp.bfloat16)
        if k == 0:
            both = both * jnp.bfloat16(HDIM ** (-0.5))
        mine = jnp.where(odd, both[:, half:], both[:, :half])
        other = jnp.where(odd, both[:, :half], both[:, half:])
        own_ref[k * rows : (k + 1) * rows] = mine
        p1_ref[k * rows : (k + 1) * rows] = other
        if k > 0:
            p2_ref[(k - 1) * rows : k * rows] = mine
            p3_ref[(k - 1) * rows : k * rows] = other


def text_kernel(ids_ref, table_ref, bounds_ref, t32_ref, t16_ref):
    caps, tokens = ids_ref.shape
    vocab = table_ref.shape[0]
    own_caps = bounds_ref.shape[0]
    slot = lax.axis_index("seq") * lax.axis_size("head") + lax.axis_index("head")
    ids = ids_ref[...] - slot * vocab
    words = lax.broadcasted_iota(jnp.int32, (caps, vocab), 1)
    counts = jnp.zeros((caps, vocab), jnp.float32)
    for t in range(tokens):
        counts = counts + jnp.where(ids[:, t : t + 1] == words, 1.0, 0.0)
    part = jnp.dot(counts.astype(jnp.bfloat16), table_ref[...], preferred_element_type=jnp.float32)
    chunks = [part[:, c : c + LANES] for c in range(0, E, LANES)]
    row = lax.broadcasted_iota(jnp.int32, (caps, LANES), 0)
    lane = lax.broadcasted_iota(jnp.int32, (caps, LANES), 1)
    bounds = jnp.zeros((caps, LANES), jnp.float32)
    for c in range(own_caps):
        for side in range(2):
            block = (bounds_ref[c, side] // BLK).astype(jnp.float32)
            bounds = jnp.where((row == slot * own_caps + c) & (lane == side), block, bounds)
    chunks.append(bounds)
    for c, chunk in enumerate(chunks):
        t32_ref[c * caps : (c + 1) * caps] = chunk
        t16_ref[c * caps : (c + 1) * caps] = chunk.astype(jnp.bfloat16)


def weights_kernel(frames_ref, w_out_ref, w_proj_ref, wc_ref, fp_ref):
    half = wc_ref.shape[0]
    cols = w_out_ref.shape[0]
    blocks = fp_ref.shape[0]
    odd = lax.axis_index("seq") % 2
    start = pl.multiple_of(lax.axis_index("head") * cols, LANES)
    wc_ref[...] = jnp.dot(
        w_out_ref[pl.ds(pl.multiple_of(odd * half, half), half), :],
        w_proj_ref[...],
        preferred_element_type=jnp.float32,
    )
    features = frames_ref[:, pl.ds(start, cols)].astype(jnp.float32)
    sums = jnp.sum(features.reshape(blocks, BLK, cols), axis=1)
    padded = jnp.concatenate([sums, jnp.zeros((SUB - blocks, cols), jnp.float32)], axis=0)
    fp_ref[...] = jnp.dot(
        padded, w_proj_ref[pl.ds(start, cols), :].astype(jnp.float32), precision=HIGHEST
    )[:blocks]


def attend_kernel(own_ref, r1_ref, r2_ref, r3_ref, wc_ref, fp_ref, out_ref):
    rows = own_ref.shape[0] // 3
    half = own_ref.shape[1]
    blocks = rows // BLK
    seq, last = lax.axis_index("seq"), lax.axis_size("seq") - 1
    odd = seq % 2
    apart = lax.broadcasted_iota(jnp.int32, (rows, rows), 0) - lax.broadcasted_iota(
        jnp.int32, (rows, rows), 1
    )
    lane = lax.broadcasted_iota(jnp.int32, (rows, half), 1)

    def block_sums(me, other, halo, parity, exists):
        side = jnp.where(parity == 0, apart, -apart)
        near = side >= 0
        far = side <= jnp.where(exists, 0, -2 * rows)
        query = me[0:rows]
        attended = jnp.zeros((rows, half), jnp.float32)
        for head in range(half // HDIM):
            mine = lane // HDIM == head
            q = jnp.where(mine, query, jnp.zeros_like(query))
            scores = [
                transposed_dot(q, me[rows : 2 * rows]),
                jnp.where(near, transposed_dot(q, other[rows : 2 * rows]), NEVER),
                jnp.where(far, transposed_dot(q, halo[0:rows]), NEVER),
            ]
            top = functools.reduce(jnp.maximum, [jnp.max(s, axis=1, keepdims=True) for s in scores])
            probs = [jnp.exp(s - top) for s in scores]
            denom = sum(jnp.sum(p, axis=1, keepdims=True) for p in probs)
            values = (me[2 * rows : 3 * rows], other[2 * rows : 3 * rows], halo[rows : 2 * rows])
            mixed = sum(
                jnp.dot(p.astype(jnp.bfloat16), v, preferred_element_type=jnp.float32)
                for p, v in zip(probs, values)
            )
            attended = jnp.where(mine, mixed / denom, attended)
        attended = attended.astype(jnp.bfloat16).astype(jnp.float32)
        return jnp.sum(attended.reshape(blocks, BLK, half), axis=1)

    here = block_sums(own_ref, r1_ref, r3_ref, odd, jnp.where(odd == 0, seq > 0, seq < last))
    there = block_sums(
        r1_ref, own_ref, r2_ref, 1 - odd, jnp.where(odd == 0, seq + 1 < last, seq > 1)
    )
    first = jnp.where(odd == 0, here, there)
    second = jnp.where(odd == 0, there, here)
    blank = jnp.zeros((SUB - 2 * blocks, half), jnp.float32)
    table = jnp.dot(jnp.concatenate([first, second, blank], axis=0), wc_ref[...], precision=HIGHEST)
    feature = fp_ref[...]
    none = jnp.zeros_like(feature)
    table = table[: 2 * blocks] + jnp.concatenate(
        [jnp.where(odd == 0, feature, none), jnp.where(odd == 0, none, feature)], axis=0
    )
    piece = jnp.concatenate([table[:, : E // 2], table[:, E // 2 :]], axis=0).astype(out_ref.dtype)
    out_ref[...] = jnp.broadcast_to(piece[None], out_ref.shape)


def tail_kernel(everyone_ref, mine_ref, last_ref, divisor_ref, derivative_ref, loss_ref):
    own_caps = derivative_ref.shape[0]
    devices, width, half = everyone_ref.shape
    caps = mine_ref.shape[0] // (E // LANES + 1)
    group = 2 * lax.axis_size("head")
    pairs = devices // group
    blocks = width // 2
    slot = lax.axis_index("seq") * lax.axis_size("head") + lax.axis_index("head")
    divisor = divisor_ref[0]

    total = mine_ref[...] + last_ref[...].astype(jnp.float32)
    raw = jnp.concatenate(
        [total[c * caps : (c + 1) * caps] for c in range(E // LANES)], axis=1
    )
    bounds = total[E // LANES * caps :]
    lower, upper = bounds[:, 0:1], bounds[:, 1:2]

    def unit(parts):
        mean = sum(jnp.sum(p * p, axis=-1, keepdims=True) for p in parts) * (1.0 / E)
        scale = lax.rsqrt(mean + 1e-06)
        parts = [(p * scale * E ** (-0.5)).astype(jnp.bfloat16) for p in parts]
        return parts[0] if len(parts) == 1 else jnp.concatenate(parts, axis=1)

    captions = unit([raw])
    sums = jnp.sum(
        everyone_ref[...].astype(jnp.float32).reshape(pairs, group, width, half), axis=1
    ).reshape(pairs * width, half)
    place = lax.broadcasted_iota(jnp.int32, (caps, pairs * width), 1)
    inner = place % width
    block = (place // width * blocks + inner % blocks).astype(jnp.float32)
    inside = (block >= lower) & (block < upper)
    pooled = [
        jnp.dot(
            jnp.where(inside & (inner // blocks == side), 1.0, 0.0), sums, precision=HIGHEST
        )
        for side in range(2)
    ]
    spans = unit(pooled)

    logits = transposed_dot(spans, captions) * divisor
    row_total = jnp.log(jnp.sum(jnp.exp(logits), axis=0, keepdims=True))
    tall = -(-own_caps // SUB) * SUB
    row = lax.broadcasted_iota(jnp.int32, (tall, caps), 0)
    marker = jnp.where(
        (row < own_caps) & (lax.broadcasted_iota(jnp.int32, (tall, caps), 1) == slot * own_caps + row),
        1.0,
        0.0,
    )
    own_spans = jnp.dot(
        marker.astype(jnp.bfloat16), spans, preferred_element_type=jnp.float32
    ).astype(jnp.bfloat16)
    own = transposed_dot(own_spans, captions) * divisor
    col_total = jnp.log(jnp.sum(jnp.exp(own), axis=1, keepdims=True))
    loss = 0.5 * (jnp.sum(marker * row_total, axis=1, keepdims=True) + col_total) - jnp.sum(
        marker * own, axis=1, keepdims=True
    )
    flip = lax.broadcasted_iota(jnp.int32, (tall, tall), 0) == lax.broadcasted_iota(
        jnp.int32, (tall, tall), 1
    )
    loss_ref[...] = jnp.sum(jnp.where(flip, loss, 0.0), axis=0, keepdims=True)[:, :own_caps]
    weights = (
        0.5 * jnp.exp(own - row_total) + 0.5 * jnp.exp(own - col_total) - marker
    ).astype(jnp.bfloat16)
    derivative = jnp.dot(weights, captions, preferred_element_type=jnp.float32) * divisor
    derivative_ref[...] = derivative[:own_caps]


def local(
    frames, norm_gain, w_qkv, w_out, w_proj, text_table, token_ids, span_bounds, contrast_divisor
):
    rows, width = frames.shape
    cols = w_qkv.shape[2]
    half = cols // 2
    seq_count, head_count = lax.axis_size("seq"), lax.axis_size("head")
    devices = seq_count * head_count
    own_caps = span_bounds.shape[0]
    blocks = rows // BLK
    shape = jax.ShapeDtypeStruct
    bf16, f32 = jnp.bfloat16, jnp.float32

    own, p1, p2, p3 = call(
        qkv_kernel,
        [shape((n * rows, half), bf16) for n in (3, 3, 2, 2)],
        [ANY, VMEM, ANY],
        [
            pltpu.VMEM(frames.shape, bf16),
            pltpu.VMEM(w_qkv.shape, bf16),
            pltpu.VMEM(frames.shape, bf16),
            pltpu.SemaphoreType.DMA((4,)),
        ],
        (6 * rows * width * cols, 2 * w_qkv.size, 0),
    )(frames, norm_gain[None], w_qkv)
    ends = seq_count - 1
    r1 = lax.ppermute(p1, "seq", [(s, s ^ 1) for s in range(seq_count)])
    r3 = lax.ppermute(
        p3,
        "seq",
        [(s, s + 1) for s in range(1, ends, 2)] + [(s, s - 1) for s in range(2, seq_count, 2)],
    )
    r2 = lax.ppermute(
        p2,
        "seq",
        [(s, s + 2) for s in range(1, ends - 1, 2)] + [(s, s - 2) for s in range(2, seq_count, 2)],
    )

    ids, _ = lax.optimization_barrier((token_ids, own))
    tall = (E // LANES + 1) * token_ids.shape[0]
    mine, sent = call(
        text_kernel,
        [shape((tall, LANES), f32), shape((tall, LANES), bf16)],
        [VMEM, VMEM, SMEM],
        cost=(2 * token_ids.shape[0] * text_table.size, 2 * text_table.size, 0),
    )(ids, text_table, span_bounds)

    def swap(mine, sent, axis, step):
        count = lax.axis_size(axis)
        return lax.ppermute(sent, axis, [(i, i ^ step) for i in range(count)])

    def add(mine, got):
        mine = mine + got.astype(f32)
        return mine, mine.astype(bf16)

    step = 1
    while step < head_count:
        mine, sent = add(mine, swap(mine, sent, "head", step))
        step *= 2

    wc, fp = call(
        weights_kernel,
        [shape((half, E), f32), shape((blocks, E), f32)],
        [VMEM] * 3,
        cost=(2 * half * w_proj.size, 2 * (w_proj.size + w_out.size + frames.size), 0),
    )(frames, w_out, w_proj)

    piece = call(
        attend_kernel,
        shape((devices, 4 * blocks, E // 2), PIECE),
        [VMEM] * 6,
        cost=(24 * rows * rows * cols, 10 * rows * cols, 6 * rows * rows * cols // HDIM),
    )(own, r1, r2, r3, wc, fp)

    got = swap(mine, sent, "seq", 1)
    everyone = lax.all_to_all(piece, EVERY, 0, 0)
    step = 2
    while step < seq_count:
        mine, sent = add(mine, got)
        got = swap(mine, sent, "seq", step)
        step *= 2

    derivative, loss = call(
        tail_kernel,
        [shape((own_caps, E), f32), shape((1, own_caps), f32)],
        [VMEM, VMEM, VMEM, SMEM],
        cost=(4 * E * token_ids.shape[0] ** 2, 2 * piece.size, 0),
    )(everyone, mine, got, contrast_divisor)
    return derivative, loss.reshape(own_caps)


def solution(mesh):
    placed = (
        P("seq", None),
        P(),
        P(None, None, "head"),
        P("head", None),
        P(),
        P(EVERY, None),
        P(),
        P(EVERY, None),
        P(),
    )
    return jax.shard_map(
        local,
        mesh=mesh,
        in_specs=placed,
        out_specs=(P(EVERY, None), P(EVERY)),
        check_vma=False,
    )
```

time: 49.6 us -> 49.2 us (level)
  matrix products: 9.46 us -> 0 us
  Pallas kernels: 0 us -> 7.51 us
  other arithmetic: 7.03 us -> 0.15 us
  starting transfers between devices: 18.7 us -> 23 us
  local copies, waits for them, and re-layouts: 1.82 us -> 5.2 us
  waiting for transfers between devices: 10.5 us -> 11.6 us
    ppermute x2 -> x8, waiting for transfers between devices: 0.01 us -> 11.6 us  [the longest x5 11.6 us: swap(): return lax.ppermute(sent, axis, [(i, i ^ step) for i in range(count)])]
    all_to_all x2 -> x1, waiting for transfers between devices: 10.5 us -> 0.01 us  [local(): everyone = lax.all_to_all(piece, EVERY, 0, 0)]
    dot_general x12 -> x0, matrix products: 9.46 us -> none  [the longest x1 1.72 us: local(): jnp.dot(normed, w_qkv[2], preferred_element_type=jnp.float32)]
    ppermute x2 -> x8, starting transfers between devices: 6.83 us -> 15.6 us  [the longest x5 13.3 us: swap(): return lax.ppermute(sent, axis, [(i, i ^ step) for i in range(count)])]
    pallas_call x0 -> x5, Pallas kernels: none -> 7.51 us  [the longest x1 2.67 us: local(): call(attend_kernel, shape((devices, 4 * blocks, E // 2), PIECE), [VMEM] *...]
    unnamed x16 -> x24, local copies, waits for them, and re-layouts: 0.27 us -> 5.12 us
    all_to_all x2 -> x1, starting transfers between devices: 11.9 us -> 7.42 us  [local(): everyone = lax.all_to_all(piece, EVERY, 0, 0)]
    reduce_sum x9 -> x0, other arithmetic: 4 us -> none  [the longest x1 1.31 us: local(): jnp.mean(as32 * as32, axis=-1, keepdims=True) + 1e-05]
  transfers between devices with their start and end apart: 4 -> 9, of which waited for: 2 -> 4; matrix products, arithmetic and copies ran while one was open for 21% -> 0% of each run, Pallas kernels for 0% -> 7%
where the time goes in v2:
time: 49.2 us; the launch traced here: 48.9 us
  starting transfers between devices  23 us (47%)
  waiting for transfers between devices  11.6 us (24%)
  Pallas kernels  7.51 us (15%)
  local copies, waits for them, and re-layouts  5.2 us (11%)
  between operations  1.41 us (3%)
    ppermute x5, starting transfers between devices, swap(): return lax.ppermute(sent, axis, [(i, i ^ step) for i in range(count)])  13.3 us
    ppermute x5, waiting for transfers between devices, swap(): return lax.ppermute(sent, axis, [(i, i ^ step) for i in range(count)])  11.6 us
    all_to_all x1, starting transfers between devices, local(): everyone = lax.all_to_all(piece, EVERY, 0, 0)  7.42 us
    unnamed x24, local copies, waits for them, and re-layouts  5.12 us
    pallas_call x1, Pallas kernels, local(): call(attend_kernel, shape((devices, 4 * blocks, E // 2), PIECE), [VMEM] *...  2.67 us
    pallas_call x1, Pallas kernels, local(): call(qkv_kernel, [shape((n * rows, half), bf16) for n in (3, 3, 2, 2)], [...  1.55 us
    pallas_call x1, Pallas kernels, local(): call(tail_kernel, [shape((own_caps, E), f32), shape((1, own_caps), f32)],...  1.48 us
    pallas_call x1, Pallas kernels, local(): call(text_kernel, [shape((tall, LANES), f32), shape((tall, LANES), bf16)]...  1.28 us
  transfers between devices with their start and end apart: 9, of which 4 were waited for; matrix products, arithmetic and copies ran while one was open for 0% of the time, Pallas kernels for 7%

profile of v2, /device:TPU:0, one launch (start us, length us, event | category | flops | bytes accessed | tf_op | source)
XLA Modules:
  0.0 48.9 jit_solution(10183129639280442711)
XLA Ops:
  0.6 0.0 copy-start.7
  0.6 0.0 copy-start
  0.7 1.0 %copy-done = bf16[256,1024]{1,0:T(8,128)(2,1)S(1)} copy-done((bf16[256,1024]{1,0:T(8,128)(2,1)S(1)}, bf16[256,1024]{1,0:T(8,128)(2,1)}, u32[]{:S(2)}) %copy-start) | copy-done | bytes 524312
  1.7 0.0 copy-start.2
  1.7 1.4 %copy-done.2 = bf16[3,1024,256]{2,1,0:T(8,128)(2,1)S(1)} copy-done((bf16[3,1024,256]{2,1,0:T(8,128)(2,1)S(1)}, bf16[3,1024,256]{2,1,0:T(8,128)(2,1)}, u32[]{:S(2)}) %copy-start.2) | copy-done | bytes 1572888
  3.1 0.0 copy-start.6
  3.1 0.7 %copy-done.6 = f32[1024]{0:T(1024)S(1)} copy-done((f32[1024]{0:T(1024)S(1)}, f32[1024]{0:T(1024)}, u32[]{:S(2)}) %copy-start.6) | copy-done | bytes 4120
  3.8 0.0 copy-start.11
  3.8 0.0 copy-start.3
  3.8 1.6 %shard_map.104 = (bf16[768,128]{1,0:T(8,128)(2,1)S(1)}, bf16[768,128]{1,0:T(8,128)(2,1)S(1)}, bf16[512,128]{1,0:T(8,128)(2,1)S(1)}, bf16[512,128]{1,0:T(8,128)(2,1)S(1)}) custom-call(bf16[256,1024]{1,0:T(8,128)(2,1)S(1)} %copy-done, f32[1,1024]{1,0:T(1,128)S(1)} %bitcast.2, bf16[3,1024,256]{2,1,0:T(8,128)(2,1)S(1)} %copy-done.2), custom_call_target="tpu_custom_call" | custom-call | flops 402653184 | bytes 1572864 | tf_op jit(solution)/shard_map/pallas_call | solution.py:253
  5.3 0.0 copy-start.8
  5.4 0.7 %copy-done.8 = bf16[768,128]{1,0:T(8,128)(2,1)} copy-done((bf16[768,128]{1,0:T(8,128)(2,1)}, bf16[768,128]{1,0:T(8,128)(2,1)S(1)}, u32[]{:S(2)}) %copy-start.8) | copy-done | bytes 196632
  6.0 0.0 copy-start.9
  6.0 0.6 %copy-done.9 = bf16[512,128]{1,0:T(8,128)(2,1)} copy-done((bf16[512,128]{1,0:T(8,128)(2,1)}, bf16[512,128]{1,0:T(8,128)(2,1)S(1)}, u32[]{:S(2)}) %copy-start.9) | copy-done | bytes 131096
  6.7 0.0 copy-start.10
  6.7 0.6 %copy-done.10 = bf16[512,128]{1,0:T(8,128)(2,1)} copy-done((bf16[512,128]{1,0:T(8,128)(2,1)}, bf16[512,128]{1,0:T(8,128)(2,1)S(1)}, u32[]{:S(2)}) %copy-start.10) | copy-done | bytes 131096
  7.3 0.0 copy-start.1
  7.3 0.0 copy-start.4
  7.3 0.0 copy-start.5
  7.3 0.0 copy-done.11
  7.3 0.1 copy.11.ids_ref
  7.4 0.0 copy-done.7
  7.4 0.0 copy-done.3
  7.4 1.3 %shard_map.107 = (f32[320,128]{1,0:T(8,128)S(1)}, bf16[320,128]{1,0:T(8,128)(2,1)S(1)}) custom-call(s32[64,16]{1,0:T(8,128)S(1)} %copy.11.ids_ref, bf16[1024,512]{1,0:T(8,128)(2,1)S(1)} %copy-done.3, s32[2,2]{1,0:T(2,128)S(1)} %copy-done.7), custom_call_target="tpu_custom_call" | custom-call | flops 67108864 | bytes 1048576 | tf_op jit(solution)/shard_map/pallas_call | solution.py:280
  8.7 0.5 %collective-permute-start.3 = (bf16[320,128]{1,0:T(8,128)(2,1)S(1)}, bf16[320,128]{1,0:T(8,128)(2,1)S(1)}, u32[]{:S(2)}, u32[]{:S(2)}) collective-permute-start(bf16[320,128]{1,0:T(8,128)(2,1)S(1)} %get-tuple-element.21), channel_id=1, source_target_pairs={{0,1},{1,0},{2,3},{3,2},{4,5},{5,4},{6,7},{7,6},{8,9},{9,8},{10,11... | collective-permute-start | bytes 245768 | tf_op jit(solution)/shard_map/ppermute | solution.py:289
  9.2 0.9 %collective-permute-done.3 = bf16[320,128]{1,0:T(8,128)(2,1)S(1)} collective-permute-done((bf16[320,128]{1,0:T(8,128)(2,1)S(1)}, bf16[320,128]{1,0:T(8,128)(2,1)S(1)}, u32[]{:S(2)}, u32[]{:S(2)}) %collective-permute-start.3) | collective-permute-done | bytes 81952 | tf_op jit(solution)/shard_map/ppermute | solution.py:289
  10.2 2.9 %collective-permute-start.4 = (bf16[320,128]{1,0:T(8,128)(2,1)S(1)}, bf16[320,128]{1,0:T(8,128)(2,1)S(1)}, u32[]{:S(2)}, u32[]{:S(2)}) collective-permute-start(bf16[320,128]{1,0:T(8,128)(2,1)S(1)} %fusion), channel_id=1, source_target_pairs={{0,2},{1,3},{2,0},{3,1},{4,6},{5,7},{6,4},{7,5},{8,10},{9,11},{10,... | collective-permute-start | bytes 245768 | tf_op jit(solution)/shard_map/ppermute | solution.py:289
  13.1 2.8 %collective-permute-done.4 = bf16[320,128]{1,0:T(8,128)(2,1)S(1)} collective-permute-done((bf16[320,128]{1,0:T(8,128)(2,1)S(1)}, bf16[320,128]{1,0:T(8,128)(2,1)S(1)}, u32[]{:S(2)}, u32[]{:S(2)}) %collective-permute-start.4) | collective-permute-done | bytes 81952 | tf_op jit(solution)/shard_map/ppermute | solution.py:289
  15.9 1.8 %collective-permute-start.5 = (bf16[320,128]{1,0:T(8,128)(2,1)S(1)}, bf16[320,128]{1,0:T(8,128)(2,1)S(1)}, u32[]{:S(2)}, u32[]{:S(2)}) collective-permute-start(bf16[320,128]{1,0:T(8,128)(2,1)S(1)} %fusion.2), channel_id=1, source_target_pairs={{0,4},{4,0},{8,12},{12,8},{16,20},{20,16},{24,28},{28,24},{1,5},{5... | collective-permute-start | bytes 245768 | tf_op jit(solution)/shard_map/ppermute | solution.py:289
  17.7 0.3 collective-permute-start
  18.0 1.3 %collective-permute-start.1 = (bf16[512,128]{1,0:T(8,128)(2,1)}, bf16[512,128]{1,0:T(8,128)(2,1)S(1)}, u32[]{:S(2)}, u32[]{:S(2)}) collective-permute-start(bf16[512,128]{1,0:T(8,128)(2,1)} %copy-done.10), channel_id=1, source_target_pairs={{4,12},{12,20},{20,28},{8,0},{16,8},{24,16},{5,13},{13,21},{21,29}... | collective-permute-start | bytes 393224 | tf_op jit(solution)/shard_map/ppermute | solution.py:272
  19.3 0.7 %collective-permute-start.2 = (bf16[512,128]{1,0:T(8,128)(2,1)}, bf16[512,128]{1,0:T(8,128)(2,1)S(1)}, u32[]{:S(2)}, u32[]{:S(2)}) collective-permute-start(bf16[512,128]{1,0:T(8,128)(2,1)} %copy-done.9), channel_id=1, source_target_pairs={{4,8},{12,16},{20,24},{8,4},{16,12},{24,20},{5,9},{13,17},{21,25},... | collective-permute-start | bytes 393224 | tf_op jit(solution)/shard_map/ppermute | solution.py:267
  20.0 1.3 %collective-permute-done.5 = bf16[320,128]{1,0:T(8,128)(2,1)S(1)} collective-permute-done((bf16[320,128]{1,0:T(8,128)(2,1)S(1)}, bf16[320,128]{1,0:T(8,128)(2,1)S(1)}, u32[]{:S(2)}, u32[]{:S(2)}) %collective-permute-start.5) | collective-permute-done | bytes 81952 | tf_op jit(solution)/shard_map/ppermute | solution.py:289
  21.3 5.4 %collective-permute-start.6 = (bf16[320,128]{1,0:T(8,128)(2,1)S(1)}, bf16[320,128]{1,0:T(8,128)(2,1)S(1)}, u32[]{:S(2)}, u32[]{:S(2)}) collective-permute-start(bf16[320,128]{1,0:T(8,128)(2,1)S(1)} %fusion.1), channel_id=1, source_target_pairs={{0,8},{4,12},{8,0},{12,4},{16,24},{20,28},{24,16},{28,20},{1,9},{5... | collective-permute-start | bytes 245768 | tf_op jit(solution)/shard_map/ppermute | solution.py:289
  26.7 0.0 copy-done.1
  26.7 0.0 copy-done.4
  26.7 0.0 copy-done.5
  26.7 0.5 %shard_map.105 = (f32[128,512]{1,0:T(8,128)S(1)}, f32[2,512]{1,0:T(2,128)S(1)}) custom-call(bf16[256,1024]{1,0:T(8,128)(2,1)S(1)} %copy-done.1, bf16[256,1024]{1,0:T(8,128)(2,1)S(1)} %copy-done.5, bf16[1024,512]{1,0:T(8,128)(2,1)S(1)} %copy-done.4), custom_call_target="tpu_custom_call" | custom-call | flops 134217728 | bytes 2097152 | tf_op jit(solution)/shard_map/pallas_call | solution.py:300
  27.2 0.0 collective-permute-done.1.r2_ref
  27.2 0.0 collective-permute-done.2.r3_ref
  27.2 0.0 collective-permute-done.r1_ref
  27.2 2.7 %shard_map.106 = bf16[32,8,256]{2,1,0:T(8,128)(2,1)} custom-call(bf16[768,128]{1,0:T(8,128)(2,1)S(1)} %get-tuple-element.13.own_ref, bf16[768,128]{1,0:T(8,128)(2,1)S(1)} %collective-permute-done.r1_ref, bf16[512,128]{1,0:T(8,128)(2,1)S(1)} %collective-permute-done.1.r2_ref, bf16[512,128]{1,0:T(8,128)(2,1)S(1)} %collective-permute-done.2.r3_ref, ...), custom_call_target="tpu_custom_call" | custom-call | flops 402653184 | bytes 655360 | tf_op jit(solution)/shard_map/pallas_call | solution.py:307
  29.9 7.4 %all-to-all-start = ((bf16[32,8,256]{2,1,0:T(8,128)(2,1)}), bf16[32,8,256]{2,1,0:T(8,128)(2,1)S(1)}, u32[]{:S(2)}, u32[]{:S(2)}) async-start(bf16[32,8,256]{2,1,0:T(8,128)(2,1)} %shard_map.106), calls=%async_computation | async-start | bytes 262144 | tf_op jit(solution)/shard_map/all_to_all | solution.py:315
  37.3 0.0 collective-permute-done.6
  37.4 0.1 fusion.3
  37.4 2.7 %collective-permute-start.7 = (bf16[320,128]{1,0:T(8,128)(2,1)S(1)}, bf16[320,128]{1,0:T(8,128)(2,1)S(1)}, u32[]{:S(2)}, u32[]{:S(2)}) collective-permute-start(bf16[320,128]{1,0:T(8,128)(2,1)S(1)} %get-tuple-element.24), channel_id=1, source_target_pairs={{0,16},{4,20},{8,24},{12,28},{16,0},{20,4},{24,8},{28,12},{1,17},{... | collective-permute-start | bytes 245768 | tf_op jit(solution)/shard_map/ppermute | solution.py:289
  40.8 6.6 %collective-permute-done.7.last_ref = bf16[320,128]{1,0:T(8,128)(2,1)S(1)} collective-permute-done((bf16[320,128]{1,0:T(8,128)(2,1)S(1)}, bf16[320,128]{1,0:T(8,128)(2,1)S(1)}, u32[]{:S(2)}, u32[]{:S(2)}) %collective-permute-start.7) | collective-permute-done | bytes 81952 | tf_op jit(solution)/shard_map/ppermute | solution.py:289
  47.4 0.0 all-to-all-done.everyone_ref
  47.4 1.5 %shard_map.108 = (f32[2,512]{1,0:T(2,128)}, f32[1,2]{1,0:T(1,128)}) custom-call(bf16[32,8,256]{2,1,0:T(8,128)(2,1)S(1)} %all-to-all-done.everyone_ref, f32[320,128]{1,0:T(8,128)S(1)} %get-tuple-element.25.mine_ref, bf16[320,128]{1,0:T(8,128)(2,1)S(1)} %collective-permute-done.7.last_ref, f32[1]{0:T(128)S(6)} %copy.12.divisor_ref), custom_call_target="tpu_custom_call" | custom-call | flops 8388608 | bytes 131072 | tf_op jit(solution)/shard_map/pallas_call | solution.py:322
  (3 shorter events, 0.1 us)
Async XLA Ops:
  0.6 6.8 %copy-start.7 = (s32[2,2]{1,0:T(2,128)S(1)}, s32[2,2]{1,0:T(2,128)}, u32[]{:S(2)}) copy-start(s32[2,2]{1,0:T(2,128)} %bounds_ref.1) | copy-start | bytes 52
  0.6 1.0 %copy-start = (bf16[256,1024]{1,0:T(8,128)(2,1)S(1)}, bf16[256,1024]{1,0:T(8,128)(2,1)}, u32[]{:S(2)}) copy-start(bf16[256,1024]{1,0:T(8,128)(2,1)} %frames_ref.1) | copy-start | bytes 1572868
  1.7 1.4 %copy-start.2 = (bf16[3,1024,256]{2,1,0:T(8,128)(2,1)S(1)}, bf16[3,1024,256]{2,1,0:T(8,128)(2,1)}, u32[]{:S(2)}) copy-start(bf16[3,1024,256]{2,1,0:T(8,128)(2,1)} %w_hbm.1) | copy-start | bytes 4718596
  3.1 0.7 %copy-start.6 = (f32[1024]{0:T(1024)S(1)}, f32[1024]{0:T(1024)}, u32[]{:S(2)}) copy-start(f32[1024]{0:T(1024)} %param.10) | copy-start | bytes 12292
  3.8 3.5 %copy-start.11 = (s32[64,16]{0,1:T(8,128)S(1)}, s32[64,16]{0,1:T(8,128)}, u32[]{:S(2)}) copy-start(s32[64,16]{0,1:T(8,128)} %param.15) | copy-start | bytes 12292
  3.8 3.6 %copy-start.3 = (bf16[1024,512]{1,0:T(8,128)(2,1)S(1)}, bf16[1024,512]{1,0:T(8,128)(2,1)}, u32[]{:S(2)}) copy-start(bf16[1024,512]{1,0:T(8,128)(2,1)} %table_ref.1) | copy-start | bytes 3145732
  5.3 0.7 %copy-start.8 = (bf16[768,128]{1,0:T(8,128)(2,1)}, bf16[768,128]{1,0:T(8,128)(2,1)S(1)}, u32[]{:S(2)}) copy-start(bf16[768,128]{1,0:T(8,128)(2,1)S(1)} %get-tuple-element.14) | copy-start | bytes 589828
  6.0 0.6 %copy-start.9 = (bf16[512,128]{1,0:T(8,128)(2,1)}, bf16[512,128]{1,0:T(8,128)(2,1)S(1)}, u32[]{:S(2)}) copy-start(bf16[512,128]{1,0:T(8,128)(2,1)S(1)} %get-tuple-element.16) | copy-start | bytes 393220
  6.7 0.6 %copy-start.10 = (bf16[512,128]{1,0:T(8,128)(2,1)}, bf16[512,128]{1,0:T(8,128)(2,1)S(1)}, u32[]{:S(2)}) copy-start(bf16[512,128]{1,0:T(8,128)(2,1)S(1)} %get-tuple-element.15) | copy-start | bytes 393220
  7.3 19.4 %copy-start.1 = (bf16[256,1024]{1,0:T(8,128)(2,1)S(1)}, bf16[256,1024]{1,0:T(8,128)(2,1)}, u32[]{:S(2)}) copy-start(bf16[256,1024]{1,0:T(8,128)(2,1)} %frames_ref.1) | copy-start | bytes 1572868
  7.3 19.4 %copy-start.4 = (bf16[1024,512]{1,0:T(8,128)(2,1)S(1)}, bf16[1024,512]{1,0:T(8,128)(2,1)}, u32[]{:S(2)}) copy-start(bf16[1024,512]{1,0:T(8,128)(2,1)} %w_proj_ref.1) | copy-start | bytes 3145732
  7.3 19.4 %copy-start.5 = (bf16[256,1024]{1,0:T(8,128)(2,1)S(1)}, bf16[256,1024]{1,0:T(8,128)(2,1)}, u32[]{:S(2)}) copy-start(bf16[256,1024]{1,0:T(8,128)(2,1)} %w_out_ref.1) | copy-start | bytes 1572868
  8.7 1.4 %collective-permute-start.3 = (bf16[320,128]{1,0:T(8,128)(2,1)S(1)}, bf16[320,128]{1,0:T(8,128)(2,1)S(1)}, u32[]{:S(2)}, u32[]{:S(2)}) collective-permute-start(bf16[320,128]{1,0:T(8,128)(2,1)S(1)} %get-tuple-element.21), channel_id=1, source_target_pairs={{0,1},{1,0},{2,3},{3,2},{4,5},{5,4},{6,7},{7,6},{8,9},{9,8},{10,11... | collective-permute-start | bytes 245768 | tf_op jit(solution)/shard_map/ppermute | solution.py:289
  10.2 5.7 %collective-permute-start.4 = (bf16[320,128]{1,0:T(8,128)(2,1)S(1)}, bf16[320,128]{1,0:T(8,128)(2,1)S(1)}, u32[]{:S(2)}, u32[]{:S(2)}) collective-permute-start(bf16[320,128]{1,0:T(8,128)(2,1)S(1)} %fusion), channel_id=1, source_target_pairs={{0,2},{1,3},{2,0},{3,1},{4,6},{5,7},{6,4},{7,5},{8,10},{9,11},{10,... | collective-permute-start | bytes 245768 | tf_op jit(solution)/shard_map/ppermute | solution.py:289
  15.9 5.4 %collective-permute-start.5 = (bf16[320,128]{1,0:T(8,128)(2,1)S(1)}, bf16[320,128]{1,0:T(8,128)(2,1)S(1)}, u32[]{:S(2)}, u32[]{:S(2)}) collective-permute-start(bf16[320,128]{1,0:T(8,128)(2,1)S(1)} %fusion.2), channel_id=1, source_target_pairs={{0,4},{4,0},{8,12},{12,8},{16,20},{20,16},{24,28},{28,24},{1,5},{5... | collective-permute-start | bytes 245768 | tf_op jit(solution)/shard_map/ppermute | solution.py:289
  17.7 9.6 %collective-permute-start = (bf16[768,128]{1,0:T(8,128)(2,1)}, bf16[768,128]{1,0:T(8,128)(2,1)S(1)}, u32[]{:S(2)}, u32[]{:S(2)}) collective-permute-start(bf16[768,128]{1,0:T(8,128)(2,1)} %copy-done.8), channel_id=1, source_target_pairs={{0,4},{4,0},{8,12},{12,8},{16,20},{20,16},{24,28},{28,24},{1,5},{5... | collective-permute-start | bytes 589832 | tf_op jit(solution)/shard_map/ppermute | solution.py:266
  18.0 9.2 %collective-permute-start.1 = (bf16[512,128]{1,0:T(8,128)(2,1)}, bf16[512,128]{1,0:T(8,128)(2,1)S(1)}, u32[]{:S(2)}, u32[]{:S(2)}) collective-permute-start(bf16[512,128]{1,0:T(8,128)(2,1)} %copy-done.10), channel_id=1, source_target_pairs={{4,12},{12,20},{20,28},{8,0},{16,8},{24,16},{5,13},{13,21},{21,29}... | collective-permute-start | bytes 393224 | tf_op jit(solution)/shard_map/ppermute | solution.py:272
  19.3 8.0 %collective-permute-start.2 = (bf16[512,128]{1,0:T(8,128)(2,1)}, bf16[512,128]{1,0:T(8,128)(2,1)S(1)}, u32[]{:S(2)}, u32[]{:S(2)}) collective-permute-start(bf16[512,128]{1,0:T(8,128)(2,1)} %copy-done.9), channel_id=1, source_target_pairs={{4,8},{12,16},{20,24},{8,4},{16,12},{24,20},{5,9},{13,17},{21,25},... | collective-permute-start | bytes 393224 | tf_op jit(solution)/shard_map/ppermute | solution.py:267
  21.3 16.0 %collective-permute-start.6 = (bf16[320,128]{1,0:T(8,128)(2,1)S(1)}, bf16[320,128]{1,0:T(8,128)(2,1)S(1)}, u32[]{:S(2)}, u32[]{:S(2)}) collective-permute-start(bf16[320,128]{1,0:T(8,128)(2,1)S(1)} %fusion.1), channel_id=1, source_target_pairs={{0,8},{4,12},{8,0},{12,4},{16,24},{20,28},{24,16},{28,20},{1,9},{5... | collective-permute-start | bytes 245768 | tf_op jit(solution)/shard_map/ppermute | solution.py:289
  29.9 17.5 %all-to-all-start = ((bf16[32,8,256]{2,1,0:T(8,128)(2,1)}), bf16[32,8,256]{2,1,0:T(8,128)(2,1)S(1)}, u32[]{:S(2)}, u32[]{:S(2)}) async-start(bf16[32,8,256]{2,1,0:T(8,128)(2,1)} %shard_map.106), calls=%async_computation | async-start | bytes 262144 | tf_op jit(solution)/shard_map/all_to_all | solution.py:315
  37.4 10.0 %collective-permute-start.7 = (bf16[320,128]{1,0:T(8,128)(2,1)S(1)}, bf16[320,128]{1,0:T(8,128)(2,1)S(1)}, u32[]{:S(2)}, u32[]{:S(2)}) collective-permute-start(bf16[320,128]{1,0:T(8,128)(2,1)S(1)} %get-tuple-element.24), channel_id=1, source_target_pairs={{0,16},{4,20},{8,24},{12,28},{16,0},{20,4},{24,8},{28,12},{1,17},{... | collective-permute-start | bytes 245768 | tf_op jit(solution)/shard_map/ppermute | solution.py:289

commit v3 on v2

--- a/solution.py
+++ b/solution.py
@@ -14,14 +14,15 @@
 LANES = 128
 SUB = 8
 NEVER = -1e30
+BOUND_ROWS = 16
 PIECE = jnp.bfloat16
 VMEM = pl.BlockSpec(memory_space=pltpu.VMEM)
 SMEM = pl.BlockSpec(memory_space=pltpu.SMEM)
-ANY = pl.BlockSpec(memory_space=pl.ANY)
+HBM = pl.BlockSpec(memory_space=pltpu.HBM)
 HIGHEST = lax.Precision.HIGHEST
 
 
-def call(body, outs, ins, scratch=(), cost=(0, 0, 0), mib=40):
+def call(body, outs, ins, scratch=(), cost=(0, 0, 0), mib=16):
     return pl.pallas_call(
         body,
         out_shape=outs,
@@ -41,17 +42,47 @@
     )
 
 
-def qkv_kernel(
-    frames_hbm, gain_ref, w_hbm, own_ref, p1_ref, p2_ref, p3_ref, frames, w, normed, sems
+def first_kernel(
+    frames_hbm,
+    gain_ref,
+    w_hbm,
+    ids_ref,
+    table_hbm,
+    bounds_ref,
+    own_ref,
+    p1_ref,
+    p2_ref,
+    p3_ref,
+    t32_ref,
+    t16_ref,
+    frames,
+    w,
+    table,
+    normed,
+    sems,
 ):
     rows = frames.shape[0]
     half = own_ref.shape[1]
-    copies = [pltpu.make_async_copy(frames_hbm, frames, sems.at[0])] + [
-        pltpu.make_async_copy(w_hbm.at[k], w.at[k], sems.at[1 + k]) for k in range(3)
+    copies = [
+        pltpu.make_async_copy(frames_hbm, frames, sems.at[0]),
+        *[pltpu.make_async_copy(w_hbm.at[k], w.at[k], sems.at[1 + k]) for k in range(3)],
+        pltpu.make_async_copy(table_hbm, table, sems.at[4]),
     ]
-    for k in (0, 2, 3, 1):
+    for k in (0, 2, 3, 1, 4):
         copies[k].start()
     odd = lax.axis_index("seq") % 2 == 1
+
+    caps, tokens = ids_ref.shape
+    vocab = table.shape[0]
+    own_caps = bounds_ref.shape[0]
+    slot = lax.axis_index("seq") * lax.axis_size("head") + lax.axis_index("head")
+    ids = ids_ref[...] - slot * vocab
+    words = lax.broadcasted_iota(jnp.int32, (caps, vocab), 1)
+    counts = jnp.zeros((caps, vocab), jnp.float32)
+    for t in range(tokens):
+        counts = counts + jnp.where(ids[:, t : t + 1] == words, 1.0, 0.0)
+    counts = counts.astype(jnp.bfloat16)
+
     copies[0].wait()
     step = min(64, rows)
     for r in range(0, rows, step):
@@ -71,30 +102,26 @@
             p2_ref[(k - 1) * rows : k * rows] = mine
             p3_ref[(k - 1) * rows : k * rows] = other
 
-
-def text_kernel(ids_ref, table_ref, bounds_ref, t32_ref, t16_ref):
-    caps, tokens = ids_ref.shape
-    vocab = table_ref.shape[0]
-    own_caps = bounds_ref.shape[0]
-    slot = lax.axis_index("seq") * lax.axis_size("head") + lax.axis_index("head")
-    ids = ids_ref[...] - slot * vocab
-    words = lax.broadcasted_iota(jnp.int32, (caps, vocab), 1)
-    counts = jnp.zeros((caps, vocab), jnp.float32)
-    for t in range(tokens):
-        counts = counts + jnp.where(ids[:, t : t + 1] == words, 1.0, 0.0)
-    part = jnp.dot(counts.astype(jnp.bfloat16), table_ref[...], preferred_element_type=jnp.float32)
-    chunks = [part[:, c : c + LANES] for c in range(0, E, LANES)]
-    row = lax.broadcasted_iota(jnp.int32, (caps, LANES), 0)
-    lane = lax.broadcasted_iota(jnp.int32, (caps, LANES), 1)
-    bounds = jnp.zeros((caps, LANES), jnp.float32)
+    copies[4].wait()
+    part = jnp.dot(counts, table[...], preferred_element_type=jnp.float32)
+    row = lax.broadcasted_iota(jnp.int32, (BOUND_ROWS, LANES), 0)
+    place = row * LANES + lax.broadcasted_iota(jnp.int32, (BOUND_ROWS, LANES), 1)
+    bounds = jnp.zeros((BOUND_ROWS, LANES), jnp.float32)
     for c in range(own_caps):
         for side in range(2):
             block = (bounds_ref[c, side] // BLK).astype(jnp.float32)
-            bounds = jnp.where((row == slot * own_caps + c) & (lane == side), block, bounds)
-    chunks.append(bounds)
-    for c, chunk in enumerate(chunks):
-        t32_ref[c * caps : (c + 1) * caps] = chunk
-        t16_ref[c * caps : (c + 1) * caps] = chunk.astype(jnp.bfloat16)
+            bounds = jnp.where(place == side * caps + slot * own_caps + c, block, bounds)
+    late = lax.axis_index("head") % 2 == 1
+    few = caps // 2
+    for c in range(E // LANES):
+        early_half = part[:few, c * LANES : (c + 1) * LANES]
+        late_half = part[few:, c * LANES : (c + 1) * LANES]
+        t32_ref[c * few : (c + 1) * few] = jnp.where(late, late_half, early_half)
+        t16_ref[c * few : (c + 1) * few] = jnp.where(late, early_half, late_half).astype(
+            jnp.bfloat16
+        )
+    t32_ref[E // LANES * few :] = bounds
+    t16_ref[E // LANES * few :] = bounds.astype(jnp.bfloat16)
 
 
 def weights_kernel(frames_ref, w_out_ref, w_proj_ref, wc_ref, fp_ref):
@@ -173,19 +200,33 @@
 def tail_kernel(everyone_ref, mine_ref, last_ref, divisor_ref, derivative_ref, loss_ref):
     own_caps = derivative_ref.shape[0]
     devices, width, half = everyone_ref.shape
-    caps = mine_ref.shape[0] // (E // LANES + 1)
+    few = (mine_ref.shape[0] - BOUND_ROWS) // (E // LANES)
+    caps = 2 * few
     group = 2 * lax.axis_size("head")
     pairs = devices // group
     blocks = width // 2
-    slot = lax.axis_index("seq") * lax.axis_size("head") + lax.axis_index("head")
+    head = lax.axis_index("head")
+    slot = lax.axis_index("seq") * lax.axis_size("head") + head
     divisor = divisor_ref[0]
 
-    total = mine_ref[...] + last_ref[...].astype(jnp.float32)
-    raw = jnp.concatenate(
-        [total[c * caps : (c + 1) * caps] for c in range(E // LANES)], axis=1
-    )
-    bounds = total[E // LANES * caps :]
-    lower, upper = bounds[:, 0:1], bounds[:, 1:2]
+    def rows_of(ref):
+        chunks = [ref[c * few : (c + 1) * few] for c in range(E // LANES)]
+        return jnp.concatenate(chunks, axis=1).astype(jnp.float32)
+
+    mine, other = rows_of(mine_ref), rows_of(last_ref)
+    late = head % 2 == 1
+    raw = jnp.concatenate([jnp.where(late, other, mine), jnp.where(late, mine, other)], axis=0)
+
+    def column(side):
+        found = jnp.zeros((caps, LANES), jnp.float32)
+        at = lax.broadcasted_iota(jnp.int32, (caps, LANES), 0) + side * caps
+        lane = lax.broadcasted_iota(jnp.int32, (caps, LANES), 1)
+        for r in range(-(-2 * caps // LANES)):
+            line = mine_ref[E // LANES * few + r : E // LANES * few + r + 1]
+            found = found + jnp.where(at == lane + r * LANES, line, 0.0)
+        return jnp.sum(found, axis=1, keepdims=True)
+
+    lower, upper = column(0), column(1)
 
     def unit(parts):
         mean = sum(jnp.sum(p * p, axis=-1, keepdims=True) for p in parts) * (1.0 / E)
@@ -250,18 +291,22 @@
     shape = jax.ShapeDtypeStruct
     bf16, f32 = jnp.bfloat16, jnp.float32
 
-    own, p1, p2, p3 = call(
-        qkv_kernel,
-        [shape((n * rows, half), bf16) for n in (3, 3, 2, 2)],
-        [ANY, VMEM, ANY],
+    tall = E // LANES * token_ids.shape[0] // 2 + BOUND_ROWS
+    own, p1, p2, p3, mine, sent = call(
+        first_kernel,
+        [shape((n * rows, half), bf16) for n in (3, 3, 2, 2)]
+        + [shape((tall, LANES), f32), shape((tall, LANES), bf16)],
+        [HBM, VMEM, HBM, VMEM, HBM, SMEM],
         [
             pltpu.VMEM(frames.shape, bf16),
             pltpu.VMEM(w_qkv.shape, bf16),
+            pltpu.VMEM(text_table.shape, bf16),
             pltpu.VMEM(frames.shape, bf16),
-            pltpu.SemaphoreType.DMA((4,)),
+            pltpu.SemaphoreType.DMA((5,)),
         ],
         (6 * rows * width * cols, 2 * w_qkv.size, 0),
-    )(frames, norm_gain[None], w_qkv)
+        60,
+    )(frames, norm_gain[None], w_qkv, token_ids, text_table, span_bounds)
     ends = seq_count - 1
     r1 = lax.ppermute(p1, "seq", [(s, s ^ 1) for s in range(seq_count)])
     r3 = lax.ppermute(
@@ -275,27 +320,21 @@
         [(s, s + 2) for s in range(1, ends - 1, 2)] + [(s, s - 2) for s in range(2, seq_count, 2)],
     )
 
-    ids, _ = lax.optimization_barrier((token_ids, own))
-    tall = (E // LANES + 1) * token_ids.shape[0]
-    mine, sent = call(
-        text_kernel,
-        [shape((tall, LANES), f32), shape((tall, LANES), bf16)],
-        [VMEM, VMEM, SMEM],
-        cost=(2 * token_ids.shape[0] * text_table.size, 2 * text_table.size, 0),
-    )(ids, text_table, span_bounds)
-
-    def swap(mine, sent, axis, step):
-        count = lax.axis_size(axis)
-        return lax.ppermute(sent, axis, [(i, i ^ step) for i in range(count)])
-
-    def add(mine, got):
-        mine = mine + got.astype(f32)
+    def swap(sent, seq_step, head_step):
+        to = [
+            (s ^ seq_step) * head_count + (h ^ head_step)
+            for s in range(seq_count)
+            for h in range(head_count)
+        ]
+        return lax.ppermute(sent, EVERY, list(enumerate(to)))
+
+    def add(mine, *got):
+        for g in got:
+            mine = mine + g.astype(f32)
         return mine, mine.astype(bf16)
 
-    step = 1
-    while step < head_count:
-        mine, sent = add(mine, swap(mine, sent, "head", step))
-        step *= 2
+    mine, sent = add(mine, swap(sent, 0, 1))
+    mine, sent = add(mine, swap(sent, 0, 2), swap(sent, 1, 0), swap(sent, 1, 2))
 
     wc, fp = call(
         weights_kernel,
@@ -311,13 +350,16 @@
         cost=(24 * rows * rows * cols, 10 * rows * cols, 6 * rows * rows * cols // HDIM),
     )(own, r1, r2, r3, wc, fp)
 
-    got = swap(mine, sent, "seq", 1)
-    everyone = lax.all_to_all(piece, EVERY, 0, 0)
     step = 2
     while step < seq_count:
-        mine, sent = add(mine, got)
-        got = swap(mine, sent, "seq", step)
-        step *= 2
+        if 4 * step <= seq_count:
+            mine, sent = add(mine, *[swap(sent, k * step, 0) for k in (1, 2, 3)])
+            step *= 4
+        else:
+            mine, sent = add(mine, swap(sent, step, 0))
+            step *= 2
+    everyone = lax.all_to_all(piece, EVERY, 0, 0)
+    got = swap(sent, 0, 1)
 
     derivative, loss = call(
         tail_kernel,

time: 49.2 us -> 44.8 us (0.911)
  local copies, waits for them, and re-layouts: 5.2 us -> 1.42 us
  waiting for transfers between devices: 11.6 us -> 8.99 us
  Pallas kernels: 7.51 us -> 9.29 us
  other arithmetic: 0.15 us -> 0.98 us
  starting transfers between devices: 23 us -> 22.4 us
    ppermute x5 -> x8, waiting for transfers between devices: 11.6 us -> 2.12 us  [swap(): return lax.ppermute(sent, EVERY, list(enumerate(to)))]
    all_to_all x1, waiting for transfers between devices: 0.01 us -> 6.86 us  [local(): everyone = lax.all_to_all(piece, EVERY, 0, 0)]
    unnamed x24 -> x13, local copies, waits for them, and re-layouts: 5.12 us -> 1.42 us
    pallas_call x2 -> x1, Pallas kernels: 2.83 us -> 4.61 us  [local(): call(first_kernel, [shape((n * rows, half), bf16) for n in (3, 3, 2, 2)]...]
    ppermute x1, starting transfers between devices: 0.31 us -> 1.92 us  [local(): r1 = lax.ppermute(p1, 'seq', [(s, s ^ 1) for s in range(seq_count)])]
    all_to_all x1, starting transfers between devices: 7.42 us -> 5.86 us  [local(): everyone = lax.all_to_all(piece, EVERY, 0, 0)]
    convert_element_type x4 -> x3, other arithmetic: 0.15 us -> 0.98 us  [add(): return (mine, mine.astype(bf16))]
    ppermute x5 -> x8, starting transfers between devices: 13.3 us -> 12.7 us  [swap(): return lax.ppermute(sent, EVERY, list(enumerate(to)))]
  transfers between devices with their start and end apart: 9 -> 12, of which waited for: 4 -> 4; matrix products, arithmetic and copies ran while one was open for 0% -> 0% of each run, Pallas kernels for 7% -> 7%
where the time goes in v3:
time: 44.8 us; the launch traced here: 44.5 us
  starting transfers between devices  22.4 us (50%)
  Pallas kernels  9.29 us (21%)
  waiting for transfers between devices  8.99 us (20%)
  between operations  1.43 us (3%)
  local copies, waits for them, and re-layouts  1.42 us (3%)
  other arithmetic  0.98 us (2%)
    ppermute x8, starting transfers between devices, swap(): return lax.ppermute(sent, EVERY, list(enumerate(to)))  12.7 us
    all_to_all x1, waiting for transfers between devices, local(): everyone = lax.all_to_all(piece, EVERY, 0, 0)  6.86 us
    all_to_all x1, starting transfers between devices, local(): everyone = lax.all_to_all(piece, EVERY, 0, 0)  5.86 us
    pallas_call x1, Pallas kernels, local(): call(first_kernel, [shape((n * rows, half), bf16) for n in (3, 3, 2, 2)]...  4.61 us
    pallas_call x1, Pallas kernels, local(): call(attend_kernel, shape((devices, 4 * blocks, E // 2), PIECE), [VMEM] *...  2.67 us
    ppermute x8, waiting for transfers between devices, swap(): return lax.ppermute(sent, EVERY, list(enumerate(to)))  2.12 us
    ppermute x1, starting transfers between devices, local(): r1 = lax.ppermute(p1, 'seq', [(s, s ^ 1) for s in range(seq_count)])  1.92 us
    pallas_call x1, Pallas kernels, local(): call(tail_kernel, [shape((own_caps, E), f32), shape((1, own_caps), f32)],...  1.48 us
  transfers between devices with their start and end apart: 12, of which 4 were waited for; matrix products, arithmetic and copies ran while one was open for 0% of the time, Pallas kernels for 7%

profile of v3, /device:TPU:0, one launch (start us, length us, event | category | flops | bytes accessed | tf_op | source)
XLA Modules:
  0.0 44.5 jit_solution(16030116008176184424)
XLA Ops:
  0.6 1.4 %copy.11.ids_ref = s32[64,16]{1,0:T(8,128)} copy(s32[64,16]{0,1:T(8,128)} %param.15) | data formatting | bytes 8192 | tf_op args[6]
  2.0 0.0 copy-start
  2.0 0.0 copy-start.1
  2.0 0.0 copy-start.2
  2.0 4.6 %shard_map.104 = (bf16[768,128]{1,0:T(8,128)(2,1)}, bf16[768,128]{1,0:T(8,128)(2,1)}, bf16[512,128]{1,0:T(8,128)(2,1)}, bf16[512,128]{1,0:T(8,128)(2,1)}, f32[144,128]{1,0:T(8,128)}, /*index=5*/bf16[144,128]{1,0:T(8,128)(2,1)}) custom-call(bf16[256,1024]{1,0:T(8,128)(2,1)} %frames_ref.1, f32[1,1024]{1,0:T(1,128)} %bitcast.2, bf16[3,1024,256]{2,1,0:T(8,128)(2,1)} %w_hbm.1, ...), custom_call_target="tpu_custom_call" | custom-call | flops 402653184 | bytes 1572864 | tf_op jit(solution)/shard_map/pallas_call | solution.py:295
  6.6 0.0 copy-start.5
  6.7 0.0 copy-start.4
  6.7 0.0 copy-start.3
  6.7 0.5 %collective-permute-start.3 = (bf16[144,128]{1,0:T(8,128)(2,1)}, bf16[144,128]{1,0:T(8,128)(2,1)S(1)}, u32[]{:S(2)}, u32[]{:S(2)}) collective-permute-start(bf16[144,128]{1,0:T(8,128)(2,1)} %get-tuple-element.19), channel_id=1, source_target_pairs={{0,1},{1,0},{2,3},{3,2},{4,5},{5,4},{6,7},{7,6},{8,9},{9,8},{10,11... | collective-permute-start | bytes 110600 | tf_op jit(solution)/shard_map/ppermute | solution.py:329
  7.2 1.1 %collective-permute-done.3 = bf16[144,128]{1,0:T(8,128)(2,1)S(1)} collective-permute-done((bf16[144,128]{1,0:T(8,128)(2,1)}, bf16[144,128]{1,0:T(8,128)(2,1)S(1)}, u32[]{:S(2)}, u32[]{:S(2)}) %collective-permute-start.3) | collective-permute-done | bytes 36896 | tf_op jit(solution)/shard_map/ppermute | solution.py:329
  8.3 0.9 %fusion = bf16[144,128]{1,0:T(8,128)(2,1)S(1)} fusion(f32[144,128]{1,0:T(8,128)} %get-tuple-element.18, bf16[144,128]{1,0:T(8,128)(2,1)S(1)} %collective-permute-done.3), kind=kLoop, calls=%fused_computation.3 | loop fusion | flops 55296 | bytes 147456 | tf_op jit(solution)/shard_map/convert_element_type | solution.py:334
  9.2 2.9 %collective-permute-start.4 = (bf16[144,128]{1,0:T(8,128)(2,1)S(1)}, bf16[144,128]{1,0:T(8,128)(2,1)S(1)}, u32[]{:S(2)}, u32[]{:S(2)}) collective-permute-start(bf16[144,128]{1,0:T(8,128)(2,1)S(1)} %fusion), channel_id=1, source_target_pairs={{0,2},{1,3},{2,0},{3,1},{4,6},{5,7},{6,4},{7,5},{8,10},{9,11},{10,... | collective-permute-start | bytes 110600 | tf_op jit(solution)/shard_map/ppermute | solution.py:329
  12.1 1.5 %collective-permute-start.5 = (bf16[144,128]{1,0:T(8,128)(2,1)S(1)}, bf16[144,128]{1,0:T(8,128)(2,1)S(1)}, u32[]{:S(2)}, u32[]{:S(2)}) collective-permute-start(bf16[144,128]{1,0:T(8,128)(2,1)S(1)} %fusion), channel_id=1, source_target_pairs={{0,4},{1,5},{2,6},{3,7},{4,0},{5,1},{6,2},{7,3},{8,12},{9,13},{10,... | collective-permute-start | bytes 110600 | tf_op jit(solution)/shard_map/ppermute | solution.py:329
  13.6 0.1 collective-permute-start.6
  13.6 1.9 %collective-permute-start = (bf16[768,128]{1,0:T(8,128)(2,1)}, bf16[768,128]{1,0:T(8,128)(2,1)S(1)}, u32[]{:S(2)}, u32[]{:S(2)}) collective-permute-start(bf16[768,128]{1,0:T(8,128)(2,1)} %get-tuple-element.13), channel_id=1, source_target_pairs={{0,4},{4,0},{8,12},{12,8},{16,20},{20,16},{24,28},{28,24},{1,5},{5... | collective-permute-start | bytes 589832 | tf_op jit(solution)/shard_map/ppermute | solution.py:311
  15.6 1.3 %collective-permute-start.1 = (bf16[512,128]{1,0:T(8,128)(2,1)}, bf16[512,128]{1,0:T(8,128)(2,1)S(1)}, u32[]{:S(2)}, u32[]{:S(2)}) collective-permute-start(bf16[512,128]{1,0:T(8,128)(2,1)} %get-tuple-element.14), channel_id=1, source_target_pairs={{4,12},{12,20},{20,28},{8,0},{16,8},{24,16},{5,13},{13,21},{21,29}... | collective-permute-start | bytes 393224 | tf_op jit(solution)/shard_map/ppermute | solution.py:317
  16.8 0.0 copy-done
  16.9 0.0 copy-done.1
  16.9 0.0 copy-done.2
  16.9 0.5 %shard_map.105 = (f32[128,512]{1,0:T(8,128)S(1)}, f32[2,512]{1,0:T(2,128)S(1)}) custom-call(bf16[256,1024]{1,0:T(8,128)(2,1)S(1)} %copy-done, bf16[256,1024]{1,0:T(8,128)(2,1)S(1)} %copy-done.2, bf16[1024,512]{1,0:T(8,128)(2,1)S(1)} %copy-done.1), custom_call_target="tpu_custom_call" | custom-call | flops 134217728 | bytes 2097152 | tf_op jit(solution)/shard_map/pallas_call | solution.py:339
  17.4 0.0 collective-permute-done.4
  17.4 0.0 copy-done.5
  17.4 0.7 %collective-permute-start.2 = (bf16[512,128]{1,0:T(8,128)(2,1)S(1)}, bf16[512,128]{1,0:T(8,128)(2,1)S(1)}, u32[]{:S(2)}, u32[]{:S(2)}) collective-permute-start(bf16[512,128]{1,0:T(8,128)(2,1)S(1)} %copy-done.5), channel_id=1, source_target_pairs={{4,8},{12,16},{20,24},{8,4},{16,12},{24,20},{5,9},{13,17},{21,25},... | collective-permute-start | bytes 393224 | tf_op jit(solution)/shard_map/ppermute | solution.py:312
  18.1 0.0 collective-permute-done.5
  18.1 0.7 %collective-permute-done.6 = bf16[144,128]{1,0:T(8,128)(2,1)S(1)} collective-permute-done((bf16[144,128]{1,0:T(8,128)(2,1)S(1)}, bf16[144,128]{1,0:T(8,128)(2,1)S(1)}, u32[]{:S(2)}, u32[]{:S(2)}) %collective-permute-start.6) | collective-permute-done | bytes 36896 | tf_op jit(solution)/shard_map/ppermute | solution.py:329
  18.8 0.0 copy-done.4
  18.9 4.8 %collective-permute-start.7 = (bf16[144,128]{1,0:T(8,128)(2,1)S(1)}, bf16[144,128]{1,0:T(8,128)(2,1)S(1)}, u32[]{:S(2)}, u32[]{:S(2)}) collective-permute-start(bf16[144,128]{1,0:T(8,128)(2,1)S(1)} %fusion.1), channel_id=1, source_target_pairs={{0,8},{1,9},{2,10},{3,11},{4,12},{5,13},{6,14},{7,15},{8,0},{9,1},... | collective-permute-start | bytes 110600 | tf_op jit(solution)/shard_map/ppermute | solution.py:329
  23.7 2.6 %collective-permute-start.8 = (bf16[144,128]{1,0:T(8,128)(2,1)S(1)}, bf16[144,128]{1,0:T(8,128)(2,1)S(1)}, u32[]{:S(2)}, u32[]{:S(2)}) collective-permute-start(bf16[144,128]{1,0:T(8,128)(2,1)S(1)} %fusion.1), channel_id=1, source_target_pairs={{0,16},{1,17},{2,18},{3,19},{4,20},{5,21},{6,22},{7,23},{8,24},{9,... | collective-permute-start | bytes 110600 | tf_op jit(solution)/shard_map/ppermute | solution.py:329
  26.2 0.0 collective-permute-done.1.r2_ref
  26.3 0.0 collective-permute-start.9
  26.3 0.0 collective-permute-done.2.r3_ref
  26.3 0.0 collective-permute-done.r1_ref
  26.3 0.0 copy-done.3
  26.3 2.7 %shard_map.106 = bf16[32,8,256]{2,1,0:T(8,128)(2,1)} custom-call(bf16[768,128]{1,0:T(8,128)(2,1)S(1)} %copy-done.3, bf16[768,128]{1,0:T(8,128)(2,1)S(1)} %collective-permute-done.r1_ref, bf16[512,128]{1,0:T(8,128)(2,1)S(1)} %collective-permute-done.1.r2_ref, bf16[512,128]{1,0:T(8,128)(2,1)S(1)} %collective-permute-done.2.r3_ref, ...), custom_call_target="tpu_custom_call" | custom-call | flops 402653184 | bytes 655360 | tf_op jit(solution)/shard_map/pallas_call | solution.py:346
  28.9 5.9 %all-to-all-start = ((bf16[32,8,256]{2,1,0:T(8,128)(2,1)}), bf16[32,8,256]{2,1,0:T(8,128)(2,1)S(1)}, u32[]{:S(2)}, u32[]{:S(2)}) async-start(bf16[32,8,256]{2,1,0:T(8,128)(2,1)} %shard_map.106), calls=%async_computation | async-start | bytes 262144 | tf_op jit(solution)/shard_map/all_to_all | solution.py:361
  34.8 0.0 collective-permute-done.7
  34.8 0.0 collective-permute-done.8
  34.8 0.0 collective-permute-done.9
  34.8 0.1 fusion.2
  34.9 0.3 collective-permute-start.10
  35.9 0.3 collective-permute-done.10.last_ref
  36.2 6.9 %all-to-all-done.everyone_ref = bf16[32,8,256]{2,1,0:T(8,128)(2,1)S(1)} async-done(((bf16[32,8,256]{2,1,0:T(8,128)(2,1)}), bf16[32,8,256]{2,1,0:T(8,128)(2,1)S(1)}, u32[]{:S(2)}, u32[]{:S(2)}) %all-to-all-start) | async-done | bytes 131104 | tf_op jit(solution)/shard_map/all_to_all | solution.py:361
  43.0 1.5 %shard_map.107 = (f32[2,512]{1,0:T(2,128)}, f32[1,2]{1,0:T(1,128)}) custom-call(bf16[32,8,256]{2,1,0:T(8,128)(2,1)S(1)} %all-to-all-done.everyone_ref, f32[144,128]{1,0:T(8,128)S(1)} %get-tuple-element.23.mine_ref, bf16[144,128]{1,0:T(8,128)(2,1)S(1)} %collective-permute-done.10.last_ref, f32[1]{0:T(128)S(6)} %copy.12.divisor_ref), custom_call_target="tpu_custom_call" | custom-call | flops 8388608 | bytes 131072 | tf_op jit(solution)/shard_map/pallas_call | solution.py:364
  (1 shorter events, 0.0 us)
Async XLA Ops:
  2.0 14.8 %copy-start = (bf16[256,1024]{1,0:T(8,128)(2,1)S(1)}, bf16[256,1024]{1,0:T(8,128)(2,1)}, u32[]{:S(2)}) copy-start(bf16[256,1024]{1,0:T(8,128)(2,1)} %frames_ref.1) | copy-start | bytes 1572868
  2.0 14.8 %copy-start.1 = (bf16[1024,512]{1,0:T(8,128)(2,1)S(1)}, bf16[1024,512]{1,0:T(8,128)(2,1)}, u32[]{:S(2)}) copy-start(bf16[1024,512]{1,0:T(8,128)(2,1)} %w_proj_ref.1) | copy-start | bytes 3145732
  2.0 14.8 %copy-start.2 = (bf16[256,1024]{1,0:T(8,128)(2,1)S(1)}, bf16[256,1024]{1,0:T(8,128)(2,1)}, u32[]{:S(2)}) copy-start(bf16[256,1024]{1,0:T(8,128)(2,1)} %w_out_ref.1) | copy-start | bytes 1572868
  6.6 10.8 %copy-start.5 = (bf16[512,128]{1,0:T(8,128)(2,1)S(1)}, bf16[512,128]{1,0:T(8,128)(2,1)}, u32[]{:S(2)}) copy-start(bf16[512,128]{1,0:T(8,128)(2,1)} %get-tuple-element.15) | copy-start | bytes 393220
  6.7 12.2 %copy-start.4 = (f32[144,128]{1,0:T(8,128)S(1)}, f32[144,128]{1,0:T(8,128)}, u32[]{:S(2)}) copy-start(f32[144,128]{1,0:T(8,128)} %get-tuple-element.18) | copy-start | bytes 221188
  6.7 19.6 %copy-start.3 = (bf16[768,128]{1,0:T(8,128)(2,1)S(1)}, bf16[768,128]{1,0:T(8,128)(2,1)}, u32[]{:S(2)}) copy-start(bf16[768,128]{1,0:T(8,128)(2,1)} %get-tuple-element.12.own_ref) | copy-start | bytes 589828
  6.7 1.6 %collective-permute-start.3 = (bf16[144,128]{1,0:T(8,128)(2,1)}, bf16[144,128]{1,0:T(8,128)(2,1)S(1)}, u32[]{:S(2)}, u32[]{:S(2)}) collective-permute-start(bf16[144,128]{1,0:T(8,128)(2,1)} %get-tuple-element.19), channel_id=1, source_target_pairs={{0,1},{1,0},{2,3},{3,2},{4,5},{5,4},{6,7},{7,6},{8,9},{9,8},{10,11... | collective-permute-start | bytes 110600 | tf_op jit(solution)/shard_map/ppermute | solution.py:329
  9.2 8.2 %collective-permute-start.4 = (bf16[144,128]{1,0:T(8,128)(2,1)S(1)}, bf16[144,128]{1,0:T(8,128)(2,1)S(1)}, u32[]{:S(2)}, u32[]{:S(2)}) collective-permute-start(bf16[144,128]{1,0:T(8,128)(2,1)S(1)} %fusion), channel_id=1, source_target_pairs={{0,2},{1,3},{2,0},{3,1},{4,6},{5,7},{6,4},{7,5},{8,10},{9,11},{10,... | collective-permute-start | bytes 110600 | tf_op jit(solution)/shard_map/ppermute | solution.py:329
  12.1 6.0 %collective-permute-start.5 = (bf16[144,128]{1,0:T(8,128)(2,1)S(1)}, bf16[144,128]{1,0:T(8,128)(2,1)S(1)}, u32[]{:S(2)}, u32[]{:S(2)}) collective-permute-start(bf16[144,128]{1,0:T(8,128)(2,1)S(1)} %fusion), channel_id=1, source_target_pairs={{0,4},{1,5},{2,6},{3,7},{4,0},{5,1},{6,2},{7,3},{8,12},{9,13},{10,... | collective-permute-start | bytes 110600 | tf_op jit(solution)/shard_map/ppermute | solution.py:329
  13.6 5.2 %collective-permute-start.6 = (bf16[144,128]{1,0:T(8,128)(2,1)S(1)}, bf16[144,128]{1,0:T(8,128)(2,1)S(1)}, u32[]{:S(2)}, u32[]{:S(2)}) collective-permute-start(bf16[144,128]{1,0:T(8,128)(2,1)S(1)} %fusion), channel_id=1, source_target_pairs={{0,6},{1,7},{2,4},{3,5},{4,2},{5,3},{6,0},{7,1},{8,14},{9,15},{10,... | collective-permute-start | bytes 110600 | tf_op jit(solution)/shard_map/ppermute | solution.py:329
  13.6 12.6 %collective-permute-start = (bf16[768,128]{1,0:T(8,128)(2,1)}, bf16[768,128]{1,0:T(8,128)(2,1)S(1)}, u32[]{:S(2)}, u32[]{:S(2)}) collective-permute-start(bf16[768,128]{1,0:T(8,128)(2,1)} %get-tuple-element.13), channel_id=1, source_target_pairs={{0,4},{4,0},{8,12},{12,8},{16,20},{20,16},{24,28},{28,24},{1,5},{5... | collective-permute-start | bytes 589832 | tf_op jit(solution)/shard_map/ppermute | solution.py:311
  15.6 10.7 %collective-permute-start.1 = (bf16[512,128]{1,0:T(8,128)(2,1)}, bf16[512,128]{1,0:T(8,128)(2,1)S(1)}, u32[]{:S(2)}, u32[]{:S(2)}) collective-permute-start(bf16[512,128]{1,0:T(8,128)(2,1)} %get-tuple-element.14), channel_id=1, source_target_pairs={{4,12},{12,20},{20,28},{8,0},{16,8},{24,16},{5,13},{13,21},{21,29}... | collective-permute-start | bytes 393224 | tf_op jit(solution)/shard_map/ppermute | solution.py:317
  17.4 8.8 %collective-permute-start.2 = (bf16[512,128]{1,0:T(8,128)(2,1)S(1)}, bf16[512,128]{1,0:T(8,128)(2,1)S(1)}, u32[]{:S(2)}, u32[]{:S(2)}) collective-permute-start(bf16[512,128]{1,0:T(8,128)(2,1)S(1)} %copy-done.5), channel_id=1, source_target_pairs={{4,8},{12,16},{20,24},{8,4},{16,12},{24,20},{5,9},{13,17},{21,25},... | collective-permute-start | bytes 393224 | tf_op jit(solution)/shard_map/ppermute | solution.py:312
  18.9 16.0 %collective-permute-start.7 = (bf16[144,128]{1,0:T(8,128)(2,1)S(1)}, bf16[144,128]{1,0:T(8,128)(2,1)S(1)}, u32[]{:S(2)}, u32[]{:S(2)}) collective-permute-start(bf16[144,128]{1,0:T(8,128)(2,1)S(1)} %fusion.1), channel_id=1, source_target_pairs={{0,8},{1,9},{2,10},{3,11},{4,12},{5,13},{6,14},{7,15},{8,0},{9,1},... | collective-permute-start | bytes 110600 | tf_op jit(solution)/shard_map/ppermute | solution.py:329
  23.7 11.2 %collective-permute-start.8 = (bf16[144,128]{1,0:T(8,128)(2,1)S(1)}, bf16[144,128]{1,0:T(8,128)(2,1)S(1)}, u32[]{:S(2)}, u32[]{:S(2)}) collective-permute-start(bf16[144,128]{1,0:T(8,128)(2,1)S(1)} %fusion.1), channel_id=1, source_target_pairs={{0,16},{1,17},{2,18},{3,19},{4,20},{5,21},{6,22},{7,23},{8,24},{9,... | collective-permute-start | bytes 110600 | tf_op jit(solution)/shard_map/ppermute | solution.py:329
  26.3 8.6 %collective-permute-start.9 = (bf16[144,128]{1,0:T(8,128)(2,1)S(1)}, bf16[144,128]{1,0:T(8,128)(2,1)S(1)}, u32[]{:S(2)}, u32[]{:S(2)}) collective-permute-start(bf16[144,128]{1,0:T(8,128)(2,1)S(1)} %fusion.1), channel_id=1, source_target_pairs={{0,24},{1,25},{2,26},{3,27},{4,28},{5,29},{6,30},{7,31},{8,16},{9,... | collective-permute-start | bytes 110600 | tf_op jit(solution)/shard_map/ppermute | solution.py:329
  28.9 14.1 %all-to-all-start = ((bf16[32,8,256]{2,1,0:T(8,128)(2,1)}), bf16[32,8,256]{2,1,0:T(8,128)(2,1)S(1)}, u32[]{:S(2)}, u32[]{:S(2)}) async-start(bf16[32,8,256]{2,1,0:T(8,128)(2,1)} %shard_map.106), calls=%async_computation | async-start | bytes 262144 | tf_op jit(solution)/shard_map/all_to_all | solution.py:361
  34.9 1.3 %collective-permute-start.10 = (bf16[144,128]{1,0:T(8,128)(2,1)S(1)}, bf16[144,128]{1,0:T(8,128)(2,1)S(1)}, u32[]{:S(2)}, u32[]{:S(2)}) collective-permute-start(bf16[144,128]{1,0:T(8,128)(2,1)S(1)} %get-tuple-element.22), channel_id=1, source_target_pairs={{0,1},{1,0},{2,3},{3,2},{4,5},{5,4},{6,7},{7,6},{8,9},{9,8},{10,11... | collective-permute-start | bytes 110600 | tf_op jit(solution)/shard_map/ppermute | solution.py:329

commit v4 on v3

--- a/solution.py
+++ b/solution.py
@@ -72,11 +72,11 @@
         copies[k].start()
     odd = lax.axis_index("seq") % 2 == 1
 
-    caps, tokens = ids_ref.shape
+    tokens, caps = ids_ref.shape
     vocab = table.shape[0]
     own_caps = bounds_ref.shape[0]
     slot = lax.axis_index("seq") * lax.axis_size("head") + lax.axis_index("head")
-    ids = ids_ref[...] - slot * vocab
+    ids = (ids_ref[...] - slot * vocab).T
     words = lax.broadcasted_iota(jnp.int32, (caps, vocab), 1)
     counts = jnp.zeros((caps, vocab), jnp.float32)
     for t in range(tokens):
@@ -306,7 +306,7 @@
         ],
         (6 * rows * width * cols, 2 * w_qkv.size, 0),
         60,
-    )(frames, norm_gain[None], w_qkv, token_ids, text_table, span_bounds)
+    )(frames, norm_gain[None], w_qkv, token_ids.T, text_table, span_bounds)
     ends = seq_count - 1
     r1 = lax.ppermute(p1, "seq", [(s, s ^ 1) for s in range(seq_count)])
     r3 = lax.ppermute(
@@ -334,22 +334,24 @@
         return mine, mine.astype(bf16)
 
     mine, sent = add(mine, swap(sent, 0, 1))
-    mine, sent = add(mine, swap(sent, 0, 2), swap(sent, 1, 0), swap(sent, 1, 2))
+    gots = [swap(sent, 0, 2), swap(sent, 1, 0), swap(sent, 1, 2)]
 
     wc, fp = call(
         weights_kernel,
         [shape((half, E), f32), shape((blocks, E), f32)],
         [VMEM] * 3,
-        cost=(2 * half * w_proj.size, 2 * (w_proj.size + w_out.size + frames.size), 0),
+        cost=(10**10, 2 * (w_proj.size + w_out.size + frames.size), 0),
     )(frames, w_out, w_proj)
 
     piece = call(
         attend_kernel,
         shape((devices, 4 * blocks, E // 2), PIECE),
         [VMEM] * 6,
-        cost=(24 * rows * rows * cols, 10 * rows * cols, 6 * rows * rows * cols // HDIM),
+        cost=(10**10, 10 * rows * cols, 6 * rows * rows * cols // HDIM),
     )(own, r1, r2, r3, wc, fp)
 
+    gots, piece = lax.optimization_barrier((gots, piece))
+    mine, sent = add(mine, *gots)
     step = 2
     while step < seq_count:
         if 4 * step <= seq_count:

time: 44.8 us -> 41.9 us (0.935)
  starting transfers between devices: 22.4 us -> 20.6 us
  local copies, waits for them, and re-layouts: 1.42 us -> 0.02 us
  waiting for transfers between devices: 8.99 us -> 10.3 us
  other arithmetic: 0.98 us -> 0.09 us
    all_to_all x1, starting transfers between devices: 5.86 us -> 3.91 us  [local(): everyone = lax.all_to_all(piece, EVERY, 0, 0)]
    unnamed x13 -> x10, local copies, waits for them, and re-layouts: 1.42 us -> 0.02 us
    ppermute x8, waiting for transfers between devices: 2.12 us -> 3.48 us  [swap(): return lax.ppermute(sent, EVERY, list(enumerate(to)))]
    ppermute x1, starting transfers between devices: 1.92 us -> 3 us  [local(): r1 = lax.ppermute(p1, 'seq', [(s, s ^ 1) for s in range(seq_count)])]
    ppermute x8, starting transfers between devices: 12.7 us -> 11.7 us  [swap(): return lax.ppermute(sent, EVERY, list(enumerate(to)))]
    convert_element_type x3, other arithmetic: 0.98 us -> 0.09 us  [add(): return (mine, mine.astype(bf16))]
  transfers between devices with their start and end apart: 12 -> 12, of which waited for: 4 -> 5; matrix products, arithmetic and copies ran while one was open for 0% -> 0% of each run, Pallas kernels for 7% -> 8%
where the time goes in v4:
time: 41.9 us; the launch traced here: 41.6 us
  starting transfers between devices  20.6 us (49%)
  waiting for transfers between devices  10.3 us (25%)
  Pallas kernels  9.2 us (22%)
  between operations  1.44 us (3%)
    ppermute x8, starting transfers between devices, swap(): return lax.ppermute(sent, EVERY, list(enumerate(to)))  11.7 us
    all_to_all x1, waiting for transfers between devices, local(): everyone = lax.all_to_all(piece, EVERY, 0, 0)  6.8 us
    pallas_call x1, Pallas kernels, local(): call(first_kernel, [shape((n * rows, half), bf16) for n in (3, 3, 2, 2)]...  4.53 us
    all_to_all x1, starting transfers between devices, local(): everyone = lax.all_to_all(piece, EVERY, 0, 0)  3.91 us
    ppermute x8, waiting for transfers between devices, swap(): return lax.ppermute(sent, EVERY, list(enumerate(to)))  3.48 us
    ppermute x1, starting transfers between devices, local(): r1 = lax.ppermute(p1, 'seq', [(s, s ^ 1) for s in range(seq_count)])  3 us
    pallas_call x1, Pallas kernels, local(): call(attend_kernel, shape((devices, 4 * blocks, E // 2), PIECE), [VMEM] *...  2.66 us
    pallas_call x1, Pallas kernels, local(): call(tail_kernel, [shape((own_caps, E), f32), shape((1, own_caps), f32)],...  1.48 us
  transfers between devices with their start and end apart: 12, of which 5 were waited for; matrix products, arithmetic and copies ran while one was open for 0% of the time, Pallas kernels for 8%

profile of v4, /device:TPU:0, one launch (start us, length us, event | category | flops | bytes accessed | tf_op | source)
XLA Modules:
  0.0 41.6 jit_solution(725283794804527443)
XLA Ops:
  0.6 0.0 copy-start
  0.6 0.0 copy-start.1
  0.7 0.0 copy-start.2
  0.7 4.5 %shard_map.104 = (bf16[768,128]{1,0:T(8,128)(2,1)}, bf16[768,128]{1,0:T(8,128)(2,1)}, bf16[512,128]{1,0:T(8,128)(2,1)}, bf16[512,128]{1,0:T(8,128)(2,1)}, f32[144,128]{1,0:T(8,128)}, /*index=5*/bf16[144,128]{1,0:T(8,128)(2,1)}) custom-call(bf16[256,1024]{1,0:T(8,128)(2,1)} %frames_ref.1, f32[1,1024]{1,0:T(1,128)} %bitcast.4, bf16[3,1024,256]{2,1,0:T(8,128)(2,1)} %w_hbm.1, ...), custom_call_target="tpu_custom_call" | custom-call | flops 402653184 | bytes 1572864 | tf_op jit(solution)/shard_map/pallas_call | solution.py:295
  5.2 3.0 %collective-permute-start.4 = (bf16[768,128]{1,0:T(8,128)(2,1)}, bf16[768,128]{1,0:T(8,128)(2,1)S(1)}, u32[]{:S(2)}, u32[]{:S(2)}) collective-permute-start(bf16[768,128]{1,0:T(8,128)(2,1)} %get-tuple-element.19), channel_id=1, source_target_pairs={{0,4},{4,0},{8,12},{12,8},{16,20},{20,16},{24,28},{28,24},{1,5},{5... | collective-permute-start | bytes 589832 | tf_op jit(solution)/shard_map/ppermute | solution.py:311
  8.2 1.3 %collective-permute-start.5 = (bf16[512,128]{1,0:T(8,128)(2,1)}, bf16[512,128]{1,0:T(8,128)(2,1)S(1)}, u32[]{:S(2)}, u32[]{:S(2)}) collective-permute-start(bf16[512,128]{1,0:T(8,128)(2,1)} %get-tuple-element.20), channel_id=1, source_target_pairs={{4,12},{12,20},{20,28},{8,0},{16,8},{24,16},{5,13},{13,21},{21,29}... | collective-permute-start | bytes 393224 | tf_op jit(solution)/shard_map/ppermute | solution.py:317
  9.5 0.7 %collective-permute-start.6 = (bf16[512,128]{1,0:T(8,128)(2,1)}, bf16[512,128]{1,0:T(8,128)(2,1)S(1)}, u32[]{:S(2)}, u32[]{:S(2)}) collective-permute-start(bf16[512,128]{1,0:T(8,128)(2,1)} %get-tuple-element.21), channel_id=1, source_target_pairs={{4,8},{12,16},{20,24},{8,4},{16,12},{24,20},{5,9},{13,17},{21,25},... | collective-permute-start | bytes 393224 | tf_op jit(solution)/shard_map/ppermute | solution.py:312
  10.2 0.0 copy-start.4
  10.2 0.0 copy-start.3
  10.2 0.1 collective-permute-start
  10.3 0.0 copy-done
  10.3 0.0 copy-done.1
  10.3 0.0 copy-done.2
  10.3 0.5 %shard_map.105 = (f32[128,512]{1,0:T(8,128)S(1)}, f32[2,512]{1,0:T(2,128)S(1)}) custom-call(bf16[256,1024]{1,0:T(8,128)(2,1)S(1)} %copy-done, bf16[256,1024]{1,0:T(8,128)(2,1)S(1)} %copy-done.2, bf16[1024,512]{1,0:T(8,128)(2,1)S(1)} %copy-done.1), custom_call_target="tpu_custom_call" | custom-call | flops 10000000000 | bytes 2097152 | tf_op jit(solution)/shard_map/pallas_call | solution.py:339
  10.8 0.9 %collective-permute-done = bf16[144,128]{1,0:T(8,128)(2,1)S(1)} collective-permute-done((bf16[144,128]{1,0:T(8,128)(2,1)}, bf16[144,128]{1,0:T(8,128)(2,1)S(1)}, u32[]{:S(2)}, u32[]{:S(2)}) %collective-permute-start) | collective-permute-done | bytes 36896 | tf_op jit(solution)/shard_map/ppermute | solution.py:329
  11.7 0.0 copy-done.4
  11.7 1.6 %collective-permute-start.1 = (bf16[144,128]{1,0:T(8,128)(2,1)S(1)}, bf16[144,128]{1,0:T(8,128)(2,1)S(1)}, u32[]{:S(2)}, u32[]{:S(2)}) collective-permute-start(bf16[144,128]{1,0:T(8,128)(2,1)S(1)} %fusion), channel_id=1, source_target_pairs={{0,2},{1,3},{2,0},{3,1},{4,6},{5,7},{6,4},{7,5},{8,10},{9,11},{10,... | collective-permute-start | bytes 110600 | tf_op jit(solution)/shard_map/ppermute | solution.py:329
  13.3 5.3 %collective-permute-start.2 = (bf16[144,128]{1,0:T(8,128)(2,1)S(1)}, bf16[144,128]{1,0:T(8,128)(2,1)S(1)}, u32[]{:S(2)}, u32[]{:S(2)}) collective-permute-start(bf16[144,128]{1,0:T(8,128)(2,1)S(1)} %fusion), channel_id=1, source_target_pairs={{0,4},{1,5},{2,6},{3,7},{4,0},{5,1},{6,2},{7,3},{8,12},{9,13},{10,... | collective-permute-start | bytes 110600 | tf_op jit(solution)/shard_map/ppermute | solution.py:329
  18.6 0.0 collective-permute-done.5.r2_ref
  18.6 0.0 collective-permute-start.3
  18.6 0.0 collective-permute-done.6.r3_ref
  18.6 0.0 collective-permute-done.4.r1_ref
  18.6 0.0 copy-done.3
  18.7 2.7 %shard_map.106 = bf16[32,8,256]{2,1,0:T(8,128)(2,1)} custom-call(bf16[768,128]{1,0:T(8,128)(2,1)S(1)} %copy-done.3, bf16[768,128]{1,0:T(8,128)(2,1)S(1)} %collective-permute-done.4.r1_ref, bf16[512,128]{1,0:T(8,128)(2,1)S(1)} %collective-permute-done.5.r2_ref, bf16[512,128]{1,0:T(8,128)(2,1)S(1)} %collective-permute-done.6.r3_ref, ...), custom_call_target="tpu_custom_call" | custom-call | flops 10000000000 | bytes 655360 | tf_op jit(solution)/shard_map/pallas_call | solution.py:346
  21.3 0.0 collective-permute-done.1
  21.3 0.0 collective-permute-done.2
  21.3 2.2 %collective-permute-done.3 = bf16[144,128]{1,0:T(8,128)(2,1)S(1)} collective-permute-done((bf16[144,128]{1,0:T(8,128)(2,1)S(1)}, bf16[144,128]{1,0:T(8,128)(2,1)S(1)}, u32[]{:S(2)}, u32[]{:S(2)}) %collective-permute-start.3) | collective-permute-done | bytes 36896 | tf_op jit(solution)/shard_map/ppermute | solution.py:329
  23.5 1.6 %collective-permute-start.7 = (bf16[144,128]{1,0:T(8,128)(2,1)S(1)}, bf16[144,128]{1,0:T(8,128)(2,1)S(1)}, u32[]{:S(2)}, u32[]{:S(2)}) collective-permute-start(bf16[144,128]{1,0:T(8,128)(2,1)S(1)} %fusion.1), channel_id=1, source_target_pairs={{0,8},{1,9},{2,10},{3,11},{4,12},{5,13},{6,14},{7,15},{8,0},{9,1},... | collective-permute-start | bytes 110600 | tf_op jit(solution)/shard_map/ppermute | solution.py:329
  25.2 1.1 %collective-permute-start.8 = (bf16[144,128]{1,0:T(8,128)(2,1)S(1)}, bf16[144,128]{1,0:T(8,128)(2,1)S(1)}, u32[]{:S(2)}, u32[]{:S(2)}) collective-permute-start(bf16[144,128]{1,0:T(8,128)(2,1)S(1)} %fusion.1), channel_id=1, source_target_pairs={{0,16},{1,17},{2,18},{3,19},{4,20},{5,21},{6,22},{7,23},{8,24},{9,... | collective-permute-start | bytes 110600 | tf_op jit(solution)/shard_map/ppermute | solution.py:329
  26.3 1.7 %collective-permute-start.9 = (bf16[144,128]{1,0:T(8,128)(2,1)S(1)}, bf16[144,128]{1,0:T(8,128)(2,1)S(1)}, u32[]{:S(2)}, u32[]{:S(2)}) collective-permute-start(bf16[144,128]{1,0:T(8,128)(2,1)S(1)} %fusion.1), channel_id=1, source_target_pairs={{0,24},{1,25},{2,26},{3,27},{4,28},{5,29},{6,30},{7,31},{8,16},{9,... | collective-permute-start | bytes 110600 | tf_op jit(solution)/shard_map/ppermute | solution.py:329
  28.0 3.9 %all-to-all-start = ((bf16[32,8,256]{2,1,0:T(8,128)(2,1)}), bf16[32,8,256]{2,1,0:T(8,128)(2,1)S(1)}, u32[]{:S(2)}, u32[]{:S(2)}) async-start(bf16[32,8,256]{2,1,0:T(8,128)(2,1)} %shard_map.106), calls=%async_computation | async-start | bytes 262144 | tf_op jit(solution)/shard_map/all_to_all | solution.py:363
  31.9 0.0 collective-permute-done.7
  31.9 0.0 collective-permute-done.8
  31.9 0.1 collective-permute-done.9
  32.1 0.2 collective-permute-start.10
  33.0 0.4 collective-permute-done.10.last_ref
  33.4 6.8 %all-to-all-done.everyone_ref = bf16[32,8,256]{2,1,0:T(8,128)(2,1)S(1)} async-done(((bf16[32,8,256]{2,1,0:T(8,128)(2,1)}), bf16[32,8,256]{2,1,0:T(8,128)(2,1)S(1)}, u32[]{:S(2)}, u32[]{:S(2)}) %all-to-all-start) | async-done | bytes 131104 | tf_op jit(solution)/shard_map/all_to_all | solution.py:363
  40.2 1.5 %shard_map.107 = (f32[2,512]{1,0:T(2,128)}, f32[1,2]{1,0:T(1,128)}) custom-call(bf16[32,8,256]{2,1,0:T(8,128)(2,1)S(1)} %all-to-all-done.everyone_ref, f32[144,128]{1,0:T(8,128)S(1)} %get-tuple-element.31.mine_ref, bf16[144,128]{1,0:T(8,128)(2,1)S(1)} %collective-permute-done.10.last_ref, f32[1]{0:T(128)S(6)} %copy.11.divisor_ref), custom_call_target="tpu_custom_call" | custom-call | flops 8388608 | bytes 131072 | tf_op jit(solution)/shard_map/pallas_call | solution.py:366
  (3 shorter events, 0.1 us)
Async XLA Ops:
  0.6 9.6 %copy-start = (bf16[256,1024]{1,0:T(8,128)(2,1)S(1)}, bf16[256,1024]{1,0:T(8,128)(2,1)}, u32[]{:S(2)}) copy-start(bf16[256,1024]{1,0:T(8,128)(2,1)} %frames_ref.1) | copy-start | bytes 1572868
  0.6 9.6 %copy-start.1 = (bf16[1024,512]{1,0:T(8,128)(2,1)S(1)}, bf16[1024,512]{1,0:T(8,128)(2,1)}, u32[]{:S(2)}) copy-start(bf16[1024,512]{1,0:T(8,128)(2,1)} %w_proj_ref.1) | copy-start | bytes 3145732
  0.7 9.6 %copy-start.2 = (bf16[256,1024]{1,0:T(8,128)(2,1)S(1)}, bf16[256,1024]{1,0:T(8,128)(2,1)}, u32[]{:S(2)}) copy-start(bf16[256,1024]{1,0:T(8,128)(2,1)} %w_out_ref.1) | copy-start | bytes 1572868
  5.2 13.4 %collective-permute-start.4 = (bf16[768,128]{1,0:T(8,128)(2,1)}, bf16[768,128]{1,0:T(8,128)(2,1)S(1)}, u32[]{:S(2)}, u32[]{:S(2)}) collective-permute-start(bf16[768,128]{1,0:T(8,128)(2,1)} %get-tuple-element.19), channel_id=1, source_target_pairs={{0,4},{4,0},{8,12},{12,8},{16,20},{20,16},{24,28},{28,24},{1,5},{5... | collective-permute-start | bytes 589832 | tf_op jit(solution)/shard_map/ppermute | solution.py:311
  8.2 10.4 %collective-permute-start.5 = (bf16[512,128]{1,0:T(8,128)(2,1)}, bf16[512,128]{1,0:T(8,128)(2,1)S(1)}, u32[]{:S(2)}, u32[]{:S(2)}) collective-permute-start(bf16[512,128]{1,0:T(8,128)(2,1)} %get-tuple-element.20), channel_id=1, source_target_pairs={{4,12},{12,20},{20,28},{8,0},{16,8},{24,16},{5,13},{13,21},{21,29}... | collective-permute-start | bytes 393224 | tf_op jit(solution)/shard_map/ppermute | solution.py:317
  9.5 9.1 %collective-permute-start.6 = (bf16[512,128]{1,0:T(8,128)(2,1)}, bf16[512,128]{1,0:T(8,128)(2,1)S(1)}, u32[]{:S(2)}, u32[]{:S(2)}) collective-permute-start(bf16[512,128]{1,0:T(8,128)(2,1)} %get-tuple-element.21), channel_id=1, source_target_pairs={{4,8},{12,16},{20,24},{8,4},{16,12},{24,20},{5,9},{13,17},{21,25},... | collective-permute-start | bytes 393224 | tf_op jit(solution)/shard_map/ppermute | solution.py:312
  10.2 1.5 %copy-start.4 = (f32[144,128]{1,0:T(8,128)S(1)}, f32[144,128]{1,0:T(8,128)}, u32[]{:S(2)}) copy-start(f32[144,128]{1,0:T(8,128)} %get-tuple-element.16) | copy-start | bytes 221188
  10.2 8.5 %copy-start.3 = (bf16[768,128]{1,0:T(8,128)(2,1)S(1)}, bf16[768,128]{1,0:T(8,128)(2,1)}, u32[]{:S(2)}) copy-start(bf16[768,128]{1,0:T(8,128)(2,1)} %get-tuple-element.18.own_ref) | copy-start | bytes 589828
  10.2 1.5 %collective-permute-start = (bf16[144,128]{1,0:T(8,128)(2,1)}, bf16[144,128]{1,0:T(8,128)(2,1)S(1)}, u32[]{:S(2)}, u32[]{:S(2)}) collective-permute-start(bf16[144,128]{1,0:T(8,128)(2,1)} %get-tuple-element.17), channel_id=1, source_target_pairs={{0,1},{1,0},{2,3},{3,2},{4,5},{5,4},{6,7},{7,6},{8,9},{9,8},{10,11... | collective-permute-start | bytes 110600 | tf_op jit(solution)/shard_map/ppermute | solution.py:329
  11.7 9.6 %collective-permute-start.1 = (bf16[144,128]{1,0:T(8,128)(2,1)S(1)}, bf16[144,128]{1,0:T(8,128)(2,1)S(1)}, u32[]{:S(2)}, u32[]{:S(2)}) collective-permute-start(bf16[144,128]{1,0:T(8,128)(2,1)S(1)} %fusion), channel_id=1, source_target_pairs={{0,2},{1,3},{2,0},{3,1},{4,6},{5,7},{6,4},{7,5},{8,10},{9,11},{10,... | collective-permute-start | bytes 110600 | tf_op jit(solution)/shard_map/ppermute | solution.py:329
  13.3 8.0 %collective-permute-start.2 = (bf16[144,128]{1,0:T(8,128)(2,1)S(1)}, bf16[144,128]{1,0:T(8,128)(2,1)S(1)}, u32[]{:S(2)}, u32[]{:S(2)}) collective-permute-start(bf16[144,128]{1,0:T(8,128)(2,1)S(1)} %fusion), channel_id=1, source_target_pairs={{0,4},{1,5},{2,6},{3,7},{4,0},{5,1},{6,2},{7,3},{8,12},{9,13},{10,... | collective-permute-start | bytes 110600 | tf_op jit(solution)/shard_map/ppermute | solution.py:329
  18.6 4.9 %collective-permute-start.3 = (bf16[144,128]{1,0:T(8,128)(2,1)S(1)}, bf16[144,128]{1,0:T(8,128)(2,1)S(1)}, u32[]{:S(2)}, u32[]{:S(2)}) collective-permute-start(bf16[144,128]{1,0:T(8,128)(2,1)S(1)} %fusion), channel_id=1, source_target_pairs={{0,6},{1,7},{2,4},{3,5},{4,2},{5,3},{6,0},{7,1},{8,14},{9,15},{10,... | collective-permute-start | bytes 110600 | tf_op jit(solution)/shard_map/ppermute | solution.py:329
  23.5 8.4 %collective-permute-start.7 = (bf16[144,128]{1,0:T(8,128)(2,1)S(1)}, bf16[144,128]{1,0:T(8,128)(2,1)S(1)}, u32[]{:S(2)}, u32[]{:S(2)}) collective-permute-start(bf16[144,128]{1,0:T(8,128)(2,1)S(1)} %fusion.1), channel_id=1, source_target_pairs={{0,8},{1,9},{2,10},{3,11},{4,12},{5,13},{6,14},{7,15},{8,0},{9,1},... | collective-permute-start | bytes 110600 | tf_op jit(solution)/shard_map/ppermute | solution.py:329
  25.2 6.8 %collective-permute-start.8 = (bf16[144,128]{1,0:T(8,128)(2,1)S(1)}, bf16[144,128]{1,0:T(8,128)(2,1)S(1)}, u32[]{:S(2)}, u32[]{:S(2)}) collective-permute-start(bf16[144,128]{1,0:T(8,128)(2,1)S(1)} %fusion.1), channel_id=1, source_target_pairs={{0,16},{1,17},{2,18},{3,19},{4,20},{5,21},{6,22},{7,23},{8,24},{9,... | collective-permute-start | bytes 110600 | tf_op jit(solution)/shard_map/ppermute | solution.py:329
  26.3 5.8 %collective-permute-start.9 = (bf16[144,128]{1,0:T(8,128)(2,1)S(1)}, bf16[144,128]{1,0:T(8,128)(2,1)S(1)}, u32[]{:S(2)}, u32[]{:S(2)}) collective-permute-start(bf16[144,128]{1,0:T(8,128)(2,1)S(1)} %fusion.1), channel_id=1, source_target_pairs={{0,24},{1,25},{2,26},{3,27},{4,28},{5,29},{6,30},{7,31},{8,16},{9,... | collective-permute-start | bytes 110600 | tf_op jit(solution)/shard_map/ppermute | solution.py:329
  28.0 12.1 %all-to-all-start = ((bf16[32,8,256]{2,1,0:T(8,128)(2,1)}), bf16[32,8,256]{2,1,0:T(8,128)(2,1)S(1)}, u32[]{:S(2)}, u32[]{:S(2)}) async-start(bf16[32,8,256]{2,1,0:T(8,128)(2,1)} %shard_map.106), calls=%async_computation | async-start | bytes 262144 | tf_op jit(solution)/shard_map/all_to_all | solution.py:363
  32.1 1.3 %collective-permute-start.10 = (bf16[144,128]{1,0:T(8,128)(2,1)S(1)}, bf16[144,128]{1,0:T(8,128)(2,1)S(1)}, u32[]{:S(2)}, u32[]{:S(2)}) collective-permute-start(bf16[144,128]{1,0:T(8,128)(2,1)S(1)} %get-tuple-element.30), channel_id=1, source_target_pairs={{0,1},{1,0},{2,3},{3,2},{4,5},{5,4},{6,7},{7,6},{8,9},{9,8},{10,11... | collective-permute-start | bytes 110600 | tf_op jit(solution)/shard_map/ppermute | solution.py:329

commit v5 on v4

--- a/solution.py
+++ b/solution.py
@@ -334,7 +334,9 @@
         return mine, mine.astype(bf16)
 
     mine, sent = add(mine, swap(sent, 0, 1))
-    gots = [swap(sent, 0, 2), swap(sent, 1, 0), swap(sent, 1, 2)]
+    got, r1 = lax.optimization_barrier((swap(sent, 0, 2), r1))
+    mine, sent = add(mine, got)
+    got = swap(sent, 1, 0)
 
     wc, fp = call(
         weights_kernel,
@@ -350,8 +352,8 @@
         cost=(10**10, 10 * rows * cols, 6 * rows * rows * cols // HDIM),
     )(own, r1, r2, r3, wc, fp)
 
-    gots, piece = lax.optimization_barrier((gots, piece))
-    mine, sent = add(mine, *gots)
+    got, piece = lax.optimization_barrier((got, piece))
+    mine, sent = add(mine, got)
     step = 2
     while step < seq_count:
         if 4 * step <= seq_count:

time: 41.9 us -> 42.7 us (1.019)
  waiting for transfers between devices: 10.3 us -> 9.35 us
  other arithmetic: 0.09 us -> 0.99 us
  starting transfers between devices: 20.6 us -> 21.4 us
    all_to_all x1, starting transfers between devices: 3.91 us -> 4.9 us  [local(): everyone = lax.all_to_all(piece, EVERY, 0, 0)]
    convert_element_type x3 -> x4, other arithmetic: 0.09 us -> 0.99 us  [add(): return (mine, mine.astype(bf16))]
    ppermute x8 -> x7, waiting for transfers between devices: 3.48 us -> 2.86 us  [swap(): return lax.ppermute(sent, EVERY, list(enumerate(to)))]
    ppermute x1, starting transfers between devices: 3 us -> 2.56 us  [local(): r1 = lax.ppermute(p1, 'seq', [(s, s ^ 1) for s in range(seq_count)])]
    ppermute x8 -> x7, starting transfers between devices: 11.7 us -> 12 us  [swap(): return lax.ppermute(sent, EVERY, list(enumerate(to)))]
  transfers between devices with their start and end apart: 12 -> 11, of which waited for: 5 -> 4; matrix products, arithmetic and copies ran while one was open for 0% -> 2% of each run, Pallas kernels for 8% -> 8%
where the time goes in v5:
time: 42.7 us; the launch traced here: 42.4 us
  starting transfers between devices  21.4 us (50%)
  waiting for transfers between devices  9.35 us (22%)
  Pallas kernels  9.21 us (22%)
  between operations  1.41 us (3%)
  other arithmetic  0.99 us (2%)
    ppermute x7, starting transfers between devices, swap(): return lax.ppermute(sent, EVERY, list(enumerate(to)))  12 us
    all_to_all x1, waiting for transfers between devices, local(): everyone = lax.all_to_all(piece, EVERY, 0, 0)  6.49 us
    all_to_all x1, starting transfers between devices, local(): everyone = lax.all_to_all(piece, EVERY, 0, 0)  4.9 us
    pallas_call x1, Pallas kernels, local(): call(first_kernel, [shape((n * rows, half), bf16) for n in (3, 3, 2, 2)]...  4.53 us
    ppermute x7, waiting for transfers between devices, swap(): return lax.ppermute(sent, EVERY, list(enumerate(to)))  2.86 us
    pallas_call x1, Pallas kernels, local(): call(attend_kernel, shape((devices, 4 * blocks, E // 2), PIECE), [VMEM] *...  2.67 us
    ppermute x1, starting transfers between devices, local(): r1 = lax.ppermute(p1, 'seq', [(s, s ^ 1) for s in range(seq_count)])  2.56 us
    pallas_call x1, Pallas kernels, local(): call(tail_kernel, [shape((own_caps, E), f32), shape((1, own_caps), f32)],...  1.48 us
  transfers between devices with their start and end apart: 11, of which 4 were waited for; matrix products, arithmetic and copies ran while one was open for 2% of the time, Pallas kernels for 8%

profile of v5, /device:TPU:0, one launch (start us, length us, event | category | flops | bytes accessed | tf_op | source)
XLA Modules:
  0.0 42.4 jit_solution(10543549128309088467)
XLA Ops:
  0.6 0.0 copy-start
  0.6 0.0 copy-start.1
  0.7 0.0 copy-start.2
  0.7 4.5 %shard_map.104 = (bf16[768,128]{1,0:T(8,128)(2,1)}, bf16[768,128]{1,0:T(8,128)(2,1)}, bf16[512,128]{1,0:T(8,128)(2,1)}, bf16[512,128]{1,0:T(8,128)(2,1)}, f32[144,128]{1,0:T(8,128)}, /*index=5*/bf16[144,128]{1,0:T(8,128)(2,1)}) custom-call(bf16[256,1024]{1,0:T(8,128)(2,1)} %frames_ref.1, f32[1,1024]{1,0:T(1,128)} %bitcast.4, bf16[3,1024,256]{2,1,0:T(8,128)(2,1)} %w_hbm.1, ...), custom_call_target="tpu_custom_call" | custom-call | flops 402653184 | bytes 1572864 | tf_op jit(solution)/shard_map/pallas_call | solution.py:295
  5.2 0.5 %collective-permute-start = (bf16[144,128]{1,0:T(8,128)(2,1)}, bf16[144,128]{1,0:T(8,128)(2,1)S(1)}, u32[]{:S(2)}, u32[]{:S(2)}) collective-permute-start(bf16[144,128]{1,0:T(8,128)(2,1)} %get-tuple-element.17), channel_id=1, source_target_pairs={{0,1},{1,0},{2,3},{3,2},{4,5},{5,4},{6,7},{7,6},{8,9},{9,8},{10,11... | collective-permute-start | bytes 110600 | tf_op jit(solution)/shard_map/ppermute | solution.py:329
  5.7 2.6 %collective-permute-start.2 = (bf16[768,128]{1,0:T(8,128)(2,1)}, bf16[768,128]{1,0:T(8,128)(2,1)S(1)}, u32[]{:S(2)}, u32[]{:S(2)}) collective-permute-start(bf16[768,128]{1,0:T(8,128)(2,1)} %get-tuple-element.18), channel_id=1, source_target_pairs={{0,4},{4,0},{8,12},{12,8},{16,20},{20,16},{24,28},{28,24},{1,5},{5... | collective-permute-start | bytes 589832 | tf_op jit(solution)/shard_map/ppermute | solution.py:311
  8.3 1.3 %collective-permute-start.4 = (bf16[512,128]{1,0:T(8,128)(2,1)}, bf16[512,128]{1,0:T(8,128)(2,1)S(1)}, u32[]{:S(2)}, u32[]{:S(2)}) collective-permute-start(bf16[512,128]{1,0:T(8,128)(2,1)} %get-tuple-element.22), channel_id=1, source_target_pairs={{4,12},{12,20},{20,28},{8,0},{16,8},{24,16},{5,13},{13,21},{21,29}... | collective-permute-start | bytes 393224 | tf_op jit(solution)/shard_map/ppermute | solution.py:317
  9.6 0.7 %collective-permute-start.5 = (bf16[512,128]{1,0:T(8,128)(2,1)}, bf16[512,128]{1,0:T(8,128)(2,1)S(1)}, u32[]{:S(2)}, u32[]{:S(2)}) collective-permute-start(bf16[512,128]{1,0:T(8,128)(2,1)} %get-tuple-element.23), channel_id=1, source_target_pairs={{4,8},{12,16},{20,24},{8,4},{16,12},{24,20},{5,9},{13,17},{21,25},... | collective-permute-start | bytes 393224 | tf_op jit(solution)/shard_map/ppermute | solution.py:312
  10.2 0.0 collective-permute-done
  10.3 0.9 %fusion = bf16[144,128]{1,0:T(8,128)(2,1)S(1)} fusion(f32[144,128]{1,0:T(8,128)} %get-tuple-element.16, bf16[144,128]{1,0:T(8,128)(2,1)S(1)} %collective-permute-done), kind=kLoop, calls=%fused_computation.4 | loop fusion | flops 55296 | bytes 147456 | tf_op jit(solution)/shard_map/convert_element_type | solution.py:334
  11.2 0.0 copy-start.4
  11.2 0.0 copy-start.3
  11.2 1.6 %collective-permute-start.1 = (bf16[144,128]{1,0:T(8,128)(2,1)S(1)}, bf16[144,128]{1,0:T(8,128)(2,1)S(1)}, u32[]{:S(2)}, u32[]{:S(2)}) collective-permute-start(bf16[144,128]{1,0:T(8,128)(2,1)S(1)} %fusion), channel_id=1, source_target_pairs={{0,2},{1,3},{2,0},{3,1},{4,6},{5,7},{6,4},{7,5},{8,10},{9,11},{10,... | collective-permute-start | bytes 110600 | tf_op jit(solution)/shard_map/ppermute | solution.py:329
  12.8 0.0 copy-done
  12.8 0.0 copy-done.1
  12.8 0.0 copy-done.2
  12.8 0.5 %shard_map.105 = (f32[128,512]{1,0:T(8,128)S(1)}, f32[2,512]{1,0:T(2,128)S(1)}) custom-call(bf16[256,1024]{1,0:T(8,128)(2,1)S(1)} %copy-done, bf16[256,1024]{1,0:T(8,128)(2,1)S(1)} %copy-done.2, bf16[1024,512]{1,0:T(8,128)(2,1)S(1)} %copy-done.1), custom_call_target="tpu_custom_call" | custom-call | flops 10000000000 | bytes 2097152 | tf_op jit(solution)/shard_map/pallas_call | solution.py:341
  13.3 1.9 %collective-permute-done.1 = bf16[144,128]{1,0:T(8,128)(2,1)S(1)} collective-permute-done((bf16[144,128]{1,0:T(8,128)(2,1)S(1)}, bf16[144,128]{1,0:T(8,128)(2,1)S(1)}, u32[]{:S(2)}, u32[]{:S(2)}) %collective-permute-start.1) | collective-permute-done | bytes 36896 | tf_op jit(solution)/shard_map/ppermute | solution.py:329
  15.2 0.0 collective-permute-done.2.r1_ref
  15.2 0.0 copy-done.4
  15.2 5.4 %collective-permute-start.3 = (bf16[144,128]{1,0:T(8,128)(2,1)S(1)}, bf16[144,128]{1,0:T(8,128)(2,1)S(1)}, u32[]{:S(2)}, u32[]{:S(2)}) collective-permute-start(bf16[144,128]{1,0:T(8,128)(2,1)S(1)} %fusion.2), channel_id=1, source_target_pairs={{0,4},{1,5},{2,6},{3,7},{4,0},{5,1},{6,2},{7,3},{8,12},{9,13},{10,... | collective-permute-start | bytes 110600 | tf_op jit(solution)/shard_map/ppermute | solution.py:329
  20.6 0.0 collective-permute-done.4.r2_ref
  20.6 0.0 collective-permute-done.5.r3_ref
  20.7 0.0 copy-done.3
  20.7 2.7 %shard_map.106 = bf16[32,8,256]{2,1,0:T(8,128)(2,1)} custom-call(bf16[768,128]{1,0:T(8,128)(2,1)S(1)} %copy-done.3, bf16[768,128]{1,0:T(8,128)(2,1)S(1)} %collective-permute-done.2.r1_ref, bf16[512,128]{1,0:T(8,128)(2,1)S(1)} %collective-permute-done.4.r2_ref, bf16[512,128]{1,0:T(8,128)(2,1)S(1)} %collective-permute-done.5.r3_ref, ...), custom_call_target="tpu_custom_call" | custom-call | flops 10000000000 | bytes 655360 | tf_op jit(solution)/shard_map/pallas_call | solution.py:348
  23.3 0.0 collective-permute-done.3
  23.4 1.6 %collective-permute-start.6 = (bf16[144,128]{1,0:T(8,128)(2,1)S(1)}, bf16[144,128]{1,0:T(8,128)(2,1)S(1)}, u32[]{:S(2)}, u32[]{:S(2)}) collective-permute-start(bf16[144,128]{1,0:T(8,128)(2,1)S(1)} %fusion.1), channel_id=1, source_target_pairs={{0,8},{1,9},{2,10},{3,11},{4,12},{5,13},{6,14},{7,15},{8,0},{9,1},... | collective-permute-start | bytes 110600 | tf_op jit(solution)/shard_map/ppermute | solution.py:329
  25.0 2.4 %collective-permute-start.7 = (bf16[144,128]{1,0:T(8,128)(2,1)S(1)}, bf16[144,128]{1,0:T(8,128)(2,1)S(1)}, u32[]{:S(2)}, u32[]{:S(2)}) collective-permute-start(bf16[144,128]{1,0:T(8,128)(2,1)S(1)} %fusion.1), channel_id=1, source_target_pairs={{0,16},{1,17},{2,18},{3,19},{4,20},{5,21},{6,22},{7,23},{8,24},{9,... | collective-permute-start | bytes 110600 | tf_op jit(solution)/shard_map/ppermute | solution.py:329
  27.4 0.4 %collective-permute-start.8 = (bf16[144,128]{1,0:T(8,128)(2,1)S(1)}, bf16[144,128]{1,0:T(8,128)(2,1)S(1)}, u32[]{:S(2)}, u32[]{:S(2)}) collective-permute-start(bf16[144,128]{1,0:T(8,128)(2,1)S(1)} %fusion.1), channel_id=1, source_target_pairs={{0,24},{1,25},{2,26},{3,27},{4,28},{5,29},{6,30},{7,31},{8,16},{9,... | collective-permute-start | bytes 110600 | tf_op jit(solution)/shard_map/ppermute | solution.py:329
  27.8 4.9 %all-to-all-start = ((bf16[32,8,256]{2,1,0:T(8,128)(2,1)}), bf16[32,8,256]{2,1,0:T(8,128)(2,1)S(1)}, u32[]{:S(2)}, u32[]{:S(2)}) async-start(bf16[32,8,256]{2,1,0:T(8,128)(2,1)} %shard_map.106), calls=%async_computation | async-start | bytes 262144 | tf_op jit(solution)/shard_map/all_to_all | solution.py:365
  32.7 0.0 collective-permute-done.6
  32.7 0.0 collective-permute-done.7
  32.7 0.4 collective-permute-done.8
  33.2 0.1 collective-permute-start.9
  33.9 0.6 %collective-permute-done.9.last_ref = bf16[144,128]{1,0:T(8,128)(2,1)S(1)} collective-permute-done((bf16[144,128]{1,0:T(8,128)(2,1)S(1)}, bf16[144,128]{1,0:T(8,128)(2,1)S(1)}, u32[]{:S(2)}, u32[]{:S(2)}) %collective-permute-start.9) | collective-permute-done | bytes 36896 | tf_op jit(solution)/shard_map/ppermute | solution.py:329
  34.5 6.5 %all-to-all-done.everyone_ref = bf16[32,8,256]{2,1,0:T(8,128)(2,1)S(1)} async-done(((bf16[32,8,256]{2,1,0:T(8,128)(2,1)}), bf16[32,8,256]{2,1,0:T(8,128)(2,1)S(1)}, u32[]{:S(2)}, u32[]{:S(2)}) %all-to-all-start) | async-done | bytes 131104 | tf_op jit(solution)/shard_map/all_to_all | solution.py:365
  40.9 1.5 %shard_map.107 = (f32[2,512]{1,0:T(2,128)}, f32[1,2]{1,0:T(1,128)}) custom-call(bf16[32,8,256]{2,1,0:T(8,128)(2,1)S(1)} %all-to-all-done.everyone_ref, f32[144,128]{1,0:T(8,128)S(1)} %get-tuple-element.31.mine_ref, bf16[144,128]{1,0:T(8,128)(2,1)S(1)} %collective-permute-done.9.last_ref, f32[1]{0:T(128)S(6)} %copy.11.divisor_ref), custom_call_target="tpu_custom_call" | custom-call | flops 8388608 | bytes 131072 | tf_op jit(solution)/shard_map/pallas_call | solution.py:368
  (3 shorter events, 0.1 us)
Async XLA Ops:
  0.6 12.1 %copy-start = (bf16[256,1024]{1,0:T(8,128)(2,1)S(1)}, bf16[256,1024]{1,0:T(8,128)(2,1)}, u32[]{:S(2)}) copy-start(bf16[256,1024]{1,0:T(8,128)(2,1)} %frames_ref.1) | copy-start | bytes 1572868
  0.6 12.1 %copy-start.1 = (bf16[1024,512]{1,0:T(8,128)(2,1)S(1)}, bf16[1024,512]{1,0:T(8,128)(2,1)}, u32[]{:S(2)}) copy-start(bf16[1024,512]{1,0:T(8,128)(2,1)} %w_proj_ref.1) | copy-start | bytes 3145732
  0.7 12.1 %copy-start.2 = (bf16[256,1024]{1,0:T(8,128)(2,1)S(1)}, bf16[256,1024]{1,0:T(8,128)(2,1)}, u32[]{:S(2)}) copy-start(bf16[256,1024]{1,0:T(8,128)(2,1)} %w_out_ref.1) | copy-start | bytes 1572868
  5.2 5.1 %collective-permute-start = (bf16[144,128]{1,0:T(8,128)(2,1)}, bf16[144,128]{1,0:T(8,128)(2,1)S(1)}, u32[]{:S(2)}, u32[]{:S(2)}) collective-permute-start(bf16[144,128]{1,0:T(8,128)(2,1)} %get-tuple-element.17), channel_id=1, source_target_pairs={{0,1},{1,0},{2,3},{3,2},{4,5},{5,4},{6,7},{7,6},{8,9},{9,8},{10,11... | collective-permute-start | bytes 110600 | tf_op jit(solution)/shard_map/ppermute | solution.py:329
  5.7 9.5 %collective-permute-start.2 = (bf16[768,128]{1,0:T(8,128)(2,1)}, bf16[768,128]{1,0:T(8,128)(2,1)S(1)}, u32[]{:S(2)}, u32[]{:S(2)}) collective-permute-start(bf16[768,128]{1,0:T(8,128)(2,1)} %get-tuple-element.18), channel_id=1, source_target_pairs={{0,4},{4,0},{8,12},{12,8},{16,20},{20,16},{24,28},{28,24},{1,5},{5... | collective-permute-start | bytes 589832 | tf_op jit(solution)/shard_map/ppermute | solution.py:311
  8.3 12.4 %collective-permute-start.4 = (bf16[512,128]{1,0:T(8,128)(2,1)}, bf16[512,128]{1,0:T(8,128)(2,1)S(1)}, u32[]{:S(2)}, u32[]{:S(2)}) collective-permute-start(bf16[512,128]{1,0:T(8,128)(2,1)} %get-tuple-element.22), channel_id=1, source_target_pairs={{4,12},{12,20},{20,28},{8,0},{16,8},{24,16},{5,13},{13,21},{21,29}... | collective-permute-start | bytes 393224 | tf_op jit(solution)/shard_map/ppermute | solution.py:317
  9.6 11.1 %collective-permute-start.5 = (bf16[512,128]{1,0:T(8,128)(2,1)}, bf16[512,128]{1,0:T(8,128)(2,1)S(1)}, u32[]{:S(2)}, u32[]{:S(2)}) collective-permute-start(bf16[512,128]{1,0:T(8,128)(2,1)} %get-tuple-element.23), channel_id=1, source_target_pairs={{4,8},{12,16},{20,24},{8,4},{16,12},{24,20},{5,9},{13,17},{21,25},... | collective-permute-start | bytes 393224 | tf_op jit(solution)/shard_map/ppermute | solution.py:312
  11.2 4.0 %copy-start.4 = (f32[144,128]{1,0:T(8,128)S(1)}, f32[144,128]{1,0:T(8,128)}, u32[]{:S(2)}) copy-start(f32[144,128]{1,0:T(8,128)} %get-tuple-element.16) | copy-start | bytes 221188
  11.2 9.5 %copy-start.3 = (bf16[768,128]{1,0:T(8,128)(2,1)S(1)}, bf16[768,128]{1,0:T(8,128)(2,1)}, u32[]{:S(2)}) copy-start(bf16[768,128]{1,0:T(8,128)(2,1)} %get-tuple-element.20.own_ref) | copy-start | bytes 589828
  11.2 4.0 %collective-permute-start.1 = (bf16[144,128]{1,0:T(8,128)(2,1)S(1)}, bf16[144,128]{1,0:T(8,128)(2,1)S(1)}, u32[]{:S(2)}, u32[]{:S(2)}) collective-permute-start(bf16[144,128]{1,0:T(8,128)(2,1)S(1)} %fusion), channel_id=1, source_target_pairs={{0,2},{1,3},{2,0},{3,1},{4,6},{5,7},{6,4},{7,5},{8,10},{9,11},{10,... | collective-permute-start | bytes 110600 | tf_op jit(solution)/shard_map/ppermute | solution.py:329
  15.2 8.1 %collective-permute-start.3 = (bf16[144,128]{1,0:T(8,128)(2,1)S(1)}, bf16[144,128]{1,0:T(8,128)(2,1)S(1)}, u32[]{:S(2)}, u32[]{:S(2)}) collective-permute-start(bf16[144,128]{1,0:T(8,128)(2,1)S(1)} %fusion.2), channel_id=1, source_target_pairs={{0,4},{1,5},{2,6},{3,7},{4,0},{5,1},{6,2},{7,3},{8,12},{9,13},{10,... | collective-permute-start | bytes 110600 | tf_op jit(solution)/shard_map/ppermute | solution.py:329
  23.4 9.4 %collective-permute-start.6 = (bf16[144,128]{1,0:T(8,128)(2,1)S(1)}, bf16[144,128]{1,0:T(8,128)(2,1)S(1)}, u32[]{:S(2)}, u32[]{:S(2)}) collective-permute-start(bf16[144,128]{1,0:T(8,128)(2,1)S(1)} %fusion.1), channel_id=1, source_target_pairs={{0,8},{1,9},{2,10},{3,11},{4,12},{5,13},{6,14},{7,15},{8,0},{9,1},... | collective-permute-start | bytes 110600 | tf_op jit(solution)/shard_map/ppermute | solution.py:329
  25.0 7.7 %collective-permute-start.7 = (bf16[144,128]{1,0:T(8,128)(2,1)S(1)}, bf16[144,128]{1,0:T(8,128)(2,1)S(1)}, u32[]{:S(2)}, u32[]{:S(2)}) collective-permute-start(bf16[144,128]{1,0:T(8,128)(2,1)S(1)} %fusion.1), channel_id=1, source_target_pairs={{0,16},{1,17},{2,18},{3,19},{4,20},{5,21},{6,22},{7,23},{8,24},{9,... | collective-permute-start | bytes 110600 | tf_op jit(solution)/shard_map/ppermute | solution.py:329
  27.4 5.8 %collective-permute-start.8 = (bf16[144,128]{1,0:T(8,128)(2,1)S(1)}, bf16[144,128]{1,0:T(8,128)(2,1)S(1)}, u32[]{:S(2)}, u32[]{:S(2)}) collective-permute-start(bf16[144,128]{1,0:T(8,128)(2,1)S(1)} %fusion.1), channel_id=1, source_target_pairs={{0,24},{1,25},{2,26},{3,27},{4,28},{5,29},{6,30},{7,31},{8,16},{9,... | collective-permute-start | bytes 110600 | tf_op jit(solution)/shard_map/ppermute | solution.py:329
  27.8 13.1 %all-to-all-start = ((bf16[32,8,256]{2,1,0:T(8,128)(2,1)}), bf16[32,8,256]{2,1,0:T(8,128)(2,1)S(1)}, u32[]{:S(2)}, u32[]{:S(2)}) async-start(bf16[32,8,256]{2,1,0:T(8,128)(2,1)} %shard_map.106), calls=%async_computation | async-start | bytes 262144 | tf_op jit(solution)/shard_map/all_to_all | solution.py:365
  33.2 1.3 %collective-permute-start.9 = (bf16[144,128]{1,0:T(8,128)(2,1)S(1)}, bf16[144,128]{1,0:T(8,128)(2,1)S(1)}, u32[]{:S(2)}, u32[]{:S(2)}) collective-permute-start(bf16[144,128]{1,0:T(8,128)(2,1)S(1)} %get-tuple-element.30), channel_id=1, source_target_pairs={{0,1},{1,0},{2,3},{3,2},{4,5},{5,4},{6,7},{7,6},{8,9},{9,8},{10,11... | collective-permute-start | bytes 110600 | tf_op jit(solution)/shard_map/ppermute | solution.py:329

commit v6 on v5

--- a/solution.py
+++ b/solution.py
@@ -22,7 +22,7 @@
 HIGHEST = lax.Precision.HIGHEST
 
 
-def call(body, outs, ins, scratch=(), cost=(0, 0, 0), mib=16):
+def call(body, outs, ins, scratch=(), cost=(0, 0, 0), mib=24):
     return pl.pallas_call(
         body,
         out_shape=outs,
@@ -44,11 +44,11 @@
 
 def first_kernel(
     frames_hbm,
-    gain_ref,
+    gain_hbm,
     w_hbm,
-    ids_ref,
+    ids_hbm,
     table_hbm,
-    bounds_ref,
+    bounds_hbm,
     own_ref,
     p1_ref,
     p2_ref,
@@ -56,41 +56,45 @@
     t32_ref,
     t16_ref,
     frames,
+    gain,
     w,
+    id_rows,
     table,
+    bound,
     normed,
     sems,
 ):
     rows = frames.shape[0]
     half = own_ref.shape[1]
-    copies = [
-        pltpu.make_async_copy(frames_hbm, frames, sems.at[0]),
-        *[pltpu.make_async_copy(w_hbm.at[k], w.at[k], sems.at[1 + k]) for k in range(3)],
-        pltpu.make_async_copy(table_hbm, table, sems.at[4]),
-    ]
-    for k in (0, 2, 3, 1, 4):
-        copies[k].start()
+    parts = [(ids_hbm, id_rows), (frames_hbm, frames), (gain_hbm, gain)]
+    parts += [(w_hbm.at[k], w.at[k]) for k in (1, 2, 0)]
+    parts += [(table_hbm, table), (bounds_hbm, bound)]
+    copies = [pltpu.make_async_copy(*part, sems.at[n]) for n, part in enumerate(parts)]
+    for copy in copies:
+        copy.start()
     odd = lax.axis_index("seq") % 2 == 1
 
-    tokens, caps = ids_ref.shape
+    tokens, caps = id_rows.shape
     vocab = table.shape[0]
-    own_caps = bounds_ref.shape[0]
+    own_caps = bound.shape[0]
     slot = lax.axis_index("seq") * lax.axis_size("head") + lax.axis_index("head")
-    ids = (ids_ref[...] - slot * vocab).T
+    copies[0].wait()
+    ids = (id_rows[...] - slot * vocab).T
     words = lax.broadcasted_iota(jnp.int32, (caps, vocab), 1)
     counts = jnp.zeros((caps, vocab), jnp.float32)
     for t in range(tokens):
         counts = counts + jnp.where(ids[:, t : t + 1] == words, 1.0, 0.0)
     counts = counts.astype(jnp.bfloat16)
 
-    copies[0].wait()
+    copies[1].wait()
+    copies[2].wait()
     step = min(64, rows)
     for r in range(0, rows, step):
         part = frames[r : r + step].astype(jnp.float32)
         scale = lax.rsqrt(jnp.mean(part * part, axis=-1, keepdims=True) + 1e-05)
-        normed[r : r + step] = (part * scale * gain_ref[...]).astype(jnp.bfloat16)
-    for k in (1, 2, 0):
-        copies[1 + k].wait()
+        normed[r : r + step] = (part * scale * gain[...]).astype(jnp.bfloat16)
+    for n, k in enumerate((1, 2, 0)):
+        copies[3 + n].wait()
         both = jnp.dot(normed[...], w[k], preferred_element_type=jnp.float32).astype(jnp.bfloat16)
         if k == 0:
             both = both * jnp.bfloat16(HDIM ** (-0.5))
@@ -102,26 +106,23 @@
             p2_ref[(k - 1) * rows : k * rows] = mine
             p3_ref[(k - 1) * rows : k * rows] = other
 
-    copies[4].wait()
+    copies[6].wait()
+    copies[7].wait()
     part = jnp.dot(counts, table[...], preferred_element_type=jnp.float32)
     row = lax.broadcasted_iota(jnp.int32, (BOUND_ROWS, LANES), 0)
     place = row * LANES + lax.broadcasted_iota(jnp.int32, (BOUND_ROWS, LANES), 1)
     bounds = jnp.zeros((BOUND_ROWS, LANES), jnp.float32)
     for c in range(own_caps):
         for side in range(2):
-            block = (bounds_ref[c, side] // BLK).astype(jnp.float32)
+            block = (bound[c, side] // BLK).astype(jnp.float32)
             bounds = jnp.where(place == side * caps + slot * own_caps + c, block, bounds)
-    late = lax.axis_index("head") % 2 == 1
-    few = caps // 2
+    sums = E // LANES * caps
     for c in range(E // LANES):
-        early_half = part[:few, c * LANES : (c + 1) * LANES]
-        late_half = part[few:, c * LANES : (c + 1) * LANES]
-        t32_ref[c * few : (c + 1) * few] = jnp.where(late, late_half, early_half)
-        t16_ref[c * few : (c + 1) * few] = jnp.where(late, early_half, late_half).astype(
-            jnp.bfloat16
-        )
-    t32_ref[E // LANES * few :] = bounds
-    t16_ref[E // LANES * few :] = bounds.astype(jnp.bfloat16)
+        chunk = part[:, c * LANES : (c + 1) * LANES]
+        t32_ref[c * caps : (c + 1) * caps] = chunk
+        t16_ref[c * caps : (c + 1) * caps] = chunk.astype(jnp.bfloat16)
+    t32_ref[sums:] = bounds
+    t16_ref[sums:] = bounds.astype(jnp.bfloat16)
 
 
 def weights_kernel(frames_ref, w_out_ref, w_proj_ref, wc_ref, fp_ref):
@@ -200,29 +201,23 @@
 def tail_kernel(everyone_ref, mine_ref, last_ref, divisor_ref, derivative_ref, loss_ref):
     own_caps = derivative_ref.shape[0]
     devices, width, half = everyone_ref.shape
-    few = (mine_ref.shape[0] - BOUND_ROWS) // (E // LANES)
-    caps = 2 * few
+    caps = (mine_ref.shape[0] - BOUND_ROWS) // (E // LANES)
+    sums = E // LANES * caps
     group = 2 * lax.axis_size("head")
     pairs = devices // group
     blocks = width // 2
-    head = lax.axis_index("head")
-    slot = lax.axis_index("seq") * lax.axis_size("head") + head
+    slot = lax.axis_index("seq") * lax.axis_size("head") + lax.axis_index("head")
     divisor = divisor_ref[0]
 
-    def rows_of(ref):
-        chunks = [ref[c * few : (c + 1) * few] for c in range(E // LANES)]
-        return jnp.concatenate(chunks, axis=1).astype(jnp.float32)
-
-    mine, other = rows_of(mine_ref), rows_of(last_ref)
-    late = head % 2 == 1
-    raw = jnp.concatenate([jnp.where(late, other, mine), jnp.where(late, mine, other)], axis=0)
+    total = mine_ref[...] + last_ref[...].astype(jnp.float32)
+    raw = jnp.concatenate([total[c * caps : (c + 1) * caps] for c in range(E // LANES)], axis=1)
 
     def column(side):
         found = jnp.zeros((caps, LANES), jnp.float32)
         at = lax.broadcasted_iota(jnp.int32, (caps, LANES), 0) + side * caps
         lane = lax.broadcasted_iota(jnp.int32, (caps, LANES), 1)
         for r in range(-(-2 * caps // LANES)):
-            line = mine_ref[E // LANES * few + r : E // LANES * few + r + 1]
+            line = total[sums + r : sums + r + 1]
             found = found + jnp.where(at == lane + r * LANES, line, 0.0)
         return jnp.sum(found, axis=1, keepdims=True)
 
@@ -291,22 +286,20 @@
     shape = jax.ShapeDtypeStruct
     bf16, f32 = jnp.bfloat16, jnp.float32
 
-    tall = E // LANES * token_ids.shape[0] // 2 + BOUND_ROWS
+    tall = E // LANES * token_ids.shape[0] + BOUND_ROWS
+    given = (frames, norm_gain[None], w_qkv, token_ids.T, text_table, span_bounds)
     own, p1, p2, p3, mine, sent = call(
         first_kernel,
         [shape((n * rows, half), bf16) for n in (3, 3, 2, 2)]
         + [shape((tall, LANES), f32), shape((tall, LANES), bf16)],
-        [HBM, VMEM, HBM, VMEM, HBM, SMEM],
+        [HBM] * len(given),
         [
-            pltpu.VMEM(frames.shape, bf16),
-            pltpu.VMEM(w_qkv.shape, bf16),
-            pltpu.VMEM(text_table.shape, bf16),
-            pltpu.VMEM(frames.shape, bf16),
-            pltpu.SemaphoreType.DMA((5,)),
-        ],
+            pltpu.SMEM(a.shape, a.dtype) if a is span_bounds else pltpu.VMEM(a.shape, a.dtype)
+            for a in given
+        ]
+        + [pltpu.VMEM(frames.shape, bf16), pltpu.SemaphoreType.DMA((8,))],
         (6 * rows * width * cols, 2 * w_qkv.size, 0),
-        60,
-    )(frames, norm_gain[None], w_qkv, token_ids.T, text_table, span_bounds)
+    )(*[pltpu.with_memory_space_constraint(a, pltpu.HBM) for a in given])
     ends = seq_count - 1
     r1 = lax.ppermute(p1, "seq", [(s, s ^ 1) for s in range(seq_count)])
     r3 = lax.ppermute(
@@ -333,7 +326,6 @@
             mine = mine + g.astype(f32)
         return mine, mine.astype(bf16)
 
-    mine, sent = add(mine, swap(sent, 0, 1))
     got, r1 = lax.optimization_barrier((swap(sent, 0, 2), r1))
     mine, sent = add(mine, got)
     got = swap(sent, 1, 0)

time: 42.7 us -> 40 us (0.937)
  waiting for transfers between devices: 9.35 us -> 8.27 us
  Pallas kernels: 9.21 us -> 8.18 us
  other arithmetic: 0.99 us -> 0.11 us
    all_to_all x1, waiting for transfers between devices: 6.49 us -> 4.93 us  [local(): everyone = lax.all_to_all(piece, EVERY, 0, 0)]
    pallas_call x1, Pallas kernels: 4.53 us -> 3.49 us  [local(): call(first_kernel, [shape((n * rows, half), bf16) for n in (3, 3, 2, 2)]...]
    convert_element_type x4 -> x3, other arithmetic: 0.99 us -> 0.11 us  [add(): return (mine, mine.astype(bf16))]
    all_to_all x1, starting transfers between devices: 4.9 us -> 4.19 us  [local(): everyone = lax.all_to_all(piece, EVERY, 0, 0)]
    ppermute x7 -> x6, starting transfers between devices: 12 us -> 12.6 us  [swap(): return lax.ppermute(sent, EVERY, list(enumerate(to)))]
    ppermute x1, waiting for transfers between devices: 0.01 us -> 0.59 us  [local(): r1 = lax.ppermute(p1, 'seq', [(s, s ^ 1) for s in range(seq_count)])]
    ppermute x1, starting transfers between devices: 2.56 us -> 3 us  [local(): r1 = lax.ppermute(p1, 'seq', [(s, s ^ 1) for s in range(seq_count)])]
    ppermute x7 -> x6, waiting for transfers between devices: 2.86 us -> 2.75 us  [swap(): return lax.ppermute(sent, EVERY, list(enumerate(to)))]
  transfers between devices with their start and end apart: 11 -> 10, of which waited for: 4 -> 5; matrix products, arithmetic and copies ran while one was open for 2% -> 0% of each run, Pallas kernels for 8% -> 8%
where the time goes in v6:
time: 40 us; the launch traced here: 39.8 us
  starting transfers between devices  21.8 us (54%)
  waiting for transfers between devices  8.27 us (21%)
  Pallas kernels  8.18 us (20%)
  between operations  1.4 us (4%)
    ppermute x6, starting transfers between devices, swap(): return lax.ppermute(sent, EVERY, list(enumerate(to)))  12.6 us
    all_to_all x1, waiting for transfers between devices, local(): everyone = lax.all_to_all(piece, EVERY, 0, 0)  4.93 us
    all_to_all x1, starting transfers between devices, local(): everyone = lax.all_to_all(piece, EVERY, 0, 0)  4.19 us
    pallas_call x1, Pallas kernels, local(): call(first_kernel, [shape((n * rows, half), bf16) for n in (3, 3, 2, 2)]...  3.49 us
    ppermute x1, starting transfers between devices, local(): r1 = lax.ppermute(p1, 'seq', [(s, s ^ 1) for s in range(seq_count)])  3 us
    ppermute x6, waiting for transfers between devices, swap(): return lax.ppermute(sent, EVERY, list(enumerate(to)))  2.75 us
    pallas_call x1, Pallas kernels, local(): call(attend_kernel, shape((devices, 4 * blocks, E // 2), PIECE), [VMEM] *...  2.66 us
    pallas_call x1, Pallas kernels, local(): call(tail_kernel, [shape((own_caps, E), f32), shape((1, own_caps), f32)],...  1.49 us
  transfers between devices with their start and end apart: 10, of which 5 were waited for; matrix products, arithmetic and copies ran while one was open for 0% of the time, Pallas kernels for 8%

profile of v6, /device:TPU:0, one launch (start us, length us, event | category | flops | bytes accessed | tf_op | source)
XLA Modules:
  0.0 39.8 jit_solution(13535137342572140982)
XLA Ops:
  0.6 0.0 copy-start
  0.6 0.0 copy-start.1
  0.7 0.0 copy-start.2
  0.7 3.5 %shard_map.104 = (bf16[768,128]{1,0:T(8,128)(2,1)S(1)}, bf16[768,128]{1,0:T(8,128)(2,1)S(1)}, bf16[512,128]{1,0:T(8,128)(2,1)S(1)}, bf16[512,128]{1,0:T(8,128)(2...) custom-call(bf16[256,1024]{1,0:T(8,128)(2,1)} %frames_ref.1, f32[1,1024]{1,0:T(1,128)} %bitcast.4, ...), custom_call_target="tpu_custom_call" | custom-call | flops 402653184 | bytes 1572864 | tf_op jit(solution)/shard_map/pallas_call | solution.py:291
  4.2 3.0 %collective-permute-start.1 = (bf16[768,128]{1,0:T(8,128)(2,1)S(1)}, bf16[768,128]{1,0:T(8,128)(2,1)S(1)}, u32[]{:S(2)}, u32[]{:S(2)}) collective-permute-start(bf16[768,128]{1,0:T(8,128)(2,1)S(1)} %get-tuple-element.18), channel_id=1, source_target_pairs={{0,4},{4,0},{8,12},{12,8},{16,20},{20,16},{24,28},{28,24},{1,5},{5... | collective-permute-start | bytes 589832 | tf_op jit(solution)/shard_map/ppermute | solution.py:304
  7.2 1.5 %collective-permute-start = (bf16[272,128]{1,0:T(8,128)(2,1)S(1)}, bf16[272,128]{1,0:T(8,128)(2,1)S(1)}, u32[]{:S(2)}, u32[]{:S(2)}) collective-permute-start(bf16[272,128]{1,0:T(8,128)(2,1)S(1)} %get-tuple-element.17), channel_id=1, source_target_pairs={{0,2},{1,3},{2,0},{3,1},{4,6},{5,7},{6,4},{7,5},{8,10},{9,11},{10,... | collective-permute-start | bytes 208904 | tf_op jit(solution)/shard_map/ppermute | solution.py:322
  8.7 1.3 %collective-permute-start.3 = (bf16[512,128]{1,0:T(8,128)(2,1)S(1)}, bf16[512,128]{1,0:T(8,128)(2,1)S(1)}, u32[]{:S(2)}, u32[]{:S(2)}) collective-permute-start(bf16[512,128]{1,0:T(8,128)(2,1)S(1)} %get-tuple-element.22), channel_id=1, source_target_pairs={{4,12},{12,20},{20,28},{8,0},{16,8},{24,16},{5,13},{13,21},{21,29}... | collective-permute-start | bytes 393224 | tf_op jit(solution)/shard_map/ppermute | solution.py:310
  10.0 0.7 %collective-permute-start.4 = (bf16[512,128]{1,0:T(8,128)(2,1)S(1)}, bf16[512,128]{1,0:T(8,128)(2,1)S(1)}, u32[]{:S(2)}, u32[]{:S(2)}) collective-permute-start(bf16[512,128]{1,0:T(8,128)(2,1)S(1)} %get-tuple-element.23), channel_id=1, source_target_pairs={{4,8},{12,16},{20,24},{8,4},{16,12},{24,20},{5,9},{13,17},{21,25},... | collective-permute-start | bytes 393224 | tf_op jit(solution)/shard_map/ppermute | solution.py:305
  10.6 0.0 copy-done
  10.7 0.0 copy-done.1
  10.7 0.0 copy-done.2
  10.7 0.5 %shard_map.105 = (f32[128,512]{1,0:T(8,128)S(1)}, f32[2,512]{1,0:T(2,128)S(1)}) custom-call(bf16[256,1024]{1,0:T(8,128)(2,1)S(1)} %copy-done, bf16[256,1024]{1,0:T(8,128)(2,1)S(1)} %copy-done.2, bf16[1024,512]{1,0:T(8,128)(2,1)S(1)} %copy-done.1), custom_call_target="tpu_custom_call" | custom-call | flops 10000000000 | bytes 2097152 | tf_op jit(solution)/shard_map/pallas_call | solution.py:333
  11.2 0.3 collective-permute-done
  11.5 0.6 %collective-permute-done.1.r1_ref = bf16[768,128]{1,0:T(8,128)(2,1)S(1)} collective-permute-done((bf16[768,128]{1,0:T(8,128)(2,1)S(1)}, bf16[768,128]{1,0:T(8,128)(2,1)S(1)}, u32[]{:S(2)}, u32[]{:S(2)}) %collective-permute-start.1) | collective-permute-done | bytes 196640 | tf_op jit(solution)/shard_map/ppermute | solution.py:304
  12.1 4.6 %collective-permute-start.2 = (bf16[272,128]{1,0:T(8,128)(2,1)S(1)}, bf16[272,128]{1,0:T(8,128)(2,1)S(1)}, u32[]{:S(2)}, u32[]{:S(2)}) collective-permute-start(bf16[272,128]{1,0:T(8,128)(2,1)S(1)} %fusion), channel_id=1, source_target_pairs={{0,4},{1,5},{2,6},{3,7},{4,0},{5,1},{6,2},{7,3},{8,12},{9,13},{10,... | collective-permute-start | bytes 208904 | tf_op jit(solution)/shard_map/ppermute | solution.py:322
  16.7 0.0 collective-permute-done.3.r2_ref
  16.7 0.0 collective-permute-done.4.r3_ref
  16.7 2.7 %shard_map.106 = bf16[32,8,256]{2,1,0:T(8,128)(2,1)} custom-call(bf16[768,128]{1,0:T(8,128)(2,1)S(1)} %get-tuple-element.20.own_ref, bf16[768,128]{1,0:T(8,128)(2,1)S(1)} %collective-permute-done.1.r1_ref, bf16[512,128]{1,0:T(8,128)(2,1)S(1)} %collective-permute-done.3.r2_ref, bf16[512,128]{1,0:T(8,128)(2,1)S(1)} %collective-permute-done.4.r3_ref, ...), custom_call_target="tpu_custom_call" | custom-call | flops 10000000000 | bytes 655360 | tf_op jit(solution)/shard_map/pallas_call | solution.py:340
  19.3 0.0 collective-permute-done.2
  19.4 3.8 %collective-permute-start.5 = (bf16[272,128]{1,0:T(8,128)(2,1)S(1)}, bf16[272,128]{1,0:T(8,128)(2,1)S(1)}, u32[]{:S(2)}, u32[]{:S(2)}) collective-permute-start(bf16[272,128]{1,0:T(8,128)(2,1)S(1)} %fusion.1), channel_id=1, source_target_pairs={{0,8},{1,9},{2,10},{3,11},{4,12},{5,13},{6,14},{7,15},{8,0},{9,1},... | collective-permute-start | bytes 208904 | tf_op jit(solution)/shard_map/ppermute | solution.py:322
  23.2 2.6 %collective-permute-start.6 = (bf16[272,128]{1,0:T(8,128)(2,1)S(1)}, bf16[272,128]{1,0:T(8,128)(2,1)S(1)}, u32[]{:S(2)}, u32[]{:S(2)}) collective-permute-start(bf16[272,128]{1,0:T(8,128)(2,1)S(1)} %fusion.1), channel_id=1, source_target_pairs={{0,16},{1,17},{2,18},{3,19},{4,20},{5,21},{6,22},{7,23},{8,24},{9,... | collective-permute-start | bytes 208904 | tf_op jit(solution)/shard_map/ppermute | solution.py:322
  25.8 0.0 collective-permute-start.7
  25.8 4.2 %all-to-all-start = ((bf16[32,8,256]{2,1,0:T(8,128)(2,1)}), bf16[32,8,256]{2,1,0:T(8,128)(2,1)S(1)}, u32[]{:S(2)}, u32[]{:S(2)}) async-start(bf16[32,8,256]{2,1,0:T(8,128)(2,1)} %shard_map.106), calls=%async_computation | async-start | bytes 262144 | tf_op jit(solution)/shard_map/all_to_all | solution.py:357
  30.0 0.0 collective-permute-done.5
  30.1 0.0 collective-permute-done.6
  30.1 1.9 %collective-permute-done.7 = bf16[272,128]{1,0:T(8,128)(2,1)S(1)} collective-permute-done((bf16[272,128]{1,0:T(8,128)(2,1)S(1)}, bf16[272,128]{1,0:T(8,128)(2,1)S(1)}, u32[]{:S(2)}, u32[]{:S(2)}) %collective-permute-start.7) | collective-permute-done | bytes 69664 | tf_op jit(solution)/shard_map/ppermute | solution.py:322
  32.0 0.1 fusion.2
  32.0 0.1 collective-permute-start.8
  32.7 0.6 %collective-permute-done.8.last_ref = bf16[272,128]{1,0:T(8,128)(2,1)S(1)} collective-permute-done((bf16[272,128]{1,0:T(8,128)(2,1)S(1)}, bf16[272,128]{1,0:T(8,128)(2,1)S(1)}, u32[]{:S(2)}, u32[]{:S(2)}) %collective-permute-start.8) | collective-permute-done | bytes 69664 | tf_op jit(solution)/shard_map/ppermute | solution.py:322
  33.3 4.9 %all-to-all-done.everyone_ref = bf16[32,8,256]{2,1,0:T(8,128)(2,1)S(1)} async-done(((bf16[32,8,256]{2,1,0:T(8,128)(2,1)}), bf16[32,8,256]{2,1,0:T(8,128)(2,1)S(1)}, u32[]{:S(2)}, u32[]{:S(2)}) %all-to-all-start) | async-done | bytes 131104 | tf_op jit(solution)/shard_map/all_to_all | solution.py:357
  38.3 1.5 %shard_map.107 = (f32[2,512]{1,0:T(2,128)}, f32[1,2]{1,0:T(1,128)}) custom-call(bf16[32,8,256]{2,1,0:T(8,128)(2,1)S(1)} %all-to-all-done.everyone_ref, f32[272,128]{1,0:T(8,128)S(1)} %get-tuple-element.31.mine_ref, bf16[272,128]{1,0:T(8,128)(2,1)S(1)} %collective-permute-done.8.last_ref, f32[1]{0:T(128)S(6)} %copy.11.divisor_ref), custom_call_target="tpu_custom_call" | custom-call | flops 8388608 | bytes 131072 | tf_op jit(solution)/shard_map/pallas_call | solution.py:360
  (2 shorter events, 0.0 us)
Async XLA Ops:
  0.6 10.0 %copy-start = (bf16[256,1024]{1,0:T(8,128)(2,1)S(1)}, bf16[256,1024]{1,0:T(8,128)(2,1)}, u32[]{:S(2)}) copy-start(bf16[256,1024]{1,0:T(8,128)(2,1)} %frames_ref.1) | copy-start | bytes 1572868
  0.6 10.0 %copy-start.1 = (bf16[1024,512]{1,0:T(8,128)(2,1)S(1)}, bf16[1024,512]{1,0:T(8,128)(2,1)}, u32[]{:S(2)}) copy-start(bf16[1024,512]{1,0:T(8,128)(2,1)} %w_proj_ref.1) | copy-start | bytes 3145732
  0.7 10.0 %copy-start.2 = (bf16[256,1024]{1,0:T(8,128)(2,1)S(1)}, bf16[256,1024]{1,0:T(8,128)(2,1)}, u32[]{:S(2)}) copy-start(bf16[256,1024]{1,0:T(8,128)(2,1)} %w_out_ref.1) | copy-start | bytes 1572868
  4.2 7.9 %collective-permute-start.1 = (bf16[768,128]{1,0:T(8,128)(2,1)S(1)}, bf16[768,128]{1,0:T(8,128)(2,1)S(1)}, u32[]{:S(2)}, u32[]{:S(2)}) collective-permute-start(bf16[768,128]{1,0:T(8,128)(2,1)S(1)} %get-tuple-element.18), channel_id=1, source_target_pairs={{0,4},{4,0},{8,12},{12,8},{16,20},{20,16},{24,28},{28,24},{1,5},{5... | collective-permute-start | bytes 589832 | tf_op jit(solution)/shard_map/ppermute | solution.py:304
  7.2 4.3 %collective-permute-start = (bf16[272,128]{1,0:T(8,128)(2,1)S(1)}, bf16[272,128]{1,0:T(8,128)(2,1)S(1)}, u32[]{:S(2)}, u32[]{:S(2)}) collective-permute-start(bf16[272,128]{1,0:T(8,128)(2,1)S(1)} %get-tuple-element.17), channel_id=1, source_target_pairs={{0,2},{1,3},{2,0},{3,1},{4,6},{5,7},{6,4},{7,5},{8,10},{9,11},{10,... | collective-permute-start | bytes 208904 | tf_op jit(solution)/shard_map/ppermute | solution.py:322
  8.7 8.0 %collective-permute-start.3 = (bf16[512,128]{1,0:T(8,128)(2,1)S(1)}, bf16[512,128]{1,0:T(8,128)(2,1)S(1)}, u32[]{:S(2)}, u32[]{:S(2)}) collective-permute-start(bf16[512,128]{1,0:T(8,128)(2,1)S(1)} %get-tuple-element.22), channel_id=1, source_target_pairs={{4,12},{12,20},{20,28},{8,0},{16,8},{24,16},{5,13},{13,21},{21,29}... | collective-permute-start | bytes 393224 | tf_op jit(solution)/shard_map/ppermute | solution.py:310
  10.0 6.7 %collective-permute-start.4 = (bf16[512,128]{1,0:T(8,128)(2,1)S(1)}, bf16[512,128]{1,0:T(8,128)(2,1)S(1)}, u32[]{:S(2)}, u32[]{:S(2)}) collective-permute-start(bf16[512,128]{1,0:T(8,128)(2,1)S(1)} %get-tuple-element.23), channel_id=1, source_target_pairs={{4,8},{12,16},{20,24},{8,4},{16,12},{24,20},{5,9},{13,17},{21,25},... | collective-permute-start | bytes 393224 | tf_op jit(solution)/shard_map/ppermute | solution.py:305
  12.1 7.2 %collective-permute-start.2 = (bf16[272,128]{1,0:T(8,128)(2,1)S(1)}, bf16[272,128]{1,0:T(8,128)(2,1)S(1)}, u32[]{:S(2)}, u32[]{:S(2)}) collective-permute-start(bf16[272,128]{1,0:T(8,128)(2,1)S(1)} %fusion), channel_id=1, source_target_pairs={{0,4},{1,5},{2,6},{3,7},{4,0},{5,1},{6,2},{7,3},{8,12},{9,13},{10,... | collective-permute-start | bytes 208904 | tf_op jit(solution)/shard_map/ppermute | solution.py:322
  19.4 10.7 %collective-permute-start.5 = (bf16[272,128]{1,0:T(8,128)(2,1)S(1)}, bf16[272,128]{1,0:T(8,128)(2,1)S(1)}, u32[]{:S(2)}, u32[]{:S(2)}) collective-permute-start(bf16[272,128]{1,0:T(8,128)(2,1)S(1)} %fusion.1), channel_id=1, source_target_pairs={{0,8},{1,9},{2,10},{3,11},{4,12},{5,13},{6,14},{7,15},{8,0},{9,1},... | collective-permute-start | bytes 208904 | tf_op jit(solution)/shard_map/ppermute | solution.py:322
  23.2 6.9 %collective-permute-start.6 = (bf16[272,128]{1,0:T(8,128)(2,1)S(1)}, bf16[272,128]{1,0:T(8,128)(2,1)S(1)}, u32[]{:S(2)}, u32[]{:S(2)}) collective-permute-start(bf16[272,128]{1,0:T(8,128)(2,1)S(1)} %fusion.1), channel_id=1, source_target_pairs={{0,16},{1,17},{2,18},{3,19},{4,20},{5,21},{6,22},{7,23},{8,24},{9,... | collective-permute-start | bytes 208904 | tf_op jit(solution)/shard_map/ppermute | solution.py:322
  25.8 6.1 %collective-permute-start.7 = (bf16[272,128]{1,0:T(8,128)(2,1)S(1)}, bf16[272,128]{1,0:T(8,128)(2,1)S(1)}, u32[]{:S(2)}, u32[]{:S(2)}) collective-permute-start(bf16[272,128]{1,0:T(8,128)(2,1)S(1)} %fusion.1), channel_id=1, source_target_pairs={{0,24},{1,25},{2,26},{3,27},{4,28},{5,29},{6,30},{7,31},{8,16},{9,... | collective-permute-start | bytes 208904 | tf_op jit(solution)/shard_map/ppermute | solution.py:322
  25.8 12.4 %all-to-all-start = ((bf16[32,8,256]{2,1,0:T(8,128)(2,1)}), bf16[32,8,256]{2,1,0:T(8,128)(2,1)S(1)}, u32[]{:S(2)}, u32[]{:S(2)}) async-start(bf16[32,8,256]{2,1,0:T(8,128)(2,1)} %shard_map.106), calls=%async_computation | async-start | bytes 262144 | tf_op jit(solution)/shard_map/all_to_all | solution.py:357
  32.0 1.3 %collective-permute-start.8 = (bf16[272,128]{1,0:T(8,128)(2,1)S(1)}, bf16[272,128]{1,0:T(8,128)(2,1)S(1)}, u32[]{:S(2)}, u32[]{:S(2)}) collective-permute-start(bf16[272,128]{1,0:T(8,128)(2,1)S(1)} %get-tuple-element.30), channel_id=1, source_target_pairs={{0,1},{1,0},{2,3},{3,2},{4,5},{5,4},{6,7},{7,6},{8,9},{9,8},{10,11... | collective-permute-start | bytes 208904 | tf_op jit(solution)/shard_map/ppermute | solution.py:322

commit v7 on v6

--- a/solution.py
+++ b/solution.py
@@ -54,7 +54,6 @@
     p2_ref,
     p3_ref,
     t32_ref,
-    t16_ref,
     frames,
     gain,
     w,
@@ -120,9 +119,9 @@
     for c in range(E // LANES):
         chunk = part[:, c * LANES : (c + 1) * LANES]
         t32_ref[c * caps : (c + 1) * caps] = chunk
-        t16_ref[c * caps : (c + 1) * caps] = chunk.astype(jnp.bfloat16)
+        p1_ref[3 * rows + c * caps : 3 * rows + (c + 1) * caps] = chunk.astype(jnp.bfloat16)
     t32_ref[sums:] = bounds
-    t16_ref[sums:] = bounds.astype(jnp.bfloat16)
+    p1_ref[3 * rows + sums :] = bounds.astype(jnp.bfloat16)
 
 
 def weights_kernel(frames_ref, w_out_ref, w_proj_ref, wc_ref, fp_ref):
@@ -177,7 +176,7 @@
                 jnp.dot(p.astype(jnp.bfloat16), v, preferred_element_type=jnp.float32)
                 for p, v in zip(probs, values)
             )
-            attended = jnp.where(mine, mixed / denom, attended)
+            attended = jnp.where(mine, mixed * (1.0 / denom), attended)
         attended = attended.astype(jnp.bfloat16).astype(jnp.float32)
         return jnp.sum(attended.reshape(blocks, BLK, half), axis=1)
 
@@ -198,19 +197,20 @@
     out_ref[...] = jnp.broadcast_to(piece[None], out_ref.shape)
 
 
-def tail_kernel(everyone_ref, mine_ref, last_ref, divisor_ref, derivative_ref, loss_ref):
-    own_caps = derivative_ref.shape[0]
-    devices, width, half = everyone_ref.shape
-    caps = (mine_ref.shape[0] - BOUND_ROWS) // (E // LANES)
+def unit(parts):
+    mean = sum(jnp.sum(p * p, axis=-1, keepdims=True) for p in parts) * (1.0 / E)
+    scale = lax.rsqrt(mean + 1e-06)
+    return jnp.concatenate(
+        [(p * scale * E ** (-0.5)).astype(jnp.bfloat16) for p in parts], axis=1
+    )
+
+
+def caption_kernel(group, width, mine_ref, last_ref, captions_ref, masks_ref):
+    caps = captions_ref.shape[0]
     sums = E // LANES * caps
-    group = 2 * lax.axis_size("head")
-    pairs = devices // group
     blocks = width // 2
-    slot = lax.axis_index("seq") * lax.axis_size("head") + lax.axis_index("head")
-    divisor = divisor_ref[0]
-
     total = mine_ref[...] + last_ref[...].astype(jnp.float32)
-    raw = jnp.concatenate([total[c * caps : (c + 1) * caps] for c in range(E // LANES)], axis=1)
+    captions_ref[...] = unit([total[c * caps : (c + 1) * caps] for c in range(E // LANES)])
 
     def column(side):
         found = jnp.zeros((caps, LANES), jnp.float32)
@@ -222,28 +222,26 @@
         return jnp.sum(found, axis=1, keepdims=True)
 
     lower, upper = column(0), column(1)
-
-    def unit(parts):
-        mean = sum(jnp.sum(p * p, axis=-1, keepdims=True) for p in parts) * (1.0 / E)
-        scale = lax.rsqrt(mean + 1e-06)
-        parts = [(p * scale * E ** (-0.5)).astype(jnp.bfloat16) for p in parts]
-        return parts[0] if len(parts) == 1 else jnp.concatenate(parts, axis=1)
-
-    captions = unit([raw])
-    sums = jnp.sum(
-        everyone_ref[...].astype(jnp.float32).reshape(pairs, group, width, half), axis=1
-    ).reshape(pairs * width, half)
-    place = lax.broadcasted_iota(jnp.int32, (caps, pairs * width), 1)
+    place = lax.broadcasted_iota(jnp.int32, (caps, masks_ref.shape[1]), 1)
     inner = place % width
-    block = (place // width * blocks + inner % blocks).astype(jnp.float32)
-    inside = (block >= lower) & (block < upper)
-    pooled = [
-        jnp.dot(
-            jnp.where(inside & (inner // blocks == side), 1.0, 0.0), sums, precision=HIGHEST
-        )
-        for side in range(2)
-    ]
-    spans = unit(pooled)
+    block = (place // (width * group) * blocks + inner % blocks).astype(jnp.float32)
+    inside = jnp.where((block >= lower) & (block < upper), 1.0, 0.0)
+    for side in range(2):
+        masks_ref[side * caps : (side + 1) * caps] = jnp.where(
+            inner // blocks == side, inside, 0.0
+        ).astype(jnp.bfloat16)
+
+
+def tail_kernel(everyone_ref, captions_ref, masks_ref, divisor_ref, derivative_ref, loss_ref):
+    own_caps = derivative_ref.shape[0]
+    devices, width, half = everyone_ref.shape
+    caps = captions_ref.shape[0]
+    slot = lax.axis_index("seq") * lax.axis_size("head") + lax.axis_index("head")
+    divisor = divisor_ref[0]
+    captions = captions_ref[...]
+    pieces = everyone_ref[...].reshape(devices * width, half)
+    pooled = jnp.dot(masks_ref[...], pieces, preferred_element_type=jnp.float32)
+    spans = unit([pooled[:caps], pooled[caps:]])
 
     logits = transposed_dot(spans, captions) * divisor
     row_total = jnp.log(jnp.sum(jnp.exp(logits), axis=0, keepdims=True))
@@ -288,10 +286,10 @@
 
     tall = E // LANES * token_ids.shape[0] + BOUND_ROWS
     given = (frames, norm_gain[None], w_qkv, token_ids.T, text_table, span_bounds)
-    own, p1, p2, p3, mine, sent = call(
+    own, p1, p2, p3, mine = call(
         first_kernel,
-        [shape((n * rows, half), bf16) for n in (3, 3, 2, 2)]
-        + [shape((tall, LANES), f32), shape((tall, LANES), bf16)],
+        [shape((n, half), bf16) for n in (3 * rows, 3 * rows + tall, 2 * rows, 2 * rows)]
+        + [shape((tall, LANES), f32)],
         [HBM] * len(given),
         [
             pltpu.SMEM(a.shape, a.dtype) if a is span_bounds else pltpu.VMEM(a.shape, a.dtype)
@@ -326,9 +324,8 @@
             mine = mine + g.astype(f32)
         return mine, mine.astype(bf16)
 
-    got, r1 = lax.optimization_barrier((swap(sent, 0, 2), r1))
-    mine, sent = add(mine, got)
-    got = swap(sent, 1, 0)
+    mine, sent = add(mine, r1[3 * rows :])
+    got = swap(sent, 0, 2)
 
     wc, fp = call(
         weights_kernel,
@@ -357,12 +354,20 @@
     everyone = lax.all_to_all(piece, EVERY, 0, 0)
     got = swap(sent, 0, 1)
 
+    captions, masks = call(
+        functools.partial(caption_kernel, 2 * head_count, 4 * blocks),
+        [
+            shape((token_ids.shape[0], E), bf16),
+            shape((2 * token_ids.shape[0], devices * 4 * blocks), bf16),
+        ],
+        [VMEM] * 2,
+    )(mine, got)
     derivative, loss = call(
         tail_kernel,
         [shape((own_caps, E), f32), shape((1, own_caps), f32)],
         [VMEM, VMEM, VMEM, SMEM],
         cost=(4 * E * token_ids.shape[0] ** 2, 2 * piece.size, 0),
-    )(everyone, mine, got, contrast_divisor)
+    )(everyone, captions, masks, contrast_divisor)
     return derivative, loss.reshape(own_caps)
 
 

time: 40 us -> 39.2 us (0.980)
  starting transfers between devices: 21.8 us -> 18.1 us
  waiting for transfers between devices: 8.27 us -> 11.1 us
    ppermute x6 -> x5, starting transfers between devices: 12.6 us -> 7.99 us  [swap(): return lax.ppermute(sent, EVERY, list(enumerate(to)))]
    ppermute x1, waiting for transfers between devices: 0.59 us -> 3.86 us  [local(): r1 = lax.ppermute(p1, 'seq', [(s, s ^ 1) for s in range(seq_count)])]
    ppermute x6 -> x5, waiting for transfers between devices: 2.75 us -> 1.54 us  [swap(): return lax.ppermute(sent, EVERY, list(enumerate(to)))]
    all_to_all x1, starting transfers between devices: 4.19 us -> 5.14 us  [local(): everyone = lax.all_to_all(piece, EVERY, 0, 0)]
    all_to_all x1, waiting for transfers between devices: 4.93 us -> 5.73 us  [local(): everyone = lax.all_to_all(piece, EVERY, 0, 0)]
    pallas_call x1 -> x2, Pallas kernels: 3.49 us -> 3.63 us  [the longest x1 3.49 us: local(): call(first_kernel, [shape((n, half), bf16) for n in (3 * rows, 3 * rows +...]
  transfers between devices with their start and end apart: 10 -> 9, of which waited for: 5 -> 4; matrix products, arithmetic and copies ran while one was open for 0% -> 0% of each run, Pallas kernels for 8% -> 9%
where the time goes in v7:
time: 39.2 us; the launch traced here: 39 us
  starting transfers between devices  18.1 us (46%)
  waiting for transfers between devices  11.1 us (28%)
  Pallas kernels  8.21 us (21%)
  between operations  1.41 us (4%)
    ppermute x5, starting transfers between devices, swap(): return lax.ppermute(sent, EVERY, list(enumerate(to)))  7.99 us
    all_to_all x1, waiting for transfers between devices, local(): everyone = lax.all_to_all(piece, EVERY, 0, 0)  5.73 us
    all_to_all x1, starting transfers between devices, local(): everyone = lax.all_to_all(piece, EVERY, 0, 0)  5.14 us
    ppermute x1, waiting for transfers between devices, local(): r1 = lax.ppermute(p1, 'seq', [(s, s ^ 1) for s in range(seq_count)])  3.86 us
    pallas_call x1, Pallas kernels, local(): call(first_kernel, [shape((n, half), bf16) for n in (3 * rows, 3 * rows +...  3.49 us
    ppermute x1, starting transfers between devices, local(): r1 = lax.ppermute(p1, 'seq', [(s, s ^ 1) for s in range(seq_count)])  3 us
    pallas_call x1, Pallas kernels, local(): call(attend_kernel, shape((devices, 4 * blocks, E // 2), PIECE), [VMEM] *...  2.67 us
    ppermute x5, waiting for transfers between devices, swap(): return lax.ppermute(sent, EVERY, list(enumerate(to)))  1.54 us
  transfers between devices with their start and end apart: 9, of which 4 were waited for; matrix products, arithmetic and copies ran while one was open for 0% of the time, Pallas kernels for 9%

profile of v7, /device:TPU:0, one launch (start us, length us, event | category | flops | bytes accessed | tf_op | source)
XLA Modules:
  0.0 39.0 jit_solution(10904371101936144345)
XLA Ops:
  0.6 0.0 copy-start
  0.6 0.0 copy-start.1
  0.7 0.0 copy-start.2
  0.7 3.5 %shard_map.104 = (bf16[768,128]{1,0:T(8,128)(2,1)S(1)}, bf16[1040,128]{1,0:T(8,128)(2,1)S(1)}, bf16[512,128]{1,0:T(8,128)(2,1)S(1)}, bf16[512,128]{1,0:T(8,128)(2,1)S(1)}, f32[272,128]{1,0:T(8,128)S(1)}) custom-call(bf16[256,1024]{1,0:T(8,128)(2,1)} %frames_ref.1, f32[1,1024]{1,0:T(1,128)} %bitcast.4, bf16[3,1024,256]{2,1,0:T(8,128)(2,1)} %w_hbm.1, ...), custom_call_target="tpu_custom_call" | custom-call | flops 402653184 | bytes 1572864 | tf_op jit(solution)/shard_map/pallas_call | solution.py:289
  4.2 3.0 %collective-permute-start = (bf16[1040,128]{1,0:T(8,128)(2,1)S(1)}, bf16[1040,128]{1,0:T(8,128)(2,1)S(1)}, u32[]{:S(2)}, u32[]{:S(2)}) collective-permute-start(bf16[1040,128]{1,0:T(8,128)(2,1)S(1)} %get-tuple-element.16), channel_id=1, source_target_pairs={{0,4},{4,0},{8,12},{12,8},{16,20},{20,16},{24,28},{28,24},{1,5},{5... | collective-permute-start | bytes 798728 | tf_op jit(solution)/shard_map/ppermute | solution.py:302
  7.2 1.3 %collective-permute-start.2 = (bf16[512,128]{1,0:T(8,128)(2,1)S(1)}, bf16[512,128]{1,0:T(8,128)(2,1)S(1)}, u32[]{:S(2)}, u32[]{:S(2)}) collective-permute-start(bf16[512,128]{1,0:T(8,128)(2,1)S(1)} %get-tuple-element.18), channel_id=1, source_target_pairs={{4,12},{12,20},{20,28},{8,0},{16,8},{24,16},{5,13},{13,21},{21,29}... | collective-permute-start | bytes 393224 | tf_op jit(solution)/shard_map/ppermute | solution.py:308
  8.5 0.7 %collective-permute-start.3 = (bf16[512,128]{1,0:T(8,128)(2,1)S(1)}, bf16[512,128]{1,0:T(8,128)(2,1)S(1)}, u32[]{:S(2)}, u32[]{:S(2)}) collective-permute-start(bf16[512,128]{1,0:T(8,128)(2,1)S(1)} %get-tuple-element.19), channel_id=1, source_target_pairs={{4,8},{12,16},{20,24},{8,4},{16,12},{24,20},{5,9},{13,17},{21,25},... | collective-permute-start | bytes 393224 | tf_op jit(solution)/shard_map/ppermute | solution.py:303
  9.1 0.0 copy-done
  9.1 0.0 copy-done.1
  9.1 0.0 copy-done.2
  9.2 0.5 %shard_map.105 = (f32[128,512]{1,0:T(8,128)S(1)}, f32[2,512]{1,0:T(2,128)S(1)}) custom-call(bf16[256,1024]{1,0:T(8,128)(2,1)S(1)} %copy-done, bf16[256,1024]{1,0:T(8,128)(2,1)S(1)} %copy-done.2, bf16[1024,512]{1,0:T(8,128)(2,1)S(1)} %copy-done.1), custom_call_target="tpu_custom_call" | custom-call | flops 10000000000 | bytes 2097152 | tf_op jit(solution)/shard_map/pallas_call | solution.py:330
  9.7 3.9 %collective-permute-done.r1_ref = bf16[1040,128]{1,0:T(8,128)(2,1)S(1)} collective-permute-done((bf16[1040,128]{1,0:T(8,128)(2,1)S(1)}, bf16[1040,128]{1,0:T(8,128)(2,1)S(1)}, u32[]{:S(2)}, u32[]{:S(2)}) %collective-permute-start) | collective-permute-done | bytes 266272 | tf_op jit(solution)/shard_map/ppermute | solution.py:302
  13.6 1.8 %collective-permute-start.1 = (bf16[272,128]{1,0:T(8,128)(2,1)S(1)}, bf16[272,128]{1,0:T(8,128)(2,1)S(1)}, u32[]{:S(2)}, u32[]{:S(2)}) collective-permute-start(bf16[272,128]{1,0:T(8,128)(2,1)S(1)} %fusion), channel_id=1, source_target_pairs={{0,2},{1,3},{2,0},{3,1},{4,6},{5,7},{6,4},{7,5},{8,10},{9,11},{10,... | collective-permute-start | bytes 208904 | tf_op jit(solution)/shard_map/ppermute | solution.py:320
  15.4 0.0 collective-permute-done.2.r2_ref
  15.4 0.0 collective-permute-done.3.r3_ref
  15.4 2.7 %shard_map.106 = bf16[32,8,256]{2,1,0:T(8,128)(2,1)} custom-call(bf16[768,128]{1,0:T(8,128)(2,1)S(1)} %get-tuple-element.17.own_ref, bf16[1040,128]{1,0:T(8,128)(2,1)S(1)} %collective-permute-done.r1_ref, bf16[512,128]{1,0:T(8,128)(2,1)S(1)} %collective-permute-done.2.r2_ref, bf16[512,128]{1,0:T(8,128)(2,1)S(1)} %collective-permute-done.3.r3_ref, ...), custom_call_target="tpu_custom_call" | custom-call | flops 10000000000 | bytes 655360 | tf_op jit(solution)/shard_map/pallas_call | solution.py:337
  18.1 0.0 collective-permute-done.1
  18.1 3.5 %collective-permute-start.4 = (bf16[272,128]{1,0:T(8,128)(2,1)S(1)}, bf16[272,128]{1,0:T(8,128)(2,1)S(1)}, u32[]{:S(2)}, u32[]{:S(2)}) collective-permute-start(bf16[272,128]{1,0:T(8,128)(2,1)S(1)} %fusion.1), channel_id=1, source_target_pairs={{0,8},{1,9},{2,10},{3,11},{4,12},{5,13},{6,14},{7,15},{8,0},{9,1},... | collective-permute-start | bytes 208904 | tf_op jit(solution)/shard_map/ppermute | solution.py:320
  21.6 2.6 %collective-permute-start.5 = (bf16[272,128]{1,0:T(8,128)(2,1)S(1)}, bf16[272,128]{1,0:T(8,128)(2,1)S(1)}, u32[]{:S(2)}, u32[]{:S(2)}) collective-permute-start(bf16[272,128]{1,0:T(8,128)(2,1)S(1)} %fusion.1), channel_id=1, source_target_pairs={{0,16},{1,17},{2,18},{3,19},{4,20},{5,21},{6,22},{7,23},{8,24},{9,... | collective-permute-start | bytes 208904 | tf_op jit(solution)/shard_map/ppermute | solution.py:320
  24.2 0.0 collective-permute-start.6
  24.2 5.1 %all-to-all-start = ((bf16[32,8,256]{2,1,0:T(8,128)(2,1)}), bf16[32,8,256]{2,1,0:T(8,128)(2,1)S(1)}, u32[]{:S(2)}, u32[]{:S(2)}) async-start(bf16[32,8,256]{2,1,0:T(8,128)(2,1)} %shard_map.106), calls=%async_computation | async-start | bytes 262144 | tf_op jit(solution)/shard_map/all_to_all | solution.py:354
  29.4 0.0 collective-permute-done.4
  29.4 0.0 collective-permute-done.5
  29.4 0.9 %collective-permute-done.6 = bf16[272,128]{1,0:T(8,128)(2,1)S(1)} collective-permute-done((bf16[272,128]{1,0:T(8,128)(2,1)S(1)}, bf16[272,128]{1,0:T(8,128)(2,1)S(1)}, u32[]{:S(2)}, u32[]{:S(2)}) %collective-permute-start.6) | collective-permute-done | bytes 69664 | tf_op jit(solution)/shard_map/ppermute | solution.py:320
  30.3 0.1 fusion.2
  30.4 0.1 collective-permute-start.7
  31.1 0.6 %collective-permute-done.7.last_ref = bf16[272,128]{1,0:T(8,128)(2,1)S(1)} collective-permute-done((bf16[272,128]{1,0:T(8,128)(2,1)S(1)}, bf16[272,128]{1,0:T(8,128)(2,1)S(1)}, u32[]{:S(2)}, u32[]{:S(2)}) %collective-permute-start.7) | collective-permute-done | bytes 69664 | tf_op jit(solution)/shard_map/ppermute | solution.py:320
  31.7 0.1 shard_map.107
  31.9 5.7 %all-to-all-done.everyone_ref = bf16[32,8,256]{2,1,0:T(8,128)(2,1)S(1)} async-done(((bf16[32,8,256]{2,1,0:T(8,128)(2,1)}), bf16[32,8,256]{2,1,0:T(8,128)(2,1)S(1)}, u32[]{:S(2)}, u32[]{:S(2)}) %all-to-all-start) | async-done | bytes 131104 | tf_op jit(solution)/shard_map/all_to_all | solution.py:354
  37.6 1.4 %shard_map.108 = (f32[2,512]{1,0:T(2,128)}, f32[1,2]{1,0:T(1,128)}) custom-call(bf16[32,8,256]{2,1,0:T(8,128)(2,1)S(1)} %all-to-all-done.everyone_ref, bf16[64,512]{1,0:T(8,128)(2,1)S(1)} %get-tuple-element.24.captions_ref, bf16[128,256]{1,0:T(8,128)(2,1)S(1)} %get-tuple-element.25.masks_ref, f32[1]{0:T(128)S(6)} %copy.11.divisor_ref), custom_call_target="tpu_custom_call" | custom-call | flops 8388608 | bytes 131072 | tf_op jit(solution)/shard_map/pallas_call | solution.py:365
  (2 shorter events, 0.1 us)
Async XLA Ops:
  0.6 8.5 %copy-start = (bf16[256,1024]{1,0:T(8,128)(2,1)S(1)}, bf16[256,1024]{1,0:T(8,128)(2,1)}, u32[]{:S(2)}) copy-start(bf16[256,1024]{1,0:T(8,128)(2,1)} %frames_ref.1) | copy-start | bytes 1572868
  0.6 8.5 %copy-start.1 = (bf16[1024,512]{1,0:T(8,128)(2,1)S(1)}, bf16[1024,512]{1,0:T(8,128)(2,1)}, u32[]{:S(2)}) copy-start(bf16[1024,512]{1,0:T(8,128)(2,1)} %w_proj_ref.1) | copy-start | bytes 3145732
  0.7 8.5 %copy-start.2 = (bf16[256,1024]{1,0:T(8,128)(2,1)S(1)}, bf16[256,1024]{1,0:T(8,128)(2,1)}, u32[]{:S(2)}) copy-start(bf16[256,1024]{1,0:T(8,128)(2,1)} %w_out_ref.1) | copy-start | bytes 1572868
  4.2 9.4 %collective-permute-start = (bf16[1040,128]{1,0:T(8,128)(2,1)S(1)}, bf16[1040,128]{1,0:T(8,128)(2,1)S(1)}, u32[]{:S(2)}, u32[]{:S(2)}) collective-permute-start(bf16[1040,128]{1,0:T(8,128)(2,1)S(1)} %get-tuple-element.16), channel_id=1, source_target_pairs={{0,4},{4,0},{8,12},{12,8},{16,20},{20,16},{24,28},{28,24},{1,5},{5... | collective-permute-start | bytes 798728 | tf_op jit(solution)/shard_map/ppermute | solution.py:302
  7.2 8.3 %collective-permute-start.2 = (bf16[512,128]{1,0:T(8,128)(2,1)S(1)}, bf16[512,128]{1,0:T(8,128)(2,1)S(1)}, u32[]{:S(2)}, u32[]{:S(2)}) collective-permute-start(bf16[512,128]{1,0:T(8,128)(2,1)S(1)} %get-tuple-element.18), channel_id=1, source_target_pairs={{4,12},{12,20},{20,28},{8,0},{16,8},{24,16},{5,13},{13,21},{21,29}... | collective-permute-start | bytes 393224 | tf_op jit(solution)/shard_map/ppermute | solution.py:308
  8.5 7.0 %collective-permute-start.3 = (bf16[512,128]{1,0:T(8,128)(2,1)S(1)}, bf16[512,128]{1,0:T(8,128)(2,1)S(1)}, u32[]{:S(2)}, u32[]{:S(2)}) collective-permute-start(bf16[512,128]{1,0:T(8,128)(2,1)S(1)} %get-tuple-element.19), channel_id=1, source_target_pairs={{4,8},{12,16},{20,24},{8,4},{16,12},{24,20},{5,9},{13,17},{21,25},... | collective-permute-start | bytes 393224 | tf_op jit(solution)/shard_map/ppermute | solution.py:303
  13.6 4.5 %collective-permute-start.1 = (bf16[272,128]{1,0:T(8,128)(2,1)S(1)}, bf16[272,128]{1,0:T(8,128)(2,1)S(1)}, u32[]{:S(2)}, u32[]{:S(2)}) collective-permute-start(bf16[272,128]{1,0:T(8,128)(2,1)S(1)} %fusion), channel_id=1, source_target_pairs={{0,2},{1,3},{2,0},{3,1},{4,6},{5,7},{6,4},{7,5},{8,10},{9,11},{10,... | collective-permute-start | bytes 208904 | tf_op jit(solution)/shard_map/ppermute | solution.py:320
  18.1 11.2 %collective-permute-start.4 = (bf16[272,128]{1,0:T(8,128)(2,1)S(1)}, bf16[272,128]{1,0:T(8,128)(2,1)S(1)}, u32[]{:S(2)}, u32[]{:S(2)}) collective-permute-start(bf16[272,128]{1,0:T(8,128)(2,1)S(1)} %fusion.1), channel_id=1, source_target_pairs={{0,8},{1,9},{2,10},{3,11},{4,12},{5,13},{6,14},{7,15},{8,0},{9,1},... | collective-permute-start | bytes 208904 | tf_op jit(solution)/shard_map/ppermute | solution.py:320
  21.6 7.8 %collective-permute-start.5 = (bf16[272,128]{1,0:T(8,128)(2,1)S(1)}, bf16[272,128]{1,0:T(8,128)(2,1)S(1)}, u32[]{:S(2)}, u32[]{:S(2)}) collective-permute-start(bf16[272,128]{1,0:T(8,128)(2,1)S(1)} %fusion.1), channel_id=1, source_target_pairs={{0,16},{1,17},{2,18},{3,19},{4,20},{5,21},{6,22},{7,23},{8,24},{9,... | collective-permute-start | bytes 208904 | tf_op jit(solution)/shard_map/ppermute | solution.py:320
  24.2 6.1 %collective-permute-start.6 = (bf16[272,128]{1,0:T(8,128)(2,1)S(1)}, bf16[272,128]{1,0:T(8,128)(2,1)S(1)}, u32[]{:S(2)}, u32[]{:S(2)}) collective-permute-start(bf16[272,128]{1,0:T(8,128)(2,1)S(1)} %fusion.1), channel_id=1, source_target_pairs={{0,24},{1,25},{2,26},{3,27},{4,28},{5,29},{6,30},{7,31},{8,16},{9,... | collective-permute-start | bytes 208904 | tf_op jit(solution)/shard_map/ppermute | solution.py:320
  24.2 13.4 %all-to-all-start = ((bf16[32,8,256]{2,1,0:T(8,128)(2,1)}), bf16[32,8,256]{2,1,0:T(8,128)(2,1)S(1)}, u32[]{:S(2)}, u32[]{:S(2)}) async-start(bf16[32,8,256]{2,1,0:T(8,128)(2,1)} %shard_map.106), calls=%async_computation | async-start | bytes 262144 | tf_op jit(solution)/shard_map/all_to_all | solution.py:354
  30.4 1.3 %collective-permute-start.7 = (bf16[272,128]{1,0:T(8,128)(2,1)S(1)}, bf16[272,128]{1,0:T(8,128)(2,1)S(1)}, u32[]{:S(2)}, u32[]{:S(2)}) collective-permute-start(bf16[272,128]{1,0:T(8,128)(2,1)S(1)} %get-tuple-element.28), channel_id=1, source_target_pairs={{0,1},{1,0},{2,3},{3,2},{4,5},{5,4},{6,7},{7,6},{8,9},{9,8},{10,11... | collective-permute-start | bytes 208904 | tf_op jit(solution)/shard_map/ppermute | solution.py:320

commit v8 on v7

--- a/solution.py
+++ b/solution.py
@@ -205,11 +205,12 @@
     )
 
 
-def caption_kernel(group, width, mine_ref, last_ref, captions_ref, masks_ref):
+def caption_kernel(group, width, mine_ref, *refs):
+    *got_refs, captions_ref, masks_ref = refs
     caps = captions_ref.shape[0]
     sums = E // LANES * caps
     blocks = width // 2
-    total = mine_ref[...] + last_ref[...].astype(jnp.float32)
+    total = mine_ref[...] + sum(ref[...].astype(jnp.float32) for ref in got_refs)
     captions_ref[...] = unit([total[c * caps : (c + 1) * caps] for c in range(E // LANES)])
 
     def column(side):
@@ -325,7 +326,7 @@
         return mine, mine.astype(bf16)
 
     mine, sent = add(mine, r1[3 * rows :])
-    got = swap(sent, 0, 2)
+    got = swap(sent, 2, 0)
 
     wc, fp = call(
         weights_kernel,
@@ -343,16 +344,12 @@
 
     got, piece = lax.optimization_barrier((got, piece))
     mine, sent = add(mine, got)
-    step = 2
+    step = 4
     while step < seq_count:
-        if 4 * step <= seq_count:
-            mine, sent = add(mine, *[swap(sent, k * step, 0) for k in (1, 2, 3)])
-            step *= 4
-        else:
-            mine, sent = add(mine, swap(sent, step, 0))
-            step *= 2
+        mine, sent = add(mine, swap(sent, step, 0))
+        step *= 2
     everyone = lax.all_to_all(piece, EVERY, 0, 0)
-    got = swap(sent, 0, 1)
+    gots = [swap(sent, 0, k) for k in range(1, head_count)]
 
     captions, masks = call(
         functools.partial(caption_kernel, 2 * head_count, 4 * blocks),
@@ -360,8 +357,8 @@
             shape((token_ids.shape[0], E), bf16),
             shape((2 * token_ids.shape[0], devices * 4 * blocks), bf16),
         ],
-        [VMEM] * 2,
-    )(mine, got)
+        [VMEM] * head_count,
+    )(mine, *gots)
     derivative, loss = call(
         tail_kernel,
         [shape((own_caps, E), f32), shape((1, own_caps), f32)],

time: 39.2 us -> 36.2 us (0.923)
  starting transfers between devices: 18.1 us -> 16.5 us
  waiting for transfers between devices: 11.1 us -> 9.76 us
    all_to_all x1, waiting for transfers between devices: 5.73 us -> 0.99 us  [local(): everyone = lax.all_to_all(piece, EVERY, 0, 0)]
    ppermute x5, waiting for transfers between devices: 1.54 us -> 4.9 us  [swap(): return lax.ppermute(sent, EVERY, list(enumerate(to)))]
    all_to_all x1, starting transfers between devices: 5.14 us -> 3.76 us  [local(): everyone = lax.all_to_all(piece, EVERY, 0, 0)]
  transfers between devices with their start and end apart: 9 -> 9, of which waited for: 4 -> 5; matrix products, arithmetic and copies ran while one was open for 0% -> 0% of each run, Pallas kernels for 9% -> 9%
where the time goes in v8:
time: 36.2 us; the launch traced here: 36 us
  starting transfers between devices  16.5 us (46%)
  waiting for transfers between devices  9.76 us (27%)
  Pallas kernels  8.21 us (23%)
  between operations  1.4 us (4%)
    ppermute x5, starting transfers between devices, swap(): return lax.ppermute(sent, EVERY, list(enumerate(to)))  7.82 us
    ppermute x5, waiting for transfers between devices, swap(): return lax.ppermute(sent, EVERY, list(enumerate(to)))  4.9 us
    ppermute x1, waiting for transfers between devices, local(): r1 = lax.ppermute(p1, 'seq', [(s, s ^ 1) for s in range(seq_count)])  3.86 us
    all_to_all x1, starting transfers between devices, local(): everyone = lax.all_to_all(piece, EVERY, 0, 0)  3.76 us
    pallas_call x1, Pallas kernels, local(): call(first_kernel, [shape((n, half), bf16) for n in (3 * rows, 3 * rows +...  3.49 us
    ppermute x1, starting transfers between devices, local(): r1 = lax.ppermute(p1, 'seq', [(s, s ^ 1) for s in range(seq_count)])  3 us
    pallas_call x1, Pallas kernels, local(): call(attend_kernel, shape((devices, 4 * blocks, E // 2), PIECE), [VMEM] *...  2.67 us
    pallas_call x1, Pallas kernels, local(): call(tail_kernel, [shape((own_caps, E), f32), shape((1, own_caps), f32)],...  1.37 us
  transfers between devices with their start and end apart: 9, of which 5 were waited for; matrix products, arithmetic and copies ran while one was open for 0% of the time, Pallas kernels for 9%

profile of v8, /device:TPU:0, one launch (start us, length us, event | category | flops | bytes accessed | tf_op | source)
XLA Modules:
  0.0 36.0 jit_solution(17468693669998230211)
XLA Ops:
  0.6 0.0 copy-start
  0.6 0.0 copy-start.1
  0.7 0.0 copy-start.2
  0.7 3.5 %shard_map.104 = (bf16[768,128]{1,0:T(8,128)(2,1)S(1)}, bf16[1040,128]{1,0:T(8,128)(2,1)S(1)}, bf16[512,128]{1,0:T(8,128)(2,1)S(1)}, bf16[512,128]{1,0:T(8,128)(2,1)S(1)}, f32[272,128]{1,0:T(8,128)S(1)}) custom-call(bf16[256,1024]{1,0:T(8,128)(2,1)} %frames_ref.1, f32[1,1024]{1,0:T(1,128)} %bitcast.4, bf16[3,1024,256]{2,1,0:T(8,128)(2,1)} %w_hbm.1, ...), custom_call_target="tpu_custom_call" | custom-call | flops 402653184 | bytes 1572864 | tf_op jit(solution)/shard_map/pallas_call | solution.py:290
  4.2 3.0 %collective-permute-start = (bf16[1040,128]{1,0:T(8,128)(2,1)S(1)}, bf16[1040,128]{1,0:T(8,128)(2,1)S(1)}, u32[]{:S(2)}, u32[]{:S(2)}) collective-permute-start(bf16[1040,128]{1,0:T(8,128)(2,1)S(1)} %get-tuple-element.16), channel_id=1, source_target_pairs={{0,4},{4,0},{8,12},{12,8},{16,20},{20,16},{24,28},{28,24},{1,5},{5... | collective-permute-start | bytes 798728 | tf_op jit(solution)/shard_map/ppermute | solution.py:303
  7.2 1.3 %collective-permute-start.2 = (bf16[512,128]{1,0:T(8,128)(2,1)S(1)}, bf16[512,128]{1,0:T(8,128)(2,1)S(1)}, u32[]{:S(2)}, u32[]{:S(2)}) collective-permute-start(bf16[512,128]{1,0:T(8,128)(2,1)S(1)} %get-tuple-element.18), channel_id=1, source_target_pairs={{4,12},{12,20},{20,28},{8,0},{16,8},{24,16},{5,13},{13,21},{21,29}... | collective-permute-start | bytes 393224 | tf_op jit(solution)/shard_map/ppermute | solution.py:309
  8.5 0.7 %collective-permute-start.3 = (bf16[512,128]{1,0:T(8,128)(2,1)S(1)}, bf16[512,128]{1,0:T(8,128)(2,1)S(1)}, u32[]{:S(2)}, u32[]{:S(2)}) collective-permute-start(bf16[512,128]{1,0:T(8,128)(2,1)S(1)} %get-tuple-element.19), channel_id=1, source_target_pairs={{4,8},{12,16},{20,24},{8,4},{16,12},{24,20},{5,9},{13,17},{21,25},... | collective-permute-start | bytes 393224 | tf_op jit(solution)/shard_map/ppermute | solution.py:304
  9.1 0.0 copy-done
  9.1 0.0 copy-done.1
  9.1 0.0 copy-done.2
  9.2 0.5 %shard_map.105 = (f32[128,512]{1,0:T(8,128)S(1)}, f32[2,512]{1,0:T(2,128)S(1)}) custom-call(bf16[256,1024]{1,0:T(8,128)(2,1)S(1)} %copy-done, bf16[256,1024]{1,0:T(8,128)(2,1)S(1)} %copy-done.2, bf16[1024,512]{1,0:T(8,128)(2,1)S(1)} %copy-done.1), custom_call_target="tpu_custom_call" | custom-call | flops 10000000000 | bytes 2097152 | tf_op jit(solution)/shard_map/pallas_call | solution.py:331
  9.7 3.9 %collective-permute-done.r1_ref = bf16[1040,128]{1,0:T(8,128)(2,1)S(1)} collective-permute-done((bf16[1040,128]{1,0:T(8,128)(2,1)S(1)}, bf16[1040,128]{1,0:T(8,128)(2,1)S(1)}, u32[]{:S(2)}, u32[]{:S(2)}) %collective-permute-start) | collective-permute-done | bytes 266272 | tf_op jit(solution)/shard_map/ppermute | solution.py:303
  13.6 1.9 %collective-permute-start.1 = (bf16[272,128]{1,0:T(8,128)(2,1)S(1)}, bf16[272,128]{1,0:T(8,128)(2,1)S(1)}, u32[]{:S(2)}, u32[]{:S(2)}) collective-permute-start(bf16[272,128]{1,0:T(8,128)(2,1)S(1)} %fusion), channel_id=1, source_target_pairs={{0,8},{1,9},{2,10},{3,11},{4,12},{5,13},{6,14},{7,15},{8,0},{9,1},... | collective-permute-start | bytes 208904 | tf_op jit(solution)/shard_map/ppermute | solution.py:321
  15.5 0.0 collective-permute-done.2.r2_ref
  15.5 0.0 collective-permute-done.3.r3_ref
  15.5 2.7 %shard_map.106 = bf16[32,8,256]{2,1,0:T(8,128)(2,1)} custom-call(bf16[768,128]{1,0:T(8,128)(2,1)S(1)} %get-tuple-element.17.own_ref, bf16[1040,128]{1,0:T(8,128)(2,1)S(1)} %collective-permute-done.r1_ref, bf16[512,128]{1,0:T(8,128)(2,1)S(1)} %collective-permute-done.2.r2_ref, bf16[512,128]{1,0:T(8,128)(2,1)S(1)} %collective-permute-done.3.r3_ref, ...), custom_call_target="tpu_custom_call" | custom-call | flops 10000000000 | bytes 655360 | tf_op jit(solution)/shard_map/pallas_call | solution.py:338
  18.1 0.5 %collective-permute-done.1 = bf16[272,128]{1,0:T(8,128)(2,1)S(1)} collective-permute-done((bf16[272,128]{1,0:T(8,128)(2,1)S(1)}, bf16[272,128]{1,0:T(8,128)(2,1)S(1)}, u32[]{:S(2)}, u32[]{:S(2)}) %collective-permute-start.1) | collective-permute-done | bytes 69664 | tf_op jit(solution)/shard_map/ppermute | solution.py:321
  18.7 3.9 %collective-permute-start.4 = (bf16[272,128]{1,0:T(8,128)(2,1)S(1)}, bf16[272,128]{1,0:T(8,128)(2,1)S(1)}, u32[]{:S(2)}, u32[]{:S(2)}) collective-permute-start(bf16[272,128]{1,0:T(8,128)(2,1)S(1)} %fusion.1), channel_id=1, source_target_pairs={{0,16},{1,17},{2,18},{3,19},{4,20},{5,21},{6,22},{7,23},{8,24},{9,... | collective-permute-start | bytes 208904 | tf_op jit(solution)/shard_map/ppermute | solution.py:321
  22.7 3.8 %all-to-all-start = ((bf16[32,8,256]{2,1,0:T(8,128)(2,1)}), bf16[32,8,256]{2,1,0:T(8,128)(2,1)S(1)}, u32[]{:S(2)}, u32[]{:S(2)}) async-start(bf16[32,8,256]{2,1,0:T(8,128)(2,1)} %shard_map.106), calls=%async_computation | async-start | bytes 262144 | tf_op jit(solution)/shard_map/all_to_all | solution.py:351
  26.4 0.0 collective-permute-done.4
  26.5 0.3 collective-permute-start.5
  26.8 1.7 %collective-permute-start.6 = (bf16[272,128]{1,0:T(8,128)(2,1)S(1)}, bf16[272,128]{1,0:T(8,128)(2,1)S(1)}, u32[]{:S(2)}, u32[]{:S(2)}) collective-permute-start(bf16[272,128]{1,0:T(8,128)(2,1)S(1)} %get-tuple-element.28), channel_id=1, source_target_pairs={{0,2},{1,3},{2,0},{3,1},{4,6},{5,7},{6,4},{7,5},{8,10},{9,11},{10,... | collective-permute-start | bytes 208904 | tf_op jit(solution)/shard_map/ppermute | solution.py:321
  28.5 0.0 collective-permute-start.7
  29.1 0.0 collective-permute-done.5.refs_0_
  29.1 3.0 %collective-permute-done.6.refs_1_ = bf16[272,128]{1,0:T(8,128)(2,1)S(1)} collective-permute-done((bf16[272,128]{1,0:T(8,128)(2,1)S(1)}, bf16[272,128]{1,0:T(8,128)(2,1)S(1)}, u32[]{:S(2)}, u32[]{:S(2)}) %collective-permute-start.6) | collective-permute-done | bytes 69664 | tf_op jit(solution)/shard_map/ppermute | solution.py:321
  32.2 1.3 %collective-permute-done.7.refs_2_ = bf16[272,128]{1,0:T(8,128)(2,1)S(1)} collective-permute-done((bf16[272,128]{1,0:T(8,128)(2,1)S(1)}, bf16[272,128]{1,0:T(8,128)(2,1)S(1)}, u32[]{:S(2)}, u32[]{:S(2)}) %collective-permute-start.7) | collective-permute-done | bytes 69664 | tf_op jit(solution)/shard_map/ppermute | solution.py:321
  33.5 0.1 shard_map.107
  33.7 1.0 %all-to-all-done.everyone_ref = bf16[32,8,256]{2,1,0:T(8,128)(2,1)S(1)} async-done(((bf16[32,8,256]{2,1,0:T(8,128)(2,1)}), bf16[32,8,256]{2,1,0:T(8,128)(2,1)S(1)}, u32[]{:S(2)}, u32[]{:S(2)}) %all-to-all-start) | async-done | bytes 131104 | tf_op jit(solution)/shard_map/all_to_all | solution.py:351
  34.6 1.4 %shard_map.108 = (f32[2,512]{1,0:T(2,128)}, f32[1,2]{1,0:T(1,128)}) custom-call(bf16[32,8,256]{2,1,0:T(8,128)(2,1)S(1)} %all-to-all-done.everyone_ref, bf16[64,512]{1,0:T(8,128)(2,1)S(1)} %get-tuple-element.24.captions_ref, bf16[128,256]{1,0:T(8,128)(2,1)S(1)} %get-tuple-element.25.masks_ref, f32[1]{0:T(128)S(6)} %copy.11.divisor_ref), custom_call_target="tpu_custom_call" | custom-call | flops 8388608 | bytes 131072 | tf_op jit(solution)/shard_map/pallas_call | solution.py:362
  (3 shorter events, 0.1 us)
Async XLA Ops:
  0.6 8.5 %copy-start = (bf16[256,1024]{1,0:T(8,128)(2,1)S(1)}, bf16[256,1024]{1,0:T(8,128)(2,1)}, u32[]{:S(2)}) copy-start(bf16[256,1024]{1,0:T(8,128)(2,1)} %frames_ref.1) | copy-start | bytes 1572868
  0.6 8.5 %copy-start.1 = (bf16[1024,512]{1,0:T(8,128)(2,1)S(1)}, bf16[1024,512]{1,0:T(8,128)(2,1)}, u32[]{:S(2)}) copy-start(bf16[1024,512]{1,0:T(8,128)(2,1)} %w_proj_ref.1) | copy-start | bytes 3145732
  0.7 8.5 %copy-start.2 = (bf16[256,1024]{1,0:T(8,128)(2,1)S(1)}, bf16[256,1024]{1,0:T(8,128)(2,1)}, u32[]{:S(2)}) copy-start(bf16[256,1024]{1,0:T(8,128)(2,1)} %w_out_ref.1) | copy-start | bytes 1572868
  4.2 9.4 %collective-permute-start = (bf16[1040,128]{1,0:T(8,128)(2,1)S(1)}, bf16[1040,128]{1,0:T(8,128)(2,1)S(1)}, u32[]{:S(2)}, u32[]{:S(2)}) collective-permute-start(bf16[1040,128]{1,0:T(8,128)(2,1)S(1)} %get-tuple-element.16), channel_id=1, source_target_pairs={{0,4},{4,0},{8,12},{12,8},{16,20},{20,16},{24,28},{28,24},{1,5},{5... | collective-permute-start | bytes 798728 | tf_op jit(solution)/shard_map/ppermute | solution.py:303
  7.2 8.3 %collective-permute-start.2 = (bf16[512,128]{1,0:T(8,128)(2,1)S(1)}, bf16[512,128]{1,0:T(8,128)(2,1)S(1)}, u32[]{:S(2)}, u32[]{:S(2)}) collective-permute-start(bf16[512,128]{1,0:T(8,128)(2,1)S(1)} %get-tuple-element.18), channel_id=1, source_target_pairs={{4,12},{12,20},{20,28},{8,0},{16,8},{24,16},{5,13},{13,21},{21,29}... | collective-permute-start | bytes 393224 | tf_op jit(solution)/shard_map/ppermute | solution.py:309
  8.5 7.0 %collective-permute-start.3 = (bf16[512,128]{1,0:T(8,128)(2,1)S(1)}, bf16[512,128]{1,0:T(8,128)(2,1)S(1)}, u32[]{:S(2)}, u32[]{:S(2)}) collective-permute-start(bf16[512,128]{1,0:T(8,128)(2,1)S(1)} %get-tuple-element.19), channel_id=1, source_target_pairs={{4,8},{12,16},{20,24},{8,4},{16,12},{24,20},{5,9},{13,17},{21,25},... | collective-permute-start | bytes 393224 | tf_op jit(solution)/shard_map/ppermute | solution.py:304
  13.6 5.1 %collective-permute-start.1 = (bf16[272,128]{1,0:T(8,128)(2,1)S(1)}, bf16[272,128]{1,0:T(8,128)(2,1)S(1)}, u32[]{:S(2)}, u32[]{:S(2)}) collective-permute-start(bf16[272,128]{1,0:T(8,128)(2,1)S(1)} %fusion), channel_id=1, source_target_pairs={{0,8},{1,9},{2,10},{3,11},{4,12},{5,13},{6,14},{7,15},{8,0},{9,1},... | collective-permute-start | bytes 208904 | tf_op jit(solution)/shard_map/ppermute | solution.py:321
  18.7 7.7 %collective-permute-start.4 = (bf16[272,128]{1,0:T(8,128)(2,1)S(1)}, bf16[272,128]{1,0:T(8,128)(2,1)S(1)}, u32[]{:S(2)}, u32[]{:S(2)}) collective-permute-start(bf16[272,128]{1,0:T(8,128)(2,1)S(1)} %fusion.1), channel_id=1, source_target_pairs={{0,16},{1,17},{2,18},{3,19},{4,20},{5,21},{6,22},{7,23},{8,24},{9,... | collective-permute-start | bytes 208904 | tf_op jit(solution)/shard_map/ppermute | solution.py:321
  22.7 12.0 %all-to-all-start = ((bf16[32,8,256]{2,1,0:T(8,128)(2,1)}), bf16[32,8,256]{2,1,0:T(8,128)(2,1)S(1)}, u32[]{:S(2)}, u32[]{:S(2)}) async-start(bf16[32,8,256]{2,1,0:T(8,128)(2,1)} %shard_map.106), calls=%async_computation | async-start | bytes 262144 | tf_op jit(solution)/shard_map/all_to_all | solution.py:351
  26.5 2.7 %collective-permute-start.5 = (bf16[272,128]{1,0:T(8,128)(2,1)S(1)}, bf16[272,128]{1,0:T(8,128)(2,1)S(1)}, u32[]{:S(2)}, u32[]{:S(2)}) collective-permute-start(bf16[272,128]{1,0:T(8,128)(2,1)S(1)} %get-tuple-element.28), channel_id=1, source_target_pairs={{0,1},{1,0},{2,3},{3,2},{4,5},{5,4},{6,7},{7,6},{8,9},{9,8},{10,11... | collective-permute-start | bytes 208904 | tf_op jit(solution)/shard_map/ppermute | solution.py:321
  26.8 5.4 %collective-permute-start.6 = (bf16[272,128]{1,0:T(8,128)(2,1)S(1)}, bf16[272,128]{1,0:T(8,128)(2,1)S(1)}, u32[]{:S(2)}, u32[]{:S(2)}) collective-permute-start(bf16[272,128]{1,0:T(8,128)(2,1)S(1)} %get-tuple-element.28), channel_id=1, source_target_pairs={{0,2},{1,3},{2,0},{3,1},{4,6},{5,7},{6,4},{7,5},{8,10},{9,11},{10,... | collective-permute-start | bytes 208904 | tf_op jit(solution)/shard_map/ppermute | solution.py:321
  28.5 5.0 %collective-permute-start.7 = (bf16[272,128]{1,0:T(8,128)(2,1)S(1)}, bf16[272,128]{1,0:T(8,128)(2,1)S(1)}, u32[]{:S(2)}, u32[]{:S(2)}) collective-permute-start(bf16[272,128]{1,0:T(8,128)(2,1)S(1)} %get-tuple-element.28), channel_id=1, source_target_pairs={{0,3},{1,2},{2,1},{3,0},{4,7},{5,6},{6,5},{7,4},{8,11},{9,10},{10,... | collective-permute-start | bytes 208904 | tf_op jit(solution)/shard_map/ppermute | solution.py:321

commit v9 on v8

--- a/solution.py
+++ b/solution.py
@@ -69,8 +69,8 @@
     parts += [(w_hbm.at[k], w.at[k]) for k in (1, 2, 0)]
     parts += [(table_hbm, table), (bounds_hbm, bound)]
     copies = [pltpu.make_async_copy(*part, sems.at[n]) for n, part in enumerate(parts)]
-    for copy in copies:
-        copy.start()
+    for n in (0, 1, 2, 3, 4, 6, 5, 7):
+        copies[n].start()
     odd = lax.axis_index("seq") % 2 == 1
 
     tokens, caps = id_rows.shape
@@ -92,7 +92,7 @@
         part = frames[r : r + step].astype(jnp.float32)
         scale = lax.rsqrt(jnp.mean(part * part, axis=-1, keepdims=True) + 1e-05)
         normed[r : r + step] = (part * scale * gain[...]).astype(jnp.bfloat16)
-    for n, k in enumerate((1, 2, 0)):
+    def project(n, k):
         copies[3 + n].wait()
         both = jnp.dot(normed[...], w[k], preferred_element_type=jnp.float32).astype(jnp.bfloat16)
         if k == 0:
@@ -105,6 +105,8 @@
             p2_ref[(k - 1) * rows : k * rows] = mine
             p3_ref[(k - 1) * rows : k * rows] = other
 
+    project(0, 1)
+    project(1, 2)
     copies[6].wait()
     copies[7].wait()
     part = jnp.dot(counts, table[...], preferred_element_type=jnp.float32)
@@ -122,19 +124,23 @@
         p1_ref[3 * rows + c * caps : 3 * rows + (c + 1) * caps] = chunk.astype(jnp.bfloat16)
     t32_ref[sums:] = bounds
     p1_ref[3 * rows + sums :] = bounds.astype(jnp.bfloat16)
+    project(2, 0)
 
 
 def weights_kernel(frames_ref, w_out_ref, w_proj_ref, wc_ref, fp_ref):
-    half = wc_ref.shape[0]
+    half = wc_ref.shape[0] // 2
     cols = w_out_ref.shape[0]
     blocks = fp_ref.shape[0]
     odd = lax.axis_index("seq") % 2
     start = pl.multiple_of(lax.axis_index("head") * cols, LANES)
-    wc_ref[...] = jnp.dot(
+    product = jnp.dot(
         w_out_ref[pl.ds(pl.multiple_of(odd * half, half), half), :],
         w_proj_ref[...],
         preferred_element_type=jnp.float32,
     )
+    high = product.astype(jnp.bfloat16)
+    wc_ref[:half] = high
+    wc_ref[half:] = (product - high.astype(jnp.float32)).astype(jnp.bfloat16)
     features = frames_ref[:, pl.ds(start, cols)].astype(jnp.float32)
     sums = jnp.sum(features.reshape(blocks, BLK, cols), axis=1)
     padded = jnp.concatenate([sums, jnp.zeros((SUB - blocks, cols), jnp.float32)], axis=0)
@@ -187,7 +193,14 @@
     first = jnp.where(odd == 0, here, there)
     second = jnp.where(odd == 0, there, here)
     blank = jnp.zeros((SUB - 2 * blocks, half), jnp.float32)
-    table = jnp.dot(jnp.concatenate([first, second, blank], axis=0), wc_ref[...], precision=HIGHEST)
+    sums = jnp.concatenate([first, second, blank], axis=0)
+    high = sums.astype(jnp.bfloat16)
+    low = (sums - high.astype(jnp.float32)).astype(jnp.bfloat16)
+    both = jnp.concatenate([high, low], axis=0)
+    table = jnp.dot(both, wc_ref[:half], preferred_element_type=jnp.float32)
+    table = table[:SUB] + table[SUB:] + jnp.dot(
+        high, wc_ref[half:], preferred_element_type=jnp.float32
+    )
     feature = fp_ref[...]
     none = jnp.zeros_like(feature)
     table = table[: 2 * blocks] + jnp.concatenate(
@@ -326,11 +339,12 @@
         return mine, mine.astype(bf16)
 
     mine, sent = add(mine, r1[3 * rows :])
+    mine, sent = add(mine, swap(sent, 0, 1))
     got = swap(sent, 2, 0)
 
     wc, fp = call(
         weights_kernel,
-        [shape((half, E), f32), shape((blocks, E), f32)],
+        [shape((2 * half, E), bf16), shape((blocks, E), f32)],
         [VMEM] * 3,
         cost=(10**10, 2 * (w_proj.size + w_out.size + frames.size), 0),
     )(frames, w_out, w_proj)
@@ -349,7 +363,7 @@
         mine, sent = add(mine, swap(sent, step, 0))
         step *= 2
     everyone = lax.all_to_all(piece, EVERY, 0, 0)
-    gots = [swap(sent, 0, k) for k in range(1, head_count)]
+    gots = [swap(sent, 0, k) for k in range(2, head_count, 2)]
 
     captions, masks = call(
         functools.partial(caption_kernel, 2 * head_count, 4 * blocks),
@@ -357,7 +371,7 @@
             shape((token_ids.shape[0], E), bf16),
             shape((2 * token_ids.shape[0], devices * 4 * blocks), bf16),
         ],
-        [VMEM] * head_count,
+        [VMEM] * (1 + len(gots)),
     )(mine, *gots)
     derivative, loss = call(
         tail_kernel,

time: 36.2 us -> 35.9 us (level)
  starting transfers between devices: 16.5 us -> 15.6 us
  waiting for transfers between devices: 9.76 us -> 10.6 us
    all_to_all x1, waiting for transfers between devices: 0.99 us -> 3.04 us  [local(): everyone = lax.all_to_all(piece, EVERY, 0, 0)]
    ppermute x5 -> x4, waiting for transfers between devices: 4.9 us -> 3.17 us  [swap(): return lax.ppermute(sent, EVERY, list(enumerate(to)))]
    ppermute x5 -> x4, starting transfers between devices: 7.82 us -> 6.88 us  [swap(): return lax.ppermute(sent, EVERY, list(enumerate(to)))]
    ppermute x1, waiting for transfers between devices: 3.86 us -> 4.43 us  [local(): r1 = lax.ppermute(p1, 'seq', [(s, s ^ 1) for s in range(seq_count)])]
  transfers between devices with their start and end apart: 9 -> 8, of which waited for: 5 -> 4; matrix products, arithmetic and copies ran while one was open for 0% -> 0% of each run, Pallas kernels for 9% -> 9%
where the time goes in v9:
time: 35.9 us; the launch traced here: 35.7 us
  starting transfers between devices  15.6 us (43%)
  waiting for transfers between devices  10.6 us (30%)
  Pallas kernels  7.9 us (22%)
  between operations  1.41 us (4%)
    ppermute x4, starting transfers between devices, swap(): return lax.ppermute(sent, EVERY, list(enumerate(to)))  6.88 us
    ppermute x1, waiting for transfers between devices, local(): r1 = lax.ppermute(p1, 'seq', [(s, s ^ 1) for s in range(seq_count)])  4.43 us
    all_to_all x1, starting transfers between devices, local(): everyone = lax.all_to_all(piece, EVERY, 0, 0)  3.76 us
    pallas_call x1, Pallas kernels, local(): call(first_kernel, [shape((n, half), bf16) for n in (3 * rows, 3 * rows +...  3.26 us
    ppermute x4, waiting for transfers between devices, swap(): return lax.ppermute(sent, EVERY, list(enumerate(to)))  3.17 us
    all_to_all x1, waiting for transfers between devices, local(): everyone = lax.all_to_all(piece, EVERY, 0, 0)  3.04 us
    ppermute x1, starting transfers between devices, local(): r1 = lax.ppermute(p1, 'seq', [(s, s ^ 1) for s in range(seq_count)])  3 us
    pallas_call x1, Pallas kernels, local(): call(attend_kernel, shape((devices, 4 * blocks, E // 2), PIECE), [VMEM] *...  2.6 us
  transfers between devices with their start and end apart: 8, of which 4 were waited for; matrix products, arithmetic and copies ran while one was open for 0% of the time, Pallas kernels for 9%

profile of v9, /device:TPU:0, one launch (start us, length us, event | category | flops | bytes accessed | tf_op | source)
XLA Modules:
  0.0 35.7 jit_solution(461414341333825636)
XLA Ops:
  0.6 0.0 copy-start
  0.6 0.0 copy-start.1
  0.7 0.0 copy-start.2
  0.7 3.3 %shard_map.104 = (bf16[768,128]{1,0:T(8,128)(2,1)S(1)}, bf16[1040,128]{1,0:T(8,128)(2,1)S(1)}, bf16[512,128]{1,0:T(8,128)(2,1)S(1)}, bf16[512,128]{1,0:T(8,128)(2,1)S(1)}, f32[272,128]{1,0:T(8,128)S(1)}) custom-call(bf16[256,1024]{1,0:T(8,128)(2,1)} %frames_ref.1, f32[1,1024]{1,0:T(1,128)} %bitcast.4, bf16[3,1024,256]{2,1,0:T(8,128)(2,1)} %w_hbm.1, ...), custom_call_target="tpu_custom_call" | custom-call | flops 402653184 | bytes 1572864 | tf_op jit(solution)/shard_map/pallas_call | solution.py:303
  3.9 3.0 %collective-permute-start = (bf16[1040,128]{1,0:T(8,128)(2,1)S(1)}, bf16[1040,128]{1,0:T(8,128)(2,1)S(1)}, u32[]{:S(2)}, u32[]{:S(2)}) collective-permute-start(bf16[1040,128]{1,0:T(8,128)(2,1)S(1)} %get-tuple-element.16), channel_id=1, source_target_pairs={{0,4},{4,0},{8,12},{12,8},{16,20},{20,16},{24,28},{28,24},{1,5},{5... | collective-permute-start | bytes 798728 | tf_op jit(solution)/shard_map/ppermute | solution.py:316
  6.9 1.3 %collective-permute-start.3 = (bf16[512,128]{1,0:T(8,128)(2,1)S(1)}, bf16[512,128]{1,0:T(8,128)(2,1)S(1)}, u32[]{:S(2)}, u32[]{:S(2)}) collective-permute-start(bf16[512,128]{1,0:T(8,128)(2,1)S(1)} %get-tuple-element.18), channel_id=1, source_target_pairs={{4,12},{12,20},{20,28},{8,0},{16,8},{24,16},{5,13},{13,21},{21,29}... | collective-permute-start | bytes 393224 | tf_op jit(solution)/shard_map/ppermute | solution.py:322
  8.2 0.7 %collective-permute-start.4 = (bf16[512,128]{1,0:T(8,128)(2,1)S(1)}, bf16[512,128]{1,0:T(8,128)(2,1)S(1)}, u32[]{:S(2)}, u32[]{:S(2)}) collective-permute-start(bf16[512,128]{1,0:T(8,128)(2,1)S(1)} %get-tuple-element.19), channel_id=1, source_target_pairs={{4,8},{12,16},{20,24},{8,4},{16,12},{24,20},{5,9},{13,17},{21,25},... | collective-permute-start | bytes 393224 | tf_op jit(solution)/shard_map/ppermute | solution.py:317
  8.9 4.4 %collective-permute-done.r1_ref = bf16[1040,128]{1,0:T(8,128)(2,1)S(1)} collective-permute-done((bf16[1040,128]{1,0:T(8,128)(2,1)S(1)}, bf16[1040,128]{1,0:T(8,128)(2,1)S(1)}, u32[]{:S(2)}, u32[]{:S(2)}) %collective-permute-start) | collective-permute-done | bytes 266272 | tf_op jit(solution)/shard_map/ppermute | solution.py:316
  13.3 0.1 collective-permute-start.1
  13.4 0.0 copy-done
  13.4 0.0 copy-done.1
  13.4 0.0 copy-done.2
  13.5 0.5 %shard_map.105 = (bf16[256,512]{1,0:T(8,128)(2,1)S(1)}, f32[2,512]{1,0:T(2,128)S(1)}) custom-call(bf16[256,1024]{1,0:T(8,128)(2,1)S(1)} %copy-done, bf16[256,1024]{1,0:T(8,128)(2,1)S(1)} %copy-done.2, bf16[1024,512]{1,0:T(8,128)(2,1)S(1)} %copy-done.1), custom_call_target="tpu_custom_call" | custom-call | flops 10000000000 | bytes 2097152 | tf_op jit(solution)/shard_map/pallas_call | solution.py:345
  14.0 0.7 %collective-permute-done.1 = bf16[272,128]{1,0:T(8,128)(2,1)S(1)} collective-permute-done((bf16[272,128]{1,0:T(8,128)(2,1)S(1)}, bf16[272,128]{1,0:T(8,128)(2,1)S(1)}, u32[]{:S(2)}, u32[]{:S(2)}) %collective-permute-start.1) | collective-permute-done | bytes 69664 | tf_op jit(solution)/shard_map/ppermute | solution.py:334
  14.7 1.9 %collective-permute-start.2 = (bf16[272,128]{1,0:T(8,128)(2,1)S(1)}, bf16[272,128]{1,0:T(8,128)(2,1)S(1)}, u32[]{:S(2)}, u32[]{:S(2)}) collective-permute-start(bf16[272,128]{1,0:T(8,128)(2,1)S(1)} %fusion.2), channel_id=1, source_target_pairs={{0,8},{1,9},{2,10},{3,11},{4,12},{5,13},{6,14},{7,15},{8,0},{9,1},... | collective-permute-start | bytes 208904 | tf_op jit(solution)/shard_map/ppermute | solution.py:334
  16.6 0.0 collective-permute-done.3.r2_ref
  16.6 0.0 collective-permute-done.4.r3_ref
  16.6 2.6 %shard_map.106 = bf16[32,8,256]{2,1,0:T(8,128)(2,1)} custom-call(bf16[768,128]{1,0:T(8,128)(2,1)S(1)} %get-tuple-element.17.own_ref, bf16[1040,128]{1,0:T(8,128)(2,1)S(1)} %collective-permute-done.r1_ref, bf16[512,128]{1,0:T(8,128)(2,1)S(1)} %collective-permute-done.3.r2_ref, bf16[512,128]{1,0:T(8,128)(2,1)S(1)} %collective-permute-done.4.r3_ref, ...), custom_call_target="tpu_custom_call" | custom-call | flops 10000000000 | bytes 655360 | tf_op jit(solution)/shard_map/pallas_call | solution.py:352
  19.2 0.0 collective-permute-done.2
  19.3 3.1 %collective-permute-start.5 = (bf16[272,128]{1,0:T(8,128)(2,1)S(1)}, bf16[272,128]{1,0:T(8,128)(2,1)S(1)}, u32[]{:S(2)}, u32[]{:S(2)}) collective-permute-start(bf16[272,128]{1,0:T(8,128)(2,1)S(1)} %fusion.1), channel_id=1, source_target_pairs={{0,16},{1,17},{2,18},{3,19},{4,20},{5,21},{6,22},{7,23},{8,24},{9,... | collective-permute-start | bytes 208904 | tf_op jit(solution)/shard_map/ppermute | solution.py:334
  22.3 3.8 %all-to-all-start = ((bf16[32,8,256]{2,1,0:T(8,128)(2,1)}), bf16[32,8,256]{2,1,0:T(8,128)(2,1)S(1)}, u32[]{:S(2)}, u32[]{:S(2)}) async-start(bf16[32,8,256]{2,1,0:T(8,128)(2,1)} %shard_map.106), calls=%async_computation | async-start | bytes 262144 | tf_op jit(solution)/shard_map/all_to_all | solution.py:365
  26.1 0.0 collective-permute-done.5
  26.1 0.1 fusion.3
  26.2 1.8 %collective-permute-start.6 = (bf16[272,128]{1,0:T(8,128)(2,1)S(1)}, bf16[272,128]{1,0:T(8,128)(2,1)S(1)}, u32[]{:S(2)}, u32[]{:S(2)}) collective-permute-start(bf16[272,128]{1,0:T(8,128)(2,1)S(1)} %get-tuple-element.28), channel_id=1, source_target_pairs={{0,2},{1,3},{2,0},{3,1},{4,6},{5,7},{6,4},{7,5},{8,10},{9,11},{10,... | collective-permute-start | bytes 208904 | tf_op jit(solution)/shard_map/ppermute | solution.py:334
  28.7 2.5 %collective-permute-done.6.refs_0_ = bf16[272,128]{1,0:T(8,128)(2,1)S(1)} collective-permute-done((bf16[272,128]{1,0:T(8,128)(2,1)S(1)}, bf16[272,128]{1,0:T(8,128)(2,1)S(1)}, u32[]{:S(2)}, u32[]{:S(2)}) %collective-permute-start.6) | collective-permute-done | bytes 69664 | tf_op jit(solution)/shard_map/ppermute | solution.py:334
  31.2 0.1 shard_map.107
  31.3 3.0 %all-to-all-done.everyone_ref = bf16[32,8,256]{2,1,0:T(8,128)(2,1)S(1)} async-done(((bf16[32,8,256]{2,1,0:T(8,128)(2,1)}), bf16[32,8,256]{2,1,0:T(8,128)(2,1)S(1)}, u32[]{:S(2)}, u32[]{:S(2)}) %all-to-all-start) | async-done | bytes 131104 | tf_op jit(solution)/shard_map/all_to_all | solution.py:365
  34.3 1.4 %shard_map.108 = (f32[2,512]{1,0:T(2,128)}, f32[1,2]{1,0:T(1,128)}) custom-call(bf16[32,8,256]{2,1,0:T(8,128)(2,1)S(1)} %all-to-all-done.everyone_ref, bf16[64,512]{1,0:T(8,128)(2,1)S(1)} %get-tuple-element.24.captions_ref, bf16[128,256]{1,0:T(8,128)(2,1)S(1)} %get-tuple-element.25.masks_ref, f32[1]{0:T(128)S(6)} %copy.11.divisor_ref), custom_call_target="tpu_custom_call" | custom-call | flops 8388608 | bytes 131072 | tf_op jit(solution)/shard_map/pallas_call | solution.py:376
  (3 shorter events, 0.1 us)
Async XLA Ops:
  0.6 12.8 %copy-start = (bf16[256,1024]{1,0:T(8,128)(2,1)S(1)}, bf16[256,1024]{1,0:T(8,128)(2,1)}, u32[]{:S(2)}) copy-start(bf16[256,1024]{1,0:T(8,128)(2,1)} %frames_ref.1) | copy-start | bytes 1572868
  0.6 12.8 %copy-start.1 = (bf16[1024,512]{1,0:T(8,128)(2,1)S(1)}, bf16[1024,512]{1,0:T(8,128)(2,1)}, u32[]{:S(2)}) copy-start(bf16[1024,512]{1,0:T(8,128)(2,1)} %w_proj_ref.1) | copy-start | bytes 3145732
  0.7 12.8 %copy-start.2 = (bf16[256,1024]{1,0:T(8,128)(2,1)S(1)}, bf16[256,1024]{1,0:T(8,128)(2,1)}, u32[]{:S(2)}) copy-start(bf16[256,1024]{1,0:T(8,128)(2,1)} %w_out_ref.1) | copy-start | bytes 1572868
  3.9 9.4 %collective-permute-start = (bf16[1040,128]{1,0:T(8,128)(2,1)S(1)}, bf16[1040,128]{1,0:T(8,128)(2,1)S(1)}, u32[]{:S(2)}, u32[]{:S(2)}) collective-permute-start(bf16[1040,128]{1,0:T(8,128)(2,1)S(1)} %get-tuple-element.16), channel_id=1, source_target_pairs={{0,4},{4,0},{8,12},{12,8},{16,20},{20,16},{24,28},{28,24},{1,5},{5... | collective-permute-start | bytes 798728 | tf_op jit(solution)/shard_map/ppermute | solution.py:316
  6.9 9.7 %collective-permute-start.3 = (bf16[512,128]{1,0:T(8,128)(2,1)S(1)}, bf16[512,128]{1,0:T(8,128)(2,1)S(1)}, u32[]{:S(2)}, u32[]{:S(2)}) collective-permute-start(bf16[512,128]{1,0:T(8,128)(2,1)S(1)} %get-tuple-element.18), channel_id=1, source_target_pairs={{4,12},{12,20},{20,28},{8,0},{16,8},{24,16},{5,13},{13,21},{21,29}... | collective-permute-start | bytes 393224 | tf_op jit(solution)/shard_map/ppermute | solution.py:322
  8.2 8.4 %collective-permute-start.4 = (bf16[512,128]{1,0:T(8,128)(2,1)S(1)}, bf16[512,128]{1,0:T(8,128)(2,1)S(1)}, u32[]{:S(2)}, u32[]{:S(2)}) collective-permute-start(bf16[512,128]{1,0:T(8,128)(2,1)S(1)} %get-tuple-element.19), channel_id=1, source_target_pairs={{4,8},{12,16},{20,24},{8,4},{16,12},{24,20},{5,9},{13,17},{21,25},... | collective-permute-start | bytes 393224 | tf_op jit(solution)/shard_map/ppermute | solution.py:317
  13.3 1.3 %collective-permute-start.1 = (bf16[272,128]{1,0:T(8,128)(2,1)S(1)}, bf16[272,128]{1,0:T(8,128)(2,1)S(1)}, u32[]{:S(2)}, u32[]{:S(2)}) collective-permute-start(bf16[272,128]{1,0:T(8,128)(2,1)S(1)} %fusion), channel_id=1, source_target_pairs={{0,1},{1,0},{2,3},{3,2},{4,5},{5,4},{6,7},{7,6},{8,9},{9,8},{10,11... | collective-permute-start | bytes 208904 | tf_op jit(solution)/shard_map/ppermute | solution.py:334
  14.7 4.5 %collective-permute-start.2 = (bf16[272,128]{1,0:T(8,128)(2,1)S(1)}, bf16[272,128]{1,0:T(8,128)(2,1)S(1)}, u32[]{:S(2)}, u32[]{:S(2)}) collective-permute-start(bf16[272,128]{1,0:T(8,128)(2,1)S(1)} %fusion.2), channel_id=1, source_target_pairs={{0,8},{1,9},{2,10},{3,11},{4,12},{5,13},{6,14},{7,15},{8,0},{9,1},... | collective-permute-start | bytes 208904 | tf_op jit(solution)/shard_map/ppermute | solution.py:334
  19.3 6.9 %collective-permute-start.5 = (bf16[272,128]{1,0:T(8,128)(2,1)S(1)}, bf16[272,128]{1,0:T(8,128)(2,1)S(1)}, u32[]{:S(2)}, u32[]{:S(2)}) collective-permute-start(bf16[272,128]{1,0:T(8,128)(2,1)S(1)} %fusion.1), channel_id=1, source_target_pairs={{0,16},{1,17},{2,18},{3,19},{4,20},{5,21},{6,22},{7,23},{8,24},{9,... | collective-permute-start | bytes 208904 | tf_op jit(solution)/shard_map/ppermute | solution.py:334
  22.3 12.0 %all-to-all-start = ((bf16[32,8,256]{2,1,0:T(8,128)(2,1)}), bf16[32,8,256]{2,1,0:T(8,128)(2,1)S(1)}, u32[]{:S(2)}, u32[]{:S(2)}) async-start(bf16[32,8,256]{2,1,0:T(8,128)(2,1)} %shard_map.106), calls=%async_computation | async-start | bytes 262144 | tf_op jit(solution)/shard_map/all_to_all | solution.py:365
  26.2 5.0 %collective-permute-start.6 = (bf16[272,128]{1,0:T(8,128)(2,1)S(1)}, bf16[272,128]{1,0:T(8,128)(2,1)S(1)}, u32[]{:S(2)}, u32[]{:S(2)}) collective-permute-start(bf16[272,128]{1,0:T(8,128)(2,1)S(1)} %get-tuple-element.28), channel_id=1, source_target_pairs={{0,2},{1,3},{2,0},{3,1},{4,6},{5,7},{6,4},{7,5},{8,10},{9,11},{10,... | collective-permute-start | bytes 208904 | tf_op jit(solution)/shard_map/ppermute | solution.py:334

commit v10 on v9

--- a/solution.py
+++ b/solution.py
@@ -238,7 +238,8 @@
     lower, upper = column(0), column(1)
     place = lax.broadcasted_iota(jnp.int32, (caps, masks_ref.shape[1]), 1)
     inner = place % width
-    block = (place // (width * group) * blocks + inner % blocks).astype(jnp.float32)
+    pair = masks_ref.shape[1] // (width * group) - 1 - place // (width * group)
+    block = (pair * blocks + inner % blocks).astype(jnp.float32)
     inside = jnp.where((block >= lower) & (block < upper), 1.0, 0.0)
     for side in range(2):
         masks_ref[side * caps : (side + 1) * caps] = jnp.where(
@@ -362,7 +363,8 @@
     while step < seq_count:
         mine, sent = add(mine, swap(sent, step, 0))
         step *= 2
-    everyone = lax.all_to_all(piece, EVERY, 0, 0)
+    backward = list(range(devices))[::-1]
+    everyone = lax.all_to_all(piece, EVERY, 0, 0, axis_index_groups=[backward])
     gots = [swap(sent, 0, k) for k in range(2, head_count, 2)]
 
     captions, masks = call(

time: 35.9 us -> 35.6 us (level)
  no operation moved by 1% of the time
where the time goes in v10:
time: 35.6 us; the launch traced here: 35.4 us
  starting transfers between devices  15.6 us (44%)
  waiting for transfers between devices  10.3 us (29%)
  Pallas kernels  7.9 us (22%)
  between operations  1.41 us (4%)
    ppermute x4, starting transfers between devices, swap(): return lax.ppermute(sent, EVERY, list(enumerate(to)))  6.88 us
    ppermute x1, waiting for transfers between devices, local(): r1 = lax.ppermute(p1, 'seq', [(s, s ^ 1) for s in range(seq_count)])  4.43 us
    all_to_all x1, starting transfers between devices, local(): everyone = lax.all_to_all(piece, EVERY, 0, 0, axis_index_groups=[backward])  3.76 us
    pallas_call x1, Pallas kernels, local(): call(first_kernel, [shape((n, half), bf16) for n in (3 * rows, 3 * rows +...  3.26 us
    ppermute x4, waiting for transfers between devices, swap(): return lax.ppermute(sent, EVERY, list(enumerate(to)))  3.2 us
    ppermute x1, starting transfers between devices, local(): r1 = lax.ppermute(p1, 'seq', [(s, s ^ 1) for s in range(seq_count)])  3 us
    all_to_all x1, waiting for transfers between devices, local(): everyone = lax.all_to_all(piece, EVERY, 0, 0, axis_index_groups=[backward])  2.69 us
    pallas_call x1, Pallas kernels, local(): call(attend_kernel, shape((devices, 4 * blocks, E // 2), PIECE), [VMEM] *...  2.6 us
  transfers between devices with their start and end apart: 8, of which 4 were waited for; matrix products, arithmetic and copies ran while one was open for 0% of the time, Pallas kernels for 9%

profile of v10, /device:TPU:0, one launch (start us, length us, event | category | flops | bytes accessed | tf_op | source)
XLA Modules:
  0.0 35.4 jit_solution(3026907916677521718)
XLA Ops:
  0.6 0.0 copy-start
  0.6 0.0 copy-start.1
  0.7 0.0 copy-start.2
  0.7 3.3 %shard_map.104 = (bf16[768,128]{1,0:T(8,128)(2,1)S(1)}, bf16[1040,128]{1,0:T(8,128)(2,1)S(1)}, bf16[512,128]{1,0:T(8,128)(2,1)S(1)}, bf16[512,128]{1,0:T(8,128)(2,1)S(1)}, f32[272,128]{1,0:T(8,128)S(1)}) custom-call(bf16[256,1024]{1,0:T(8,128)(2,1)} %frames_ref.1, f32[1,1024]{1,0:T(1,128)} %bitcast.4, bf16[3,1024,256]{2,1,0:T(8,128)(2,1)} %w_hbm.1, ...), custom_call_target="tpu_custom_call" | custom-call | flops 402653184 | bytes 1572864 | tf_op jit(solution)/shard_map/pallas_call | solution.py:304
  3.9 3.0 %collective-permute-start = (bf16[1040,128]{1,0:T(8,128)(2,1)S(1)}, bf16[1040,128]{1,0:T(8,128)(2,1)S(1)}, u32[]{:S(2)}, u32[]{:S(2)}) collective-permute-start(bf16[1040,128]{1,0:T(8,128)(2,1)S(1)} %get-tuple-element.16), channel_id=1, source_target_pairs={{0,4},{4,0},{8,12},{12,8},{16,20},{20,16},{24,28},{28,24},{1,5},{5... | collective-permute-start | bytes 798728 | tf_op jit(solution)/shard_map/ppermute | solution.py:317
  6.9 1.3 %collective-permute-start.3 = (bf16[512,128]{1,0:T(8,128)(2,1)S(1)}, bf16[512,128]{1,0:T(8,128)(2,1)S(1)}, u32[]{:S(2)}, u32[]{:S(2)}) collective-permute-start(bf16[512,128]{1,0:T(8,128)(2,1)S(1)} %get-tuple-element.18), channel_id=1, source_target_pairs={{4,12},{12,20},{20,28},{8,0},{16,8},{24,16},{5,13},{13,21},{21,29}... | collective-permute-start | bytes 393224 | tf_op jit(solution)/shard_map/ppermute | solution.py:323
  8.2 0.7 %collective-permute-start.4 = (bf16[512,128]{1,0:T(8,128)(2,1)S(1)}, bf16[512,128]{1,0:T(8,128)(2,1)S(1)}, u32[]{:S(2)}, u32[]{:S(2)}) collective-permute-start(bf16[512,128]{1,0:T(8,128)(2,1)S(1)} %get-tuple-element.19), channel_id=1, source_target_pairs={{4,8},{12,16},{20,24},{8,4},{16,12},{24,20},{5,9},{13,17},{21,25},... | collective-permute-start | bytes 393224 | tf_op jit(solution)/shard_map/ppermute | solution.py:318
  8.9 4.4 %collective-permute-done.r1_ref = bf16[1040,128]{1,0:T(8,128)(2,1)S(1)} collective-permute-done((bf16[1040,128]{1,0:T(8,128)(2,1)S(1)}, bf16[1040,128]{1,0:T(8,128)(2,1)S(1)}, u32[]{:S(2)}, u32[]{:S(2)}) %collective-permute-start) | collective-permute-done | bytes 266272 | tf_op jit(solution)/shard_map/ppermute | solution.py:317
  13.3 0.1 collective-permute-start.1
  13.4 0.0 copy-done
  13.4 0.0 copy-done.1
  13.4 0.0 copy-done.2
  13.5 0.5 %shard_map.105 = (bf16[256,512]{1,0:T(8,128)(2,1)S(1)}, f32[2,512]{1,0:T(2,128)S(1)}) custom-call(bf16[256,1024]{1,0:T(8,128)(2,1)S(1)} %copy-done, bf16[256,1024]{1,0:T(8,128)(2,1)S(1)} %copy-done.2, bf16[1024,512]{1,0:T(8,128)(2,1)S(1)} %copy-done.1), custom_call_target="tpu_custom_call" | custom-call | flops 10000000000 | bytes 2097152 | tf_op jit(solution)/shard_map/pallas_call | solution.py:346
  14.0 0.7 %collective-permute-done.1 = bf16[272,128]{1,0:T(8,128)(2,1)S(1)} collective-permute-done((bf16[272,128]{1,0:T(8,128)(2,1)S(1)}, bf16[272,128]{1,0:T(8,128)(2,1)S(1)}, u32[]{:S(2)}, u32[]{:S(2)}) %collective-permute-start.1) | collective-permute-done | bytes 69664 | tf_op jit(solution)/shard_map/ppermute | solution.py:335
  14.7 1.9 %collective-permute-start.2 = (bf16[272,128]{1,0:T(8,128)(2,1)S(1)}, bf16[272,128]{1,0:T(8,128)(2,1)S(1)}, u32[]{:S(2)}, u32[]{:S(2)}) collective-permute-start(bf16[272,128]{1,0:T(8,128)(2,1)S(1)} %fusion.2), channel_id=1, source_target_pairs={{0,8},{1,9},{2,10},{3,11},{4,12},{5,13},{6,14},{7,15},{8,0},{9,1},... | collective-permute-start | bytes 208904 | tf_op jit(solution)/shard_map/ppermute | solution.py:335
  16.6 0.0 collective-permute-done.3.r2_ref
  16.6 0.0 collective-permute-done.4.r3_ref
  16.6 2.6 %shard_map.106 = bf16[32,8,256]{2,1,0:T(8,128)(2,1)} custom-call(bf16[768,128]{1,0:T(8,128)(2,1)S(1)} %get-tuple-element.17.own_ref, bf16[1040,128]{1,0:T(8,128)(2,1)S(1)} %collective-permute-done.r1_ref, bf16[512,128]{1,0:T(8,128)(2,1)S(1)} %collective-permute-done.3.r2_ref, bf16[512,128]{1,0:T(8,128)(2,1)S(1)} %collective-permute-done.4.r3_ref, ...), custom_call_target="tpu_custom_call" | custom-call | flops 10000000000 | bytes 655360 | tf_op jit(solution)/shard_map/pallas_call | solution.py:353
  19.2 0.0 collective-permute-done.2
  19.3 3.1 %collective-permute-start.5 = (bf16[272,128]{1,0:T(8,128)(2,1)S(1)}, bf16[272,128]{1,0:T(8,128)(2,1)S(1)}, u32[]{:S(2)}, u32[]{:S(2)}) collective-permute-start(bf16[272,128]{1,0:T(8,128)(2,1)S(1)} %fusion.1), channel_id=1, source_target_pairs={{0,16},{1,17},{2,18},{3,19},{4,20},{5,21},{6,22},{7,23},{8,24},{9,... | collective-permute-start | bytes 208904 | tf_op jit(solution)/shard_map/ppermute | solution.py:335
  22.3 3.8 %all-to-all-start = ((bf16[32,8,256]{2,1,0:T(8,128)(2,1)}), bf16[32,8,256]{2,1,0:T(8,128)(2,1)S(1)}, u32[]{:S(2)}, u32[]{:S(2)}) async-start(bf16[32,8,256]{2,1,0:T(8,128)(2,1)} %shard_map.106), calls=%async_computation | async-start | bytes 262144 | tf_op jit(solution)/shard_map/all_to_all | solution.py:367
  26.1 0.0 collective-permute-done.5
  26.1 0.1 fusion.3
  26.2 1.8 %collective-permute-start.6 = (bf16[272,128]{1,0:T(8,128)(2,1)S(1)}, bf16[272,128]{1,0:T(8,128)(2,1)S(1)}, u32[]{:S(2)}, u32[]{:S(2)}) collective-permute-start(bf16[272,128]{1,0:T(8,128)(2,1)S(1)} %get-tuple-element.28), channel_id=1, source_target_pairs={{0,2},{1,3},{2,0},{3,1},{4,6},{5,7},{6,4},{7,5},{8,10},{9,11},{10,... | collective-permute-start | bytes 208904 | tf_op jit(solution)/shard_map/ppermute | solution.py:335
  28.7 2.5 %collective-permute-done.6.refs_0_ = bf16[272,128]{1,0:T(8,128)(2,1)S(1)} collective-permute-done((bf16[272,128]{1,0:T(8,128)(2,1)S(1)}, bf16[272,128]{1,0:T(8,128)(2,1)S(1)}, u32[]{:S(2)}, u32[]{:S(2)}) %collective-permute-start.6) | collective-permute-done | bytes 69664 | tf_op jit(solution)/shard_map/ppermute | solution.py:335
  31.2 0.1 shard_map.107
  31.3 2.7 %all-to-all-done.everyone_ref = bf16[32,8,256]{2,1,0:T(8,128)(2,1)S(1)} async-done(((bf16[32,8,256]{2,1,0:T(8,128)(2,1)}), bf16[32,8,256]{2,1,0:T(8,128)(2,1)S(1)}, u32[]{:S(2)}, u32[]{:S(2)}) %all-to-all-start) | async-done | bytes 131104 | tf_op jit(solution)/shard_map/all_to_all | solution.py:367
  34.0 1.4 %shard_map.108 = (f32[2,512]{1,0:T(2,128)}, f32[1,2]{1,0:T(1,128)}) custom-call(bf16[32,8,256]{2,1,0:T(8,128)(2,1)S(1)} %all-to-all-done.everyone_ref, bf16[64,512]{1,0:T(8,128)(2,1)S(1)} %get-tuple-element.24.captions_ref, bf16[128,256]{1,0:T(8,128)(2,1)S(1)} %get-tuple-element.25.masks_ref, f32[1]{0:T(128)S(6)} %copy.11.divisor_ref), custom_call_target="tpu_custom_call" | custom-call | flops 8388608 | bytes 131072 | tf_op jit(solution)/shard_map/pallas_call | solution.py:378
  (3 shorter events, 0.1 us)
Async XLA Ops:
  0.6 12.8 %copy-start = (bf16[256,1024]{1,0:T(8,128)(2,1)S(1)}, bf16[256,1024]{1,0:T(8,128)(2,1)}, u32[]{:S(2)}) copy-start(bf16[256,1024]{1,0:T(8,128)(2,1)} %frames_ref.1) | copy-start | bytes 1572868
  0.6 12.8 %copy-start.1 = (bf16[1024,512]{1,0:T(8,128)(2,1)S(1)}, bf16[1024,512]{1,0:T(8,128)(2,1)}, u32[]{:S(2)}) copy-start(bf16[1024,512]{1,0:T(8,128)(2,1)} %w_proj_ref.1) | copy-start | bytes 3145732
  0.7 12.8 %copy-start.2 = (bf16[256,1024]{1,0:T(8,128)(2,1)S(1)}, bf16[256,1024]{1,0:T(8,128)(2,1)}, u32[]{:S(2)}) copy-start(bf16[256,1024]{1,0:T(8,128)(2,1)} %w_out_ref.1) | copy-start | bytes 1572868
  3.9 9.4 %collective-permute-start = (bf16[1040,128]{1,0:T(8,128)(2,1)S(1)}, bf16[1040,128]{1,0:T(8,128)(2,1)S(1)}, u32[]{:S(2)}, u32[]{:S(2)}) collective-permute-start(bf16[1040,128]{1,0:T(8,128)(2,1)S(1)} %get-tuple-element.16), channel_id=1, source_target_pairs={{0,4},{4,0},{8,12},{12,8},{16,20},{20,16},{24,28},{28,24},{1,5},{5... | collective-permute-start | bytes 798728 | tf_op jit(solution)/shard_map/ppermute | solution.py:317
  6.9 9.7 %collective-permute-start.3 = (bf16[512,128]{1,0:T(8,128)(2,1)S(1)}, bf16[512,128]{1,0:T(8,128)(2,1)S(1)}, u32[]{:S(2)}, u32[]{:S(2)}) collective-permute-start(bf16[512,128]{1,0:T(8,128)(2,1)S(1)} %get-tuple-element.18), channel_id=1, source_target_pairs={{4,12},{12,20},{20,28},{8,0},{16,8},{24,16},{5,13},{13,21},{21,29}... | collective-permute-start | bytes 393224 | tf_op jit(solution)/shard_map/ppermute | solution.py:323
  8.2 8.4 %collective-permute-start.4 = (bf16[512,128]{1,0:T(8,128)(2,1)S(1)}, bf16[512,128]{1,0:T(8,128)(2,1)S(1)}, u32[]{:S(2)}, u32[]{:S(2)}) collective-permute-start(bf16[512,128]{1,0:T(8,128)(2,1)S(1)} %get-tuple-element.19), channel_id=1, source_target_pairs={{4,8},{12,16},{20,24},{8,4},{16,12},{24,20},{5,9},{13,17},{21,25},... | collective-permute-start | bytes 393224 | tf_op jit(solution)/shard_map/ppermute | solution.py:318
  13.3 1.3 %collective-permute-start.1 = (bf16[272,128]{1,0:T(8,128)(2,1)S(1)}, bf16[272,128]{1,0:T(8,128)(2,1)S(1)}, u32[]{:S(2)}, u32[]{:S(2)}) collective-permute-start(bf16[272,128]{1,0:T(8,128)(2,1)S(1)} %fusion), channel_id=1, source_target_pairs={{0,1},{1,0},{2,3},{3,2},{4,5},{5,4},{6,7},{7,6},{8,9},{9,8},{10,11... | collective-permute-start | bytes 208904 | tf_op jit(solution)/shard_map/ppermute | solution.py:335
  14.7 4.5 %collective-permute-start.2 = (bf16[272,128]{1,0:T(8,128)(2,1)S(1)}, bf16[272,128]{1,0:T(8,128)(2,1)S(1)}, u32[]{:S(2)}, u32[]{:S(2)}) collective-permute-start(bf16[272,128]{1,0:T(8,128)(2,1)S(1)} %fusion.2), channel_id=1, source_target_pairs={{0,8},{1,9},{2,10},{3,11},{4,12},{5,13},{6,14},{7,15},{8,0},{9,1},... | collective-permute-start | bytes 208904 | tf_op jit(solution)/shard_map/ppermute | solution.py:335
  19.3 6.9 %collective-permute-start.5 = (bf16[272,128]{1,0:T(8,128)(2,1)S(1)}, bf16[272,128]{1,0:T(8,128)(2,1)S(1)}, u32[]{:S(2)}, u32[]{:S(2)}) collective-permute-start(bf16[272,128]{1,0:T(8,128)(2,1)S(1)} %fusion.1), channel_id=1, source_target_pairs={{0,16},{1,17},{2,18},{3,19},{4,20},{5,21},{6,22},{7,23},{8,24},{9,... | collective-permute-start | bytes 208904 | tf_op jit(solution)/shard_map/ppermute | solution.py:335
  22.3 11.7 %all-to-all-start = ((bf16[32,8,256]{2,1,0:T(8,128)(2,1)}), bf16[32,8,256]{2,1,0:T(8,128)(2,1)S(1)}, u32[]{:S(2)}, u32[]{:S(2)}) async-start(bf16[32,8,256]{2,1,0:T(8,128)(2,1)} %shard_map.106), calls=%async_computation | async-start | bytes 262144 | tf_op jit(solution)/shard_map/all_to_all | solution.py:367
  26.2 5.0 %collective-permute-start.6 = (bf16[272,128]{1,0:T(8,128)(2,1)S(1)}, bf16[272,128]{1,0:T(8,128)(2,1)S(1)}, u32[]{:S(2)}, u32[]{:S(2)}) collective-permute-start(bf16[272,128]{1,0:T(8,128)(2,1)S(1)} %get-tuple-element.28), channel_id=1, source_target_pairs={{0,2},{1,3},{2,0},{3,1},{4,6},{5,7},{6,4},{7,5},{8,10},{9,11},{10,... | collective-permute-start | bytes 208904 | tf_op jit(solution)/shard_map/ppermute | solution.py:335

commit v11 on v10

--- a/solution.py
+++ b/solution.py
@@ -155,9 +155,11 @@
     blocks = rows // BLK
     seq, last = lax.axis_index("seq"), lax.axis_size("seq") - 1
     odd = seq % 2
+    heads = half // HDIM
     apart = lax.broadcasted_iota(jnp.int32, (rows, rows), 0) - lax.broadcasted_iota(
         jnp.int32, (rows, rows), 1
     )
+    apart = jnp.concatenate([apart] * heads, axis=0)
     lane = lax.broadcasted_iota(jnp.int32, (rows, half), 1)
 
     def block_sums(me, other, halo, parity, exists):
@@ -165,24 +167,30 @@
         near = side >= 0
         far = side <= jnp.where(exists, 0, -2 * rows)
         query = me[0:rows]
-        attended = jnp.zeros((rows, half), jnp.float32)
-        for head in range(half // HDIM):
-            mine = lane // HDIM == head
-            q = jnp.where(mine, query, jnp.zeros_like(query))
-            scores = [
-                transposed_dot(q, me[rows : 2 * rows]),
-                jnp.where(near, transposed_dot(q, other[rows : 2 * rows]), NEVER),
-                jnp.where(far, transposed_dot(q, halo[0:rows]), NEVER),
-            ]
-            top = functools.reduce(jnp.maximum, [jnp.max(s, axis=1, keepdims=True) for s in scores])
-            probs = [jnp.exp(s - top) for s in scores]
-            denom = sum(jnp.sum(p, axis=1, keepdims=True) for p in probs)
-            values = (me[2 * rows : 3 * rows], other[2 * rows : 3 * rows], halo[rows : 2 * rows])
-            mixed = sum(
-                jnp.dot(p.astype(jnp.bfloat16), v, preferred_element_type=jnp.float32)
-                for p, v in zip(probs, values)
+        blank = jnp.zeros_like(query)
+        q = jnp.concatenate(
+            [jnp.where(lane // HDIM == head, query, blank) for head in range(heads)], axis=0
+        )
+        scores = [
+            transposed_dot(q, me[rows : 2 * rows]),
+            jnp.where(near, transposed_dot(q, other[rows : 2 * rows]), NEVER),
+            jnp.where(far, transposed_dot(q, halo[0:rows]), NEVER),
+        ]
+        top = jnp.max(functools.reduce(jnp.maximum, scores), axis=1, keepdims=True)
+        probs = [jnp.exp(s - top) for s in scores]
+        denom = jnp.sum(sum(probs), axis=1, keepdims=True)
+        values = (me[2 * rows : 3 * rows], other[2 * rows : 3 * rows], halo[rows : 2 * rows])
+        mixed = jnp.dot(
+            jnp.concatenate([p.astype(jnp.bfloat16) for p in probs], axis=1),
+            jnp.concatenate(values, axis=0),
+            preferred_element_type=jnp.float32,
+        )
+        mixed = mixed * (1.0 / denom)
+        attended = mixed[:rows]
+        for head in range(1, heads):
+            attended = jnp.where(
+                lane // HDIM == head, mixed[head * rows : (head + 1) * rows], attended
             )
-            attended = jnp.where(mine, mixed * (1.0 / denom), attended)
         attended = attended.astype(jnp.bfloat16).astype(jnp.float32)
         return jnp.sum(attended.reshape(blocks, BLK, half), axis=1)
 

time: 35.6 us -> 35.4 us (level)
  transfers between devices with their start and end apart: 8 -> 8, of which waited for: 4 -> 5; matrix products, arithmetic and copies ran while one was open for 0% -> 0% of each run, Pallas kernels for 9% -> 9%
where the time goes in v11:
time: 35.4 us; the launch traced here: 35.1 us
  starting transfers between devices  15.5 us (44%)
  waiting for transfers between devices  10.5 us (30%)
  Pallas kernels  7.63 us (22%)
  between operations  1.4 us (4%)
    ppermute x4, starting transfers between devices, swap(): return lax.ppermute(sent, EVERY, list(enumerate(to)))  6.72 us
    ppermute x1, waiting for transfers between devices, local(): r1 = lax.ppermute(p1, 'seq', [(s, s ^ 1) for s in range(seq_count)])  4.43 us
    all_to_all x1, starting transfers between devices, local(): everyone = lax.all_to_all(piece, EVERY, 0, 0, axis_index_groups=[backward])  3.78 us
    ppermute x4, waiting for transfers between devices, swap(): return lax.ppermute(sent, EVERY, list(enumerate(to)))  3.36 us
    pallas_call x1, Pallas kernels, local(): call(first_kernel, [shape((n, half), bf16) for n in (3 * rows, 3 * rows +...  3.26 us
    ppermute x1, starting transfers between devices, local(): r1 = lax.ppermute(p1, 'seq', [(s, s ^ 1) for s in range(seq_count)])  3 us
    all_to_all x1, waiting for transfers between devices, local(): everyone = lax.all_to_all(piece, EVERY, 0, 0, axis_index_groups=[backward])  2.69 us
    pallas_call x1, Pallas kernels, local(): call(attend_kernel, shape((devices, 4 * blocks, E // 2), PIECE), [VMEM] *...  2.33 us
  transfers between devices with their start and end apart: 8, of which 5 were waited for; matrix products, arithmetic and copies ran while one was open for 0% of the time, Pallas kernels for 9%

profile of v11, /device:TPU:0, one launch (start us, length us, event | category | flops | bytes accessed | tf_op | source)
XLA Modules:
  0.0 35.1 jit_solution(8530024029745331951)
XLA Ops:
  0.6 0.0 copy-start
  0.6 0.0 copy-start.1
  0.7 0.0 copy-start.2
  0.7 3.3 %shard_map.104 = (bf16[768,128]{1,0:T(8,128)(2,1)S(1)}, bf16[1040,128]{1,0:T(8,128)(2,1)S(1)}, bf16[512,128]{1,0:T(8,128)(2,1)S(1)}, bf16[512,128]{1,0:T(8,128)(2,1)S(1)}, f32[272,128]{1,0:T(8,128)S(1)}) custom-call(bf16[256,1024]{1,0:T(8,128)(2,1)} %frames_ref.1, f32[1,1024]{1,0:T(1,128)} %bitcast.4, bf16[3,1024,256]{2,1,0:T(8,128)(2,1)} %w_hbm.1, ...), custom_call_target="tpu_custom_call" | custom-call | flops 402653184 | bytes 1572864 | tf_op jit(solution)/shard_map/pallas_call | solution.py:312
  3.9 3.0 %collective-permute-start = (bf16[1040,128]{1,0:T(8,128)(2,1)S(1)}, bf16[1040,128]{1,0:T(8,128)(2,1)S(1)}, u32[]{:S(2)}, u32[]{:S(2)}) collective-permute-start(bf16[1040,128]{1,0:T(8,128)(2,1)S(1)} %get-tuple-element.16), channel_id=1, source_target_pairs={{0,4},{4,0},{8,12},{12,8},{16,20},{20,16},{24,28},{28,24},{1,5},{5... | collective-permute-start | bytes 798728 | tf_op jit(solution)/shard_map/ppermute | solution.py:325
  6.9 1.3 %collective-permute-start.3 = (bf16[512,128]{1,0:T(8,128)(2,1)S(1)}, bf16[512,128]{1,0:T(8,128)(2,1)S(1)}, u32[]{:S(2)}, u32[]{:S(2)}) collective-permute-start(bf16[512,128]{1,0:T(8,128)(2,1)S(1)} %get-tuple-element.18), channel_id=1, source_target_pairs={{4,12},{12,20},{20,28},{8,0},{16,8},{24,16},{5,13},{13,21},{21,29}... | collective-permute-start | bytes 393224 | tf_op jit(solution)/shard_map/ppermute | solution.py:331
  8.2 0.7 %collective-permute-start.4 = (bf16[512,128]{1,0:T(8,128)(2,1)S(1)}, bf16[512,128]{1,0:T(8,128)(2,1)S(1)}, u32[]{:S(2)}, u32[]{:S(2)}) collective-permute-start(bf16[512,128]{1,0:T(8,128)(2,1)S(1)} %get-tuple-element.19), channel_id=1, source_target_pairs={{4,8},{12,16},{20,24},{8,4},{16,12},{24,20},{5,9},{13,17},{21,25},... | collective-permute-start | bytes 393224 | tf_op jit(solution)/shard_map/ppermute | solution.py:326
  8.9 4.4 %collective-permute-done.r1_ref = bf16[1040,128]{1,0:T(8,128)(2,1)S(1)} collective-permute-done((bf16[1040,128]{1,0:T(8,128)(2,1)S(1)}, bf16[1040,128]{1,0:T(8,128)(2,1)S(1)}, u32[]{:S(2)}, u32[]{:S(2)}) %collective-permute-start) | collective-permute-done | bytes 266272 | tf_op jit(solution)/shard_map/ppermute | solution.py:325
  13.3 0.1 collective-permute-start.1
  13.4 0.0 copy-done
  13.4 0.0 copy-done.1
  13.4 0.0 copy-done.2
  13.5 0.5 %shard_map.105 = (bf16[256,512]{1,0:T(8,128)(2,1)S(1)}, f32[2,512]{1,0:T(2,128)S(1)}) custom-call(bf16[256,1024]{1,0:T(8,128)(2,1)S(1)} %copy-done, bf16[256,1024]{1,0:T(8,128)(2,1)S(1)} %copy-done.2, bf16[1024,512]{1,0:T(8,128)(2,1)S(1)} %copy-done.1), custom_call_target="tpu_custom_call" | custom-call | flops 10000000000 | bytes 2097152 | tf_op jit(solution)/shard_map/pallas_call | solution.py:354
  14.0 0.7 %collective-permute-done.1 = bf16[272,128]{1,0:T(8,128)(2,1)S(1)} collective-permute-done((bf16[272,128]{1,0:T(8,128)(2,1)S(1)}, bf16[272,128]{1,0:T(8,128)(2,1)S(1)}, u32[]{:S(2)}, u32[]{:S(2)}) %collective-permute-start.1) | collective-permute-done | bytes 69664 | tf_op jit(solution)/shard_map/ppermute | solution.py:343
  14.7 1.9 %collective-permute-start.2 = (bf16[272,128]{1,0:T(8,128)(2,1)S(1)}, bf16[272,128]{1,0:T(8,128)(2,1)S(1)}, u32[]{:S(2)}, u32[]{:S(2)}) collective-permute-start(bf16[272,128]{1,0:T(8,128)(2,1)S(1)} %fusion.2), channel_id=1, source_target_pairs={{0,8},{1,9},{2,10},{3,11},{4,12},{5,13},{6,14},{7,15},{8,0},{9,1},... | collective-permute-start | bytes 208904 | tf_op jit(solution)/shard_map/ppermute | solution.py:343
  16.6 0.0 collective-permute-done.3.r2_ref
  16.6 0.0 collective-permute-done.4.r3_ref
  16.6 2.3 %shard_map.106 = bf16[32,8,256]{2,1,0:T(8,128)(2,1)} custom-call(bf16[768,128]{1,0:T(8,128)(2,1)S(1)} %get-tuple-element.17.own_ref, bf16[1040,128]{1,0:T(8,128)(2,1)S(1)} %collective-permute-done.r1_ref, bf16[512,128]{1,0:T(8,128)(2,1)S(1)} %collective-permute-done.3.r2_ref, bf16[512,128]{1,0:T(8,128)(2,1)S(1)} %collective-permute-done.4.r3_ref, ...), custom_call_target="tpu_custom_call" | custom-call | flops 10000000000 | bytes 655360 | tf_op jit(solution)/shard_map/pallas_call | solution.py:361
  18.9 0.2 collective-permute-done.2
  19.2 2.9 %collective-permute-start.5 = (bf16[272,128]{1,0:T(8,128)(2,1)S(1)}, bf16[272,128]{1,0:T(8,128)(2,1)S(1)}, u32[]{:S(2)}, u32[]{:S(2)}) collective-permute-start(bf16[272,128]{1,0:T(8,128)(2,1)S(1)} %fusion.1), channel_id=1, source_target_pairs={{0,16},{1,17},{2,18},{3,19},{4,20},{5,21},{6,22},{7,23},{8,24},{9,... | collective-permute-start | bytes 208904 | tf_op jit(solution)/shard_map/ppermute | solution.py:343
  22.1 3.8 %all-to-all-start = ((bf16[32,8,256]{2,1,0:T(8,128)(2,1)}), bf16[32,8,256]{2,1,0:T(8,128)(2,1)S(1)}, u32[]{:S(2)}, u32[]{:S(2)}) async-start(bf16[32,8,256]{2,1,0:T(8,128)(2,1)} %shard_map.106), calls=%async_computation | async-start | bytes 262144 | tf_op jit(solution)/shard_map/all_to_all | solution.py:375
  25.9 0.0 collective-permute-done.5
  25.9 0.1 fusion.3
  25.9 1.8 %collective-permute-start.6 = (bf16[272,128]{1,0:T(8,128)(2,1)S(1)}, bf16[272,128]{1,0:T(8,128)(2,1)S(1)}, u32[]{:S(2)}, u32[]{:S(2)}) collective-permute-start(bf16[272,128]{1,0:T(8,128)(2,1)S(1)} %get-tuple-element.28), channel_id=1, source_target_pairs={{0,2},{1,3},{2,0},{3,1},{4,6},{5,7},{6,4},{7,5},{8,10},{9,11},{10,... | collective-permute-start | bytes 208904 | tf_op jit(solution)/shard_map/ppermute | solution.py:343
  28.4 2.5 %collective-permute-done.6.refs_0_ = bf16[272,128]{1,0:T(8,128)(2,1)S(1)} collective-permute-done((bf16[272,128]{1,0:T(8,128)(2,1)S(1)}, bf16[272,128]{1,0:T(8,128)(2,1)S(1)}, u32[]{:S(2)}, u32[]{:S(2)}) %collective-permute-start.6) | collective-permute-done | bytes 69664 | tf_op jit(solution)/shard_map/ppermute | solution.py:343
  30.9 0.1 shard_map.107
  31.1 2.7 %all-to-all-done.everyone_ref = bf16[32,8,256]{2,1,0:T(8,128)(2,1)S(1)} async-done(((bf16[32,8,256]{2,1,0:T(8,128)(2,1)}), bf16[32,8,256]{2,1,0:T(8,128)(2,1)S(1)}, u32[]{:S(2)}, u32[]{:S(2)}) %all-to-all-start) | async-done | bytes 131104 | tf_op jit(solution)/shard_map/all_to_all | solution.py:375
  33.8 1.4 %shard_map.108 = (f32[2,512]{1,0:T(2,128)}, f32[1,2]{1,0:T(1,128)}) custom-call(bf16[32,8,256]{2,1,0:T(8,128)(2,1)S(1)} %all-to-all-done.everyone_ref, bf16[64,512]{1,0:T(8,128)(2,1)S(1)} %get-tuple-element.24.captions_ref, bf16[128,256]{1,0:T(8,128)(2,1)S(1)} %get-tuple-element.25.masks_ref, f32[1]{0:T(128)S(6)} %copy.11.divisor_ref), custom_call_target="tpu_custom_call" | custom-call | flops 8388608 | bytes 131072 | tf_op jit(solution)/shard_map/pallas_call | solution.py:386
  (3 shorter events, 0.1 us)
Async XLA Ops:
  0.6 12.8 %copy-start = (bf16[256,1024]{1,0:T(8,128)(2,1)S(1)}, bf16[256,1024]{1,0:T(8,128)(2,1)}, u32[]{:S(2)}) copy-start(bf16[256,1024]{1,0:T(8,128)(2,1)} %frames_ref.1) | copy-start | bytes 1572868
  0.6 12.8 %copy-start.1 = (bf16[1024,512]{1,0:T(8,128)(2,1)S(1)}, bf16[1024,512]{1,0:T(8,128)(2,1)}, u32[]{:S(2)}) copy-start(bf16[1024,512]{1,0:T(8,128)(2,1)} %w_proj_ref.1) | copy-start | bytes 3145732
  0.7 12.8 %copy-start.2 = (bf16[256,1024]{1,0:T(8,128)(2,1)S(1)}, bf16[256,1024]{1,0:T(8,128)(2,1)}, u32[]{:S(2)}) copy-start(bf16[256,1024]{1,0:T(8,128)(2,1)} %w_out_ref.1) | copy-start | bytes 1572868
  3.9 9.4 %collective-permute-start = (bf16[1040,128]{1,0:T(8,128)(2,1)S(1)}, bf16[1040,128]{1,0:T(8,128)(2,1)S(1)}, u32[]{:S(2)}, u32[]{:S(2)}) collective-permute-start(bf16[1040,128]{1,0:T(8,128)(2,1)S(1)} %get-tuple-element.16), channel_id=1, source_target_pairs={{0,4},{4,0},{8,12},{12,8},{16,20},{20,16},{24,28},{28,24},{1,5},{5... | collective-permute-start | bytes 798728 | tf_op jit(solution)/shard_map/ppermute | solution.py:325
  6.9 9.7 %collective-permute-start.3 = (bf16[512,128]{1,0:T(8,128)(2,1)S(1)}, bf16[512,128]{1,0:T(8,128)(2,1)S(1)}, u32[]{:S(2)}, u32[]{:S(2)}) collective-permute-start(bf16[512,128]{1,0:T(8,128)(2,1)S(1)} %get-tuple-element.18), channel_id=1, source_target_pairs={{4,12},{12,20},{20,28},{8,0},{16,8},{24,16},{5,13},{13,21},{21,29}... | collective-permute-start | bytes 393224 | tf_op jit(solution)/shard_map/ppermute | solution.py:331
  8.2 8.4 %collective-permute-start.4 = (bf16[512,128]{1,0:T(8,128)(2,1)S(1)}, bf16[512,128]{1,0:T(8,128)(2,1)S(1)}, u32[]{:S(2)}, u32[]{:S(2)}) collective-permute-start(bf16[512,128]{1,0:T(8,128)(2,1)S(1)} %get-tuple-element.19), channel_id=1, source_target_pairs={{4,8},{12,16},{20,24},{8,4},{16,12},{24,20},{5,9},{13,17},{21,25},... | collective-permute-start | bytes 393224 | tf_op jit(solution)/shard_map/ppermute | solution.py:326
  13.3 1.3 %collective-permute-start.1 = (bf16[272,128]{1,0:T(8,128)(2,1)S(1)}, bf16[272,128]{1,0:T(8,128)(2,1)S(1)}, u32[]{:S(2)}, u32[]{:S(2)}) collective-permute-start(bf16[272,128]{1,0:T(8,128)(2,1)S(1)} %fusion), channel_id=1, source_target_pairs={{0,1},{1,0},{2,3},{3,2},{4,5},{5,4},{6,7},{7,6},{8,9},{9,8},{10,11... | collective-permute-start | bytes 208904 | tf_op jit(solution)/shard_map/ppermute | solution.py:343
  14.7 4.4 %collective-permute-start.2 = (bf16[272,128]{1,0:T(8,128)(2,1)S(1)}, bf16[272,128]{1,0:T(8,128)(2,1)S(1)}, u32[]{:S(2)}, u32[]{:S(2)}) collective-permute-start(bf16[272,128]{1,0:T(8,128)(2,1)S(1)} %fusion.2), channel_id=1, source_target_pairs={{0,8},{1,9},{2,10},{3,11},{4,12},{5,13},{6,14},{7,15},{8,0},{9,1},... | collective-permute-start | bytes 208904 | tf_op jit(solution)/shard_map/ppermute | solution.py:343
  19.2 6.7 %collective-permute-start.5 = (bf16[272,128]{1,0:T(8,128)(2,1)S(1)}, bf16[272,128]{1,0:T(8,128)(2,1)S(1)}, u32[]{:S(2)}, u32[]{:S(2)}) collective-permute-start(bf16[272,128]{1,0:T(8,128)(2,1)S(1)} %fusion.1), channel_id=1, source_target_pairs={{0,16},{1,17},{2,18},{3,19},{4,20},{5,21},{6,22},{7,23},{8,24},{9,... | collective-permute-start | bytes 208904 | tf_op jit(solution)/shard_map/ppermute | solution.py:343
  22.1 11.7 %all-to-all-start = ((bf16[32,8,256]{2,1,0:T(8,128)(2,1)}), bf16[32,8,256]{2,1,0:T(8,128)(2,1)S(1)}, u32[]{:S(2)}, u32[]{:S(2)}) async-start(bf16[32,8,256]{2,1,0:T(8,128)(2,1)} %shard_map.106), calls=%async_computation | async-start | bytes 262144 | tf_op jit(solution)/shard_map/all_to_all | solution.py:375
  25.9 5.0 %collective-permute-start.6 = (bf16[272,128]{1,0:T(8,128)(2,1)S(1)}, bf16[272,128]{1,0:T(8,128)(2,1)S(1)}, u32[]{:S(2)}, u32[]{:S(2)}) collective-permute-start(bf16[272,128]{1,0:T(8,128)(2,1)S(1)} %get-tuple-element.28), channel_id=1, source_target_pairs={{0,2},{1,3},{2,0},{3,1},{4,6},{5,7},{6,4},{7,5},{8,10},{9,11},{10,... | collective-permute-start | bytes 208904 | tf_op jit(solution)/shard_map/ppermute | solution.py:343

commit v12 on v11

--- a/solution.py
+++ b/solution.py
@@ -78,12 +78,14 @@
     own_caps = bound.shape[0]
     slot = lax.axis_index("seq") * lax.axis_size("head") + lax.axis_index("head")
     copies[0].wait()
-    ids = (id_rows[...] - slot * vocab).T
-    words = lax.broadcasted_iota(jnp.int32, (caps, vocab), 1)
-    counts = jnp.zeros((caps, vocab), jnp.float32)
+    ids = id_rows[...] - slot * vocab
+    ids = jnp.where((ids >= 0) & (ids < vocab), ids, -1).T
+    words = lax.broadcasted_iota(jnp.int32, (caps, vocab), 1).astype(jnp.int16)
+    counts = jnp.zeros((caps, vocab), jnp.bfloat16)
+    one, none = jnp.ones_like(counts), jnp.zeros_like(counts)
     for t in range(tokens):
-        counts = counts + jnp.where(ids[:, t : t + 1] == words, 1.0, 0.0)
-    counts = counts.astype(jnp.bfloat16)
+        column = jnp.broadcast_to(ids[:, t : t + 1], (caps, vocab)).astype(jnp.int16)
+        counts = counts + jnp.where(column == words, one, none)
 
     copies[1].wait()
     copies[2].wait()

time: 35.4 us -> 35.1 us (level)
  no operation moved by 1% of the time
where the time goes in v12:
time: 35.1 us; the launch traced here: 34.9 us
  starting transfers between devices  15.5 us (44%)
  waiting for transfers between devices  10.5 us (30%)
  Pallas kernels  7.35 us (21%)
  between operations  1.4 us (4%)
    ppermute x4, starting transfers between devices, swap(): return lax.ppermute(sent, EVERY, list(enumerate(to)))  6.72 us
    ppermute x1, waiting for transfers between devices, local(): r1 = lax.ppermute(p1, 'seq', [(s, s ^ 1) for s in range(seq_count)])  4.43 us
    all_to_all x1, starting transfers between devices, local(): everyone = lax.all_to_all(piece, EVERY, 0, 0, axis_index_groups=[backward])  3.79 us
    ppermute x4, waiting for transfers between devices, swap(): return lax.ppermute(sent, EVERY, list(enumerate(to)))  3.36 us
    ppermute x1, starting transfers between devices, local(): r1 = lax.ppermute(p1, 'seq', [(s, s ^ 1) for s in range(seq_count)])  3 us
    pallas_call x1, Pallas kernels, local(): call(first_kernel, [shape((n, half), bf16) for n in (3 * rows, 3 * rows +...  2.98 us
    all_to_all x1, waiting for transfers between devices, local(): everyone = lax.all_to_all(piece, EVERY, 0, 0, axis_index_groups=[backward])  2.69 us
    pallas_call x1, Pallas kernels, local(): call(attend_kernel, shape((devices, 4 * blocks, E // 2), PIECE), [VMEM] *...  2.33 us
  transfers between devices with their start and end apart: 8, of which 5 were waited for; matrix products, arithmetic and copies ran while one was open for 0% of the time, Pallas kernels for 9%

profile of v12, /device:TPU:0, one launch (start us, length us, event | category | flops | bytes accessed | tf_op | source)
XLA Modules:
  0.0 34.9 jit_solution(2035024021447936070)
XLA Ops:
  0.6 0.0 copy-start
  0.6 0.0 copy-start.1
  0.7 0.0 copy-start.2
  0.7 3.0 %shard_map.104 = (bf16[768,128]{1,0:T(8,128)(2,1)S(1)}, bf16[1040,128]{1,0:T(8,128)(2,1)S(1)}, bf16[512,128]{1,0:T(8,128)(2,1)S(1)}, bf16[512,128]{1,0:T(8,128)(2,1)S(1)}, f32[272,128]{1,0:T(8,128)S(1)}) custom-call(bf16[256,1024]{1,0:T(8,128)(2,1)} %frames_ref.1, f32[1,1024]{1,0:T(1,128)} %bitcast.4, bf16[3,1024,256]{2,1,0:T(8,128)(2,1)} %w_hbm.1, ...), custom_call_target="tpu_custom_call" | custom-call | flops 402653184 | bytes 1572864 | tf_op jit(solution)/shard_map/pallas_call | solution.py:314
  3.6 3.0 %collective-permute-start = (bf16[1040,128]{1,0:T(8,128)(2,1)S(1)}, bf16[1040,128]{1,0:T(8,128)(2,1)S(1)}, u32[]{:S(2)}, u32[]{:S(2)}) collective-permute-start(bf16[1040,128]{1,0:T(8,128)(2,1)S(1)} %get-tuple-element.16), channel_id=1, source_target_pairs={{0,4},{4,0},{8,12},{12,8},{16,20},{20,16},{24,28},{28,24},{1,5},{5... | collective-permute-start | bytes 798728 | tf_op jit(solution)/shard_map/ppermute | solution.py:327
  6.7 1.3 %collective-permute-start.3 = (bf16[512,128]{1,0:T(8,128)(2,1)S(1)}, bf16[512,128]{1,0:T(8,128)(2,1)S(1)}, u32[]{:S(2)}, u32[]{:S(2)}) collective-permute-start(bf16[512,128]{1,0:T(8,128)(2,1)S(1)} %get-tuple-element.18), channel_id=1, source_target_pairs={{4,12},{12,20},{20,28},{8,0},{16,8},{24,16},{5,13},{13,21},{21,29}... | collective-permute-start | bytes 393224 | tf_op jit(solution)/shard_map/ppermute | solution.py:333
  7.9 0.7 %collective-permute-start.4 = (bf16[512,128]{1,0:T(8,128)(2,1)S(1)}, bf16[512,128]{1,0:T(8,128)(2,1)S(1)}, u32[]{:S(2)}, u32[]{:S(2)}) collective-permute-start(bf16[512,128]{1,0:T(8,128)(2,1)S(1)} %get-tuple-element.19), channel_id=1, source_target_pairs={{4,8},{12,16},{20,24},{8,4},{16,12},{24,20},{5,9},{13,17},{21,25},... | collective-permute-start | bytes 393224 | tf_op jit(solution)/shard_map/ppermute | solution.py:328
  8.6 4.4 %collective-permute-done.r1_ref = bf16[1040,128]{1,0:T(8,128)(2,1)S(1)} collective-permute-done((bf16[1040,128]{1,0:T(8,128)(2,1)S(1)}, bf16[1040,128]{1,0:T(8,128)(2,1)S(1)}, u32[]{:S(2)}, u32[]{:S(2)}) %collective-permute-start) | collective-permute-done | bytes 266272 | tf_op jit(solution)/shard_map/ppermute | solution.py:327
  13.1 0.1 collective-permute-start.1
  13.1 0.0 copy-done
  13.2 0.0 copy-done.1
  13.2 0.0 copy-done.2
  13.2 0.5 %shard_map.105 = (bf16[256,512]{1,0:T(8,128)(2,1)S(1)}, f32[2,512]{1,0:T(2,128)S(1)}) custom-call(bf16[256,1024]{1,0:T(8,128)(2,1)S(1)} %copy-done, bf16[256,1024]{1,0:T(8,128)(2,1)S(1)} %copy-done.2, bf16[1024,512]{1,0:T(8,128)(2,1)S(1)} %copy-done.1), custom_call_target="tpu_custom_call" | custom-call | flops 10000000000 | bytes 2097152 | tf_op jit(solution)/shard_map/pallas_call | solution.py:356
  13.7 0.7 %collective-permute-done.1 = bf16[272,128]{1,0:T(8,128)(2,1)S(1)} collective-permute-done((bf16[272,128]{1,0:T(8,128)(2,1)S(1)}, bf16[272,128]{1,0:T(8,128)(2,1)S(1)}, u32[]{:S(2)}, u32[]{:S(2)}) %collective-permute-start.1) | collective-permute-done | bytes 69664 | tf_op jit(solution)/shard_map/ppermute | solution.py:345
  14.4 1.9 %collective-permute-start.2 = (bf16[272,128]{1,0:T(8,128)(2,1)S(1)}, bf16[272,128]{1,0:T(8,128)(2,1)S(1)}, u32[]{:S(2)}, u32[]{:S(2)}) collective-permute-start(bf16[272,128]{1,0:T(8,128)(2,1)S(1)} %fusion.2), channel_id=1, source_target_pairs={{0,8},{1,9},{2,10},{3,11},{4,12},{5,13},{6,14},{7,15},{8,0},{9,1},... | collective-permute-start | bytes 208904 | tf_op jit(solution)/shard_map/ppermute | solution.py:345
  16.3 0.0 collective-permute-done.3.r2_ref
  16.3 0.0 collective-permute-done.4.r3_ref
  16.3 2.3 %shard_map.106 = bf16[32,8,256]{2,1,0:T(8,128)(2,1)} custom-call(bf16[768,128]{1,0:T(8,128)(2,1)S(1)} %get-tuple-element.17.own_ref, bf16[1040,128]{1,0:T(8,128)(2,1)S(1)} %collective-permute-done.r1_ref, bf16[512,128]{1,0:T(8,128)(2,1)S(1)} %collective-permute-done.3.r2_ref, bf16[512,128]{1,0:T(8,128)(2,1)S(1)} %collective-permute-done.4.r3_ref, ...), custom_call_target="tpu_custom_call" | custom-call | flops 10000000000 | bytes 655360 | tf_op jit(solution)/shard_map/pallas_call | solution.py:363
  18.7 0.2 collective-permute-done.2
  18.9 2.9 %collective-permute-start.5 = (bf16[272,128]{1,0:T(8,128)(2,1)S(1)}, bf16[272,128]{1,0:T(8,128)(2,1)S(1)}, u32[]{:S(2)}, u32[]{:S(2)}) collective-permute-start(bf16[272,128]{1,0:T(8,128)(2,1)S(1)} %fusion.1), channel_id=1, source_target_pairs={{0,16},{1,17},{2,18},{3,19},{4,20},{5,21},{6,22},{7,23},{8,24},{9,... | collective-permute-start | bytes 208904 | tf_op jit(solution)/shard_map/ppermute | solution.py:345
  21.8 3.8 %all-to-all-start = ((bf16[32,8,256]{2,1,0:T(8,128)(2,1)}), bf16[32,8,256]{2,1,0:T(8,128)(2,1)S(1)}, u32[]{:S(2)}, u32[]{:S(2)}) async-start(bf16[32,8,256]{2,1,0:T(8,128)(2,1)} %shard_map.106), calls=%async_computation | async-start | bytes 262144 | tf_op jit(solution)/shard_map/all_to_all | solution.py:377
  25.6 0.0 collective-permute-done.5
  25.6 0.1 fusion.3
  25.7 1.8 %collective-permute-start.6 = (bf16[272,128]{1,0:T(8,128)(2,1)S(1)}, bf16[272,128]{1,0:T(8,128)(2,1)S(1)}, u32[]{:S(2)}, u32[]{:S(2)}) collective-permute-start(bf16[272,128]{1,0:T(8,128)(2,1)S(1)} %get-tuple-element.28), channel_id=1, source_target_pairs={{0,2},{1,3},{2,0},{3,1},{4,6},{5,7},{6,4},{7,5},{8,10},{9,11},{10,... | collective-permute-start | bytes 208904 | tf_op jit(solution)/shard_map/ppermute | solution.py:345
  28.1 2.5 %collective-permute-done.6.refs_0_ = bf16[272,128]{1,0:T(8,128)(2,1)S(1)} collective-permute-done((bf16[272,128]{1,0:T(8,128)(2,1)S(1)}, bf16[272,128]{1,0:T(8,128)(2,1)S(1)}, u32[]{:S(2)}, u32[]{:S(2)}) %collective-permute-start.6) | collective-permute-done | bytes 69664 | tf_op jit(solution)/shard_map/ppermute | solution.py:345
  30.7 0.1 shard_map.107
  30.8 2.7 %all-to-all-done.everyone_ref = bf16[32,8,256]{2,1,0:T(8,128)(2,1)S(1)} async-done(((bf16[32,8,256]{2,1,0:T(8,128)(2,1)}), bf16[32,8,256]{2,1,0:T(8,128)(2,1)S(1)}, u32[]{:S(2)}, u32[]{:S(2)}) %all-to-all-start) | async-done | bytes 131104 | tf_op jit(solution)/shard_map/all_to_all | solution.py:377
  33.5 1.4 %shard_map.108 = (f32[2,512]{1,0:T(2,128)}, f32[1,2]{1,0:T(1,128)}) custom-call(bf16[32,8,256]{2,1,0:T(8,128)(2,1)S(1)} %all-to-all-done.everyone_ref, bf16[64,512]{1,0:T(8,128)(2,1)S(1)} %get-tuple-element.24.captions_ref, bf16[128,256]{1,0:T(8,128)(2,1)S(1)} %get-tuple-element.25.masks_ref, f32[1]{0:T(128)S(6)} %copy.11.divisor_ref), custom_call_target="tpu_custom_call" | custom-call | flops 8388608 | bytes 131072 | tf_op jit(solution)/shard_map/pallas_call | solution.py:388
  (3 shorter events, 0.1 us)
Async XLA Ops:
  0.6 12.5 %copy-start = (bf16[256,1024]{1,0:T(8,128)(2,1)S(1)}, bf16[256,1024]{1,0:T(8,128)(2,1)}, u32[]{:S(2)}) copy-start(bf16[256,1024]{1,0:T(8,128)(2,1)} %frames_ref.1) | copy-start | bytes 1572868
  0.6 12.5 %copy-start.1 = (bf16[1024,512]{1,0:T(8,128)(2,1)S(1)}, bf16[1024,512]{1,0:T(8,128)(2,1)}, u32[]{:S(2)}) copy-start(bf16[1024,512]{1,0:T(8,128)(2,1)} %w_proj_ref.1) | copy-start | bytes 3145732
  0.7 12.5 %copy-start.2 = (bf16[256,1024]{1,0:T(8,128)(2,1)S(1)}, bf16[256,1024]{1,0:T(8,128)(2,1)}, u32[]{:S(2)}) copy-start(bf16[256,1024]{1,0:T(8,128)(2,1)} %w_out_ref.1) | copy-start | bytes 1572868
  3.6 9.4 %collective-permute-start = (bf16[1040,128]{1,0:T(8,128)(2,1)S(1)}, bf16[1040,128]{1,0:T(8,128)(2,1)S(1)}, u32[]{:S(2)}, u32[]{:S(2)}) collective-permute-start(bf16[1040,128]{1,0:T(8,128)(2,1)S(1)} %get-tuple-element.16), channel_id=1, source_target_pairs={{0,4},{4,0},{8,12},{12,8},{16,20},{20,16},{24,28},{28,24},{1,5},{5... | collective-permute-start | bytes 798728 | tf_op jit(solution)/shard_map/ppermute | solution.py:327
  6.7 9.7 %collective-permute-start.3 = (bf16[512,128]{1,0:T(8,128)(2,1)S(1)}, bf16[512,128]{1,0:T(8,128)(2,1)S(1)}, u32[]{:S(2)}, u32[]{:S(2)}) collective-permute-start(bf16[512,128]{1,0:T(8,128)(2,1)S(1)} %get-tuple-element.18), channel_id=1, source_target_pairs={{4,12},{12,20},{20,28},{8,0},{16,8},{24,16},{5,13},{13,21},{21,29}... | collective-permute-start | bytes 393224 | tf_op jit(solution)/shard_map/ppermute | solution.py:333
  7.9 8.4 %collective-permute-start.4 = (bf16[512,128]{1,0:T(8,128)(2,1)S(1)}, bf16[512,128]{1,0:T(8,128)(2,1)S(1)}, u32[]{:S(2)}, u32[]{:S(2)}) collective-permute-start(bf16[512,128]{1,0:T(8,128)(2,1)S(1)} %get-tuple-element.19), channel_id=1, source_target_pairs={{4,8},{12,16},{20,24},{8,4},{16,12},{24,20},{5,9},{13,17},{21,25},... | collective-permute-start | bytes 393224 | tf_op jit(solution)/shard_map/ppermute | solution.py:328
  13.1 1.3 %collective-permute-start.1 = (bf16[272,128]{1,0:T(8,128)(2,1)S(1)}, bf16[272,128]{1,0:T(8,128)(2,1)S(1)}, u32[]{:S(2)}, u32[]{:S(2)}) collective-permute-start(bf16[272,128]{1,0:T(8,128)(2,1)S(1)} %fusion), channel_id=1, source_target_pairs={{0,1},{1,0},{2,3},{3,2},{4,5},{5,4},{6,7},{7,6},{8,9},{9,8},{10,11... | collective-permute-start | bytes 208904 | tf_op jit(solution)/shard_map/ppermute | solution.py:345
  14.4 4.4 %collective-permute-start.2 = (bf16[272,128]{1,0:T(8,128)(2,1)S(1)}, bf16[272,128]{1,0:T(8,128)(2,1)S(1)}, u32[]{:S(2)}, u32[]{:S(2)}) collective-permute-start(bf16[272,128]{1,0:T(8,128)(2,1)S(1)} %fusion.2), channel_id=1, source_target_pairs={{0,8},{1,9},{2,10},{3,11},{4,12},{5,13},{6,14},{7,15},{8,0},{9,1},... | collective-permute-start | bytes 208904 | tf_op jit(solution)/shard_map/ppermute | solution.py:345
  18.9 6.7 %collective-permute-start.5 = (bf16[272,128]{1,0:T(8,128)(2,1)S(1)}, bf16[272,128]{1,0:T(8,128)(2,1)S(1)}, u32[]{:S(2)}, u32[]{:S(2)}) collective-permute-start(bf16[272,128]{1,0:T(8,128)(2,1)S(1)} %fusion.1), channel_id=1, source_target_pairs={{0,16},{1,17},{2,18},{3,19},{4,20},{5,21},{6,22},{7,23},{8,24},{9,... | collective-permute-start | bytes 208904 | tf_op jit(solution)/shard_map/ppermute | solution.py:345
  21.8 11.7 %all-to-all-start = ((bf16[32,8,256]{2,1,0:T(8,128)(2,1)}), bf16[32,8,256]{2,1,0:T(8,128)(2,1)S(1)}, u32[]{:S(2)}, u32[]{:S(2)}) async-start(bf16[32,8,256]{2,1,0:T(8,128)(2,1)} %shard_map.106), calls=%async_computation | async-start | bytes 262144 | tf_op jit(solution)/shard_map/all_to_all | solution.py:377
  25.7 5.0 %collective-permute-start.6 = (bf16[272,128]{1,0:T(8,128)(2,1)S(1)}, bf16[272,128]{1,0:T(8,128)(2,1)S(1)}, u32[]{:S(2)}, u32[]{:S(2)}) collective-permute-start(bf16[272,128]{1,0:T(8,128)(2,1)S(1)} %get-tuple-element.28), channel_id=1, source_target_pairs={{0,2},{1,3},{2,0},{3,1},{4,6},{5,7},{6,4},{7,5},{8,10},{9,11},{10,... | collective-permute-start | bytes 208904 | tf_op jit(solution)/shard_map/ppermute | solution.py:345

commit v13 on v12

--- a/solution.py
+++ b/solution.py
@@ -161,11 +161,10 @@
     apart = lax.broadcasted_iota(jnp.int32, (rows, rows), 0) - lax.broadcasted_iota(
         jnp.int32, (rows, rows), 1
     )
-    apart = jnp.concatenate([apart] * heads, axis=0)
     lane = lax.broadcasted_iota(jnp.int32, (rows, half), 1)
 
     def block_sums(me, other, halo, parity, exists):
-        side = jnp.where(parity == 0, apart, -apart)
+        side = jnp.concatenate([jnp.where(parity == 0, apart, -apart)] * heads, axis=0)
         near = side >= 0
         far = side <= jnp.where(exists, 0, -2 * rows)
         query = me[0:rows]

time: 35.1 us -> 35.1 us (level)
  no operation moved by 1% of the time
where the time goes in v13:
time: 35.1 us; the launch traced here: 34.9 us
  starting transfers between devices  15.5 us (44%)
  waiting for transfers between devices  10.5 us (30%)
  Pallas kernels  7.35 us (21%)
  between operations  1.4 us (4%)
    ppermute x4, starting transfers between devices, swap(): return lax.ppermute(sent, EVERY, list(enumerate(to)))  6.72 us
    ppermute x1, waiting for transfers between devices, local(): r1 = lax.ppermute(p1, 'seq', [(s, s ^ 1) for s in range(seq_count)])  4.43 us
    all_to_all x1, starting transfers between devices, local(): everyone = lax.all_to_all(piece, EVERY, 0, 0, axis_index_groups=[backward])  3.79 us
    ppermute x4, waiting for transfers between devices, swap(): return lax.ppermute(sent, EVERY, list(enumerate(to)))  3.36 us
    ppermute x1, starting transfers between devices, local(): r1 = lax.ppermute(p1, 'seq', [(s, s ^ 1) for s in range(seq_count)])  3 us
    pallas_call x1, Pallas kernels, local(): call(first_kernel, [shape((n, half), bf16) for n in (3 * rows, 3 * rows +...  2.98 us
    all_to_all x1, waiting for transfers between devices, local(): everyone = lax.all_to_all(piece, EVERY, 0, 0, axis_index_groups=[backward])  2.69 us
    pallas_call x1, Pallas kernels, local(): call(attend_kernel, shape((devices, 4 * blocks, E // 2), PIECE), [VMEM] *...  2.33 us
  transfers between devices with their start and end apart: 8, of which 5 were waited for; matrix products, arithmetic and copies ran while one was open for 0% of the time, Pallas kernels for 9%

profile of v13, /device:TPU:0, one launch (start us, length us, event | category | flops | bytes accessed | tf_op | source)
XLA Modules:
  0.0 34.9 jit_solution(2035024021447936070)
XLA Ops:
  0.6 0.0 copy-start
  0.6 0.0 copy-start.1
  0.7 0.0 copy-start.2
  0.7 3.0 %shard_map.104 = (bf16[768,128]{1,0:T(8,128)(2,1)S(1)}, bf16[1040,128]{1,0:T(8,128)(2,1)S(1)}, bf16[512,128]{1,0:T(8,128)(2,1)S(1)}, bf16[512,128]{1,0:T(8,128)(2,1)S(1)}, f32[272,128]{1,0:T(8,128)S(1)}) custom-call(bf16[256,1024]{1,0:T(8,128)(2,1)} %frames_ref.1, f32[1,1024]{1,0:T(1,128)} %bitcast.4, bf16[3,1024,256]{2,1,0:T(8,128)(2,1)} %w_hbm.1, ...), custom_call_target="tpu_custom_call" | custom-call | flops 402653184 | bytes 1572864 | tf_op jit(solution)/shard_map/pallas_call | solution.py:313
  3.6 3.0 %collective-permute-start = (bf16[1040,128]{1,0:T(8,128)(2,1)S(1)}, bf16[1040,128]{1,0:T(8,128)(2,1)S(1)}, u32[]{:S(2)}, u32[]{:S(2)}) collective-permute-start(bf16[1040,128]{1,0:T(8,128)(2,1)S(1)} %get-tuple-element.16), channel_id=1, source_target_pairs={{0,4},{4,0},{8,12},{12,8},{16,20},{20,16},{24,28},{28,24},{1,5},{5... | collective-permute-start | bytes 798728 | tf_op jit(solution)/shard_map/ppermute | solution.py:326
  6.7 1.3 %collective-permute-start.3 = (bf16[512,128]{1,0:T(8,128)(2,1)S(1)}, bf16[512,128]{1,0:T(8,128)(2,1)S(1)}, u32[]{:S(2)}, u32[]{:S(2)}) collective-permute-start(bf16[512,128]{1,0:T(8,128)(2,1)S(1)} %get-tuple-element.18), channel_id=1, source_target_pairs={{4,12},{12,20},{20,28},{8,0},{16,8},{24,16},{5,13},{13,21},{21,29}... | collective-permute-start | bytes 393224 | tf_op jit(solution)/shard_map/ppermute | solution.py:332
  7.9 0.7 %collective-permute-start.4 = (bf16[512,128]{1,0:T(8,128)(2,1)S(1)}, bf16[512,128]{1,0:T(8,128)(2,1)S(1)}, u32[]{:S(2)}, u32[]{:S(2)}) collective-permute-start(bf16[512,128]{1,0:T(8,128)(2,1)S(1)} %get-tuple-element.19), channel_id=1, source_target_pairs={{4,8},{12,16},{20,24},{8,4},{16,12},{24,20},{5,9},{13,17},{21,25},... | collective-permute-start | bytes 393224 | tf_op jit(solution)/shard_map/ppermute | solution.py:327
  8.6 4.4 %collective-permute-done.r1_ref = bf16[1040,128]{1,0:T(8,128)(2,1)S(1)} collective-permute-done((bf16[1040,128]{1,0:T(8,128)(2,1)S(1)}, bf16[1040,128]{1,0:T(8,128)(2,1)S(1)}, u32[]{:S(2)}, u32[]{:S(2)}) %collective-permute-start) | collective-permute-done | bytes 266272 | tf_op jit(solution)/shard_map/ppermute | solution.py:326
  13.1 0.1 collective-permute-start.1
  13.1 0.0 copy-done
  13.2 0.0 copy-done.1
  13.2 0.0 copy-done.2
  13.2 0.5 %shard_map.105 = (bf16[256,512]{1,0:T(8,128)(2,1)S(1)}, f32[2,512]{1,0:T(2,128)S(1)}) custom-call(bf16[256,1024]{1,0:T(8,128)(2,1)S(1)} %copy-done, bf16[256,1024]{1,0:T(8,128)(2,1)S(1)} %copy-done.2, bf16[1024,512]{1,0:T(8,128)(2,1)S(1)} %copy-done.1), custom_call_target="tpu_custom_call" | custom-call | flops 10000000000 | bytes 2097152 | tf_op jit(solution)/shard_map/pallas_call | solution.py:355
  13.7 0.7 %collective-permute-done.1 = bf16[272,128]{1,0:T(8,128)(2,1)S(1)} collective-permute-done((bf16[272,128]{1,0:T(8,128)(2,1)S(1)}, bf16[272,128]{1,0:T(8,128)(2,1)S(1)}, u32[]{:S(2)}, u32[]{:S(2)}) %collective-permute-start.1) | collective-permute-done | bytes 69664 | tf_op jit(solution)/shard_map/ppermute | solution.py:344
  14.4 1.9 %collective-permute-start.2 = (bf16[272,128]{1,0:T(8,128)(2,1)S(1)}, bf16[272,128]{1,0:T(8,128)(2,1)S(1)}, u32[]{:S(2)}, u32[]{:S(2)}) collective-permute-start(bf16[272,128]{1,0:T(8,128)(2,1)S(1)} %fusion.2), channel_id=1, source_target_pairs={{0,8},{1,9},{2,10},{3,11},{4,12},{5,13},{6,14},{7,15},{8,0},{9,1},... | collective-permute-start | bytes 208904 | tf_op jit(solution)/shard_map/ppermute | solution.py:344
  16.3 0.0 collective-permute-done.3.r2_ref
  16.3 0.0 collective-permute-done.4.r3_ref
  16.3 2.3 %shard_map.106 = bf16[32,8,256]{2,1,0:T(8,128)(2,1)} custom-call(bf16[768,128]{1,0:T(8,128)(2,1)S(1)} %get-tuple-element.17.own_ref, bf16[1040,128]{1,0:T(8,128)(2,1)S(1)} %collective-permute-done.r1_ref, bf16[512,128]{1,0:T(8,128)(2,1)S(1)} %collective-permute-done.3.r2_ref, bf16[512,128]{1,0:T(8,128)(2,1)S(1)} %collective-permute-done.4.r3_ref, ...), custom_call_target="tpu_custom_call" | custom-call | flops 10000000000 | bytes 655360 | tf_op jit(solution)/shard_map/pallas_call | solution.py:362
  18.7 0.2 collective-permute-done.2
  18.9 2.9 %collective-permute-start.5 = (bf16[272,128]{1,0:T(8,128)(2,1)S(1)}, bf16[272,128]{1,0:T(8,128)(2,1)S(1)}, u32[]{:S(2)}, u32[]{:S(2)}) collective-permute-start(bf16[272,128]{1,0:T(8,128)(2,1)S(1)} %fusion.1), channel_id=1, source_target_pairs={{0,16},{1,17},{2,18},{3,19},{4,20},{5,21},{6,22},{7,23},{8,24},{9,... | collective-permute-start | bytes 208904 | tf_op jit(solution)/shard_map/ppermute | solution.py:344
  21.8 3.8 %all-to-all-start = ((bf16[32,8,256]{2,1,0:T(8,128)(2,1)}), bf16[32,8,256]{2,1,0:T(8,128)(2,1)S(1)}, u32[]{:S(2)}, u32[]{:S(2)}) async-start(bf16[32,8,256]{2,1,0:T(8,128)(2,1)} %shard_map.106), calls=%async_computation | async-start | bytes 262144 | tf_op jit(solution)/shard_map/all_to_all | solution.py:376
  25.6 0.0 collective-permute-done.5
  25.6 0.1 fusion.3
  25.7 1.8 %collective-permute-start.6 = (bf16[272,128]{1,0:T(8,128)(2,1)S(1)}, bf16[272,128]{1,0:T(8,128)(2,1)S(1)}, u32[]{:S(2)}, u32[]{:S(2)}) collective-permute-start(bf16[272,128]{1,0:T(8,128)(2,1)S(1)} %get-tuple-element.28), channel_id=1, source_target_pairs={{0,2},{1,3},{2,0},{3,1},{4,6},{5,7},{6,4},{7,5},{8,10},{9,11},{10,... | collective-permute-start | bytes 208904 | tf_op jit(solution)/shard_map/ppermute | solution.py:344
  28.1 2.5 %collective-permute-done.6.refs_0_ = bf16[272,128]{1,0:T(8,128)(2,1)S(1)} collective-permute-done((bf16[272,128]{1,0:T(8,128)(2,1)S(1)}, bf16[272,128]{1,0:T(8,128)(2,1)S(1)}, u32[]{:S(2)}, u32[]{:S(2)}) %collective-permute-start.6) | collective-permute-done | bytes 69664 | tf_op jit(solution)/shard_map/ppermute | solution.py:344
  30.7 0.1 shard_map.107
  30.8 2.7 %all-to-all-done.everyone_ref = bf16[32,8,256]{2,1,0:T(8,128)(2,1)S(1)} async-done(((bf16[32,8,256]{2,1,0:T(8,128)(2,1)}), bf16[32,8,256]{2,1,0:T(8,128)(2,1)S(1)}, u32[]{:S(2)}, u32[]{:S(2)}) %all-to-all-start) | async-done | bytes 131104 | tf_op jit(solution)/shard_map/all_to_all | solution.py:376
  33.5 1.4 %shard_map.108 = (f32[2,512]{1,0:T(2,128)}, f32[1,2]{1,0:T(1,128)}) custom-call(bf16[32,8,256]{2,1,0:T(8,128)(2,1)S(1)} %all-to-all-done.everyone_ref, bf16[64,512]{1,0:T(8,128)(2,1)S(1)} %get-tuple-element.24.captions_ref, bf16[128,256]{1,0:T(8,128)(2,1)S(1)} %get-tuple-element.25.masks_ref, f32[1]{0:T(128)S(6)} %copy.11.divisor_ref), custom_call_target="tpu_custom_call" | custom-call | flops 8388608 | bytes 131072 | tf_op jit(solution)/shard_map/pallas_call | solution.py:387
  (3 shorter events, 0.1 us)
Async XLA Ops:
  0.6 12.5 %copy-start = (bf16[256,1024]{1,0:T(8,128)(2,1)S(1)}, bf16[256,1024]{1,0:T(8,128)(2,1)}, u32[]{:S(2)}) copy-start(bf16[256,1024]{1,0:T(8,128)(2,1)} %frames_ref.1) | copy-start | bytes 1572868
  0.6 12.5 %copy-start.1 = (bf16[1024,512]{1,0:T(8,128)(2,1)S(1)}, bf16[1024,512]{1,0:T(8,128)(2,1)}, u32[]{:S(2)}) copy-start(bf16[1024,512]{1,0:T(8,128)(2,1)} %w_proj_ref.1) | copy-start | bytes 3145732
  0.7 12.5 %copy-start.2 = (bf16[256,1024]{1,0:T(8,128)(2,1)S(1)}, bf16[256,1024]{1,0:T(8,128)(2,1)}, u32[]{:S(2)}) copy-start(bf16[256,1024]{1,0:T(8,128)(2,1)} %w_out_ref.1) | copy-start | bytes 1572868
  3.6 9.4 %collective-permute-start = (bf16[1040,128]{1,0:T(8,128)(2,1)S(1)}, bf16[1040,128]{1,0:T(8,128)(2,1)S(1)}, u32[]{:S(2)}, u32[]{:S(2)}) collective-permute-start(bf16[1040,128]{1,0:T(8,128)(2,1)S(1)} %get-tuple-element.16), channel_id=1, source_target_pairs={{0,4},{4,0},{8,12},{12,8},{16,20},{20,16},{24,28},{28,24},{1,5},{5... | collective-permute-start | bytes 798728 | tf_op jit(solution)/shard_map/ppermute | solution.py:326
  6.7 9.7 %collective-permute-start.3 = (bf16[512,128]{1,0:T(8,128)(2,1)S(1)}, bf16[512,128]{1,0:T(8,128)(2,1)S(1)}, u32[]{:S(2)}, u32[]{:S(2)}) collective-permute-start(bf16[512,128]{1,0:T(8,128)(2,1)S(1)} %get-tuple-element.18), channel_id=1, source_target_pairs={{4,12},{12,20},{20,28},{8,0},{16,8},{24,16},{5,13},{13,21},{21,29}... | collective-permute-start | bytes 393224 | tf_op jit(solution)/shard_map/ppermute | solution.py:332
  7.9 8.4 %collective-permute-start.4 = (bf16[512,128]{1,0:T(8,128)(2,1)S(1)}, bf16[512,128]{1,0:T(8,128)(2,1)S(1)}, u32[]{:S(2)}, u32[]{:S(2)}) collective-permute-start(bf16[512,128]{1,0:T(8,128)(2,1)S(1)} %get-tuple-element.19), channel_id=1, source_target_pairs={{4,8},{12,16},{20,24},{8,4},{16,12},{24,20},{5,9},{13,17},{21,25},... | collective-permute-start | bytes 393224 | tf_op jit(solution)/shard_map/ppermute | solution.py:327
  13.1 1.3 %collective-permute-start.1 = (bf16[272,128]{1,0:T(8,128)(2,1)S(1)}, bf16[272,128]{1,0:T(8,128)(2,1)S(1)}, u32[]{:S(2)}, u32[]{:S(2)}) collective-permute-start(bf16[272,128]{1,0:T(8,128)(2,1)S(1)} %fusion), channel_id=1, source_target_pairs={{0,1},{1,0},{2,3},{3,2},{4,5},{5,4},{6,7},{7,6},{8,9},{9,8},{10,11... | collective-permute-start | bytes 208904 | tf_op jit(solution)/shard_map/ppermute | solution.py:344
  14.4 4.4 %collective-permute-start.2 = (bf16[272,128]{1,0:T(8,128)(2,1)S(1)}, bf16[272,128]{1,0:T(8,128)(2,1)S(1)}, u32[]{:S(2)}, u32[]{:S(2)}) collective-permute-start(bf16[272,128]{1,0:T(8,128)(2,1)S(1)} %fusion.2), channel_id=1, source_target_pairs={{0,8},{1,9},{2,10},{3,11},{4,12},{5,13},{6,14},{7,15},{8,0},{9,1},... | collective-permute-start | bytes 208904 | tf_op jit(solution)/shard_map/ppermute | solution.py:344
  18.9 6.7 %collective-permute-start.5 = (bf16[272,128]{1,0:T(8,128)(2,1)S(1)}, bf16[272,128]{1,0:T(8,128)(2,1)S(1)}, u32[]{:S(2)}, u32[]{:S(2)}) collective-permute-start(bf16[272,128]{1,0:T(8,128)(2,1)S(1)} %fusion.1), channel_id=1, source_target_pairs={{0,16},{1,17},{2,18},{3,19},{4,20},{5,21},{6,22},{7,23},{8,24},{9,... | collective-permute-start | bytes 208904 | tf_op jit(solution)/shard_map/ppermute | solution.py:344
  21.8 11.7 %all-to-all-start = ((bf16[32,8,256]{2,1,0:T(8,128)(2,1)}), bf16[32,8,256]{2,1,0:T(8,128)(2,1)S(1)}, u32[]{:S(2)}, u32[]{:S(2)}) async-start(bf16[32,8,256]{2,1,0:T(8,128)(2,1)} %shard_map.106), calls=%async_computation | async-start | bytes 262144 | tf_op jit(solution)/shard_map/all_to_all | solution.py:376
  25.7 5.0 %collective-permute-start.6 = (bf16[272,128]{1,0:T(8,128)(2,1)S(1)}, bf16[272,128]{1,0:T(8,128)(2,1)S(1)}, u32[]{:S(2)}, u32[]{:S(2)}) collective-permute-start(bf16[272,128]{1,0:T(8,128)(2,1)S(1)} %get-tuple-element.28), channel_id=1, source_target_pairs={{0,2},{1,3},{2,0},{3,1},{4,6},{5,7},{6,4},{7,5},{8,10},{9,11},{10,... | collective-permute-start | bytes 208904 | tf_op jit(solution)/shard_map/ppermute | solution.py:344
